TPU v7x, 32 devices: a whole 2x2x4 slice. The times are simulated.
32 devices in a mesh: dp: 16 (over z, y, core), blk: 2 (over x).
Axes of the slice: x: 2, y: 2, z: 4, core: 2. Of those that a mesh axis runs over, the one named last changes fastest.
Arguments:
- tokens: bfloat16 [32, 1024, 768], P('dp', 'blk'), may hold values from -6 to 6
- layout: int32 [32, 1024], P('dp'), may hold values from 0 to 255
- lengths: int32 [32], P('dp'), may hold values from 128 to 1024, as said below
- gain_attn: bfloat16 [768], P(('dp', 'blk')), may hold values from 0.5 to 1.5
- w_query: bfloat16 [768, 768], P(('dp', 'blk')), may hold values from -0.21875 to 0.21875
- w_key: bfloat16 [768, 768], P(('dp', 'blk')), may hold values from -0.21875 to 0.21875
- w_value: bfloat16 [768, 768], P(('dp', 'blk')), may hold values from -0.21875 to 0.21875
- w_output: bfloat16 [768, 768], P(('dp', 'blk')), may hold values from -2.5 to 2.5
- gain_ffn: bfloat16 [768], P(('dp', 'blk')), may hold values from 0.5 to 1.5
- w_in: bfloat16 [768, 3072], P(('dp', 'blk')), may hold values from -0.21875 to 0.21875
- w_out: bfloat16 [3072, 768], P(('dp', 'blk')), may hold values from -0.109375 to 0.109375
- rel_table: bfloat16 [32, 12], replicated, may hold values from -4 to 4
- grad_out: bfloat16 [32, 1024, 768], P('dp', 'blk'), may hold values from -6 to 6
Outputs:
- mixed: bfloat16 [32, 1024, 768], P('dp', 'blk')
- grad_tokens: bfloat16 [32, 1024, 768], P('dp', 'blk')
- grad_gain_attn: float32 [768], P(('dp', 'blk'))
- grad_w_query: float32 [768, 768], P(('dp', 'blk'))
- grad_w_key: float32 [768, 768], P(('dp', 'blk'))
- grad_w_value: float32 [768, 768], P(('dp', 'blk'))
- grad_w_output: float32 [768, 768], P(('dp', 'blk'))
- grad_gain_ffn: float32 [768], P(('dp', 'blk'))
- grad_w_in: float32 [768, 3072], P(('dp', 'blk'))
- grad_w_out: float32 [3072, 768], P(('dp', 'blk'))
- grad_rel_table: float32 [32, 12], replicated
Inputs may be any that keep to these rules, and one draw needn't show every extreme that they name: `lengths`: among the 2 items of each index of dp, one has length 1024 and another 1024 // 8.
All inputs are finite; a program needn't handle non-finite values.
Results may differ from a plain program's by a relative error of at most 0.023.
Values may be sent and summed in bfloat16 or wider, within the bound.
A program may use at most 192 MiB of HBM per device.

v0:
```python
import math

import jax
import jax.numpy as jnp
from jax import lax
from jax.sharding import PartitionSpec as P

EPSILON = 1e-06
SCALE = 0.125
NEGATIVE = -1e30
THRESHOLDS = (12, 16, 23, 32, 46, 64, 91)


def passed_along(x, axis, by):
    peers = lax.axis_size(axis)
    return lax.ppermute(x, axis, [(i, (i + by) % peers) for i in range(peers)])


def bucket_of(relative):
    magnitude = jnp.abs(relative)
    larger = 8 + sum(((magnitude >= limit).astype(jnp.int32) for limit in THRESHOLDS))
    return jnp.where(magnitude < 8, magnitude, larger) + 16 * (relative > 0).astype(jnp.int32)


def rms_norm(values, gain):
    return values * lax.rsqrt(jnp.mean(values * values, axis=-1, keepdims=True) + EPSILON) * gain


def gelu_exact(values):
    return jax.nn.gelu(values, approximate=False)


def block_scores(query_block, key_block, query_layout, key_layout, table):
    buckets = bucket_of(key_layout[:, None, :] - query_layout[:, :, None])
    labels = jnp.arange(table.shape[0], dtype=jnp.int32)[None, :, None, None]
    onehot = (buckets[:, None] == labels).astype(jnp.bfloat16)
    bias = jnp.einsum("sbqk,bh->shqk", onehot, table, preferred_element_type=jnp.float32)
    scores = (
        jnp.einsum("sqhe,skhe->shqk", query_block, key_block, preferred_element_type=jnp.float32)
        * SCALE
        + bias
    )
    return (scores, onehot)


def backward_block(
    query_block,
    grad_block,
    log_total,
    row_dot,
    query_layout,
    key_block,
    value_block,
    key_layout,
    key_valid,
    table,
):
    scores, onehot = block_scores(query_block, key_block, query_layout, key_layout, table)
    shares = jnp.where(key_valid[:, None, None, :], jnp.exp(scores - log_total[..., None]), 0.0)
    grad_shares = jnp.einsum(
        "sqhe,skhe->shqk", grad_block, value_block, preferred_element_type=jnp.float32
    )
    grad_scores = (shares * (grad_shares - row_dot[..., None])).astype(jnp.bfloat16)
    grad_query = (
        jnp.einsum("shqk,skhe->sqhe", grad_scores, key_block, preferred_element_type=jnp.float32)
        * SCALE
    )
    grad_key = (
        jnp.einsum("shqk,sqhe->skhe", grad_scores, query_block, preferred_element_type=jnp.float32)
        * SCALE
    )
    grad_value = jnp.einsum(
        "shqk,sqhe->skhe",
        shares.astype(jnp.bfloat16),
        grad_block,
        preferred_element_type=jnp.float32,
    )
    grad_table = jnp.einsum(
        "shqk,sbqk->bh", grad_scores, onehot, preferred_element_type=jnp.float32
    )
    return (grad_query, grad_key, grad_value, grad_table)


def on_device(
    tokens,
    layout,
    lengths,
    gain_attn,
    w_query,
    w_key,
    w_value,
    w_output,
    gain_ffn,
    w_in,
    w_out,
    rel_table,
    grad_out,
):
    gathered = (
        lax.all_gather(gain_attn, ("dp", "blk"), axis=0, tiled=True),
        lax.all_gather(w_query, ("dp", "blk"), axis=0, tiled=True),
        lax.all_gather(w_key, ("dp", "blk"), axis=0, tiled=True),
        lax.all_gather(w_value, ("dp", "blk"), axis=0, tiled=True),
        lax.all_gather(w_output, ("dp", "blk"), axis=0, tiled=True),
        lax.all_gather(gain_ffn, ("dp", "blk"), axis=0, tiled=True),
        lax.all_gather(w_in, ("dp", "blk"), axis=0, tiled=True),
        lax.all_gather(w_out, ("dp", "blk"), axis=0, tiled=True),
    )
    (
        gain_one,
        query_weight,
        key_weight,
        value_weight,
        output_weight,
        gain_two,
        inner_weight,
        outer_weight,
    ) = gathered
    item_count, local_rows, model_width = tokens.shape
    head_count = rel_table.shape[1]
    head_size = model_width // head_count
    bucket_count = rel_table.shape[0]
    group_size = lax.axis_size("blk")
    group_index = lax.axis_index("blk")
    token_rows = item_count * local_rows
    offset_here = group_index * local_rows
    item_shape = (item_count, local_rows, model_width)
    head_shape = (item_count, local_rows, head_count, head_size)
    query_layout = lax.dynamic_slice_in_dim(layout, offset_here, local_rows, 1)
    hidden = tokens.reshape(token_rows, model_width).astype(jnp.float32)
    normed, norm_one_back = jax.vjp(rms_norm, hidden, gain_one.astype(jnp.float32))
    normed = normed.astype(jnp.bfloat16)
    queries = jnp.dot(normed, query_weight, preferred_element_type=jnp.float32).astype(jnp.bfloat16)
    key_rows = jnp.dot(normed, key_weight, preferred_element_type=jnp.float32).astype(jnp.bfloat16)
    values = jnp.dot(normed, value_weight, preferred_element_type=jnp.float32).astype(jnp.bfloat16)
    queries_heads = queries.reshape(head_shape)
    key_items = key_rows.reshape(item_shape)
    value_items = values.reshape(item_shape)
    stats_shape = (item_count, head_count, local_rows)
    start_state = (
        jnp.full(stats_shape, NEGATIVE, jnp.float32),
        jnp.zeros(stats_shape, jnp.float32),
        jnp.zeros(head_shape, jnp.float32),
    )
    key_piece = lax.all_gather(key_items, "blk", axis=1, tiled=True)
    value_piece = lax.all_gather(value_items, "blk", axis=1, tiled=True)
    piece_rows = key_piece.shape[1]
    block_width = math.gcd(piece_rows, 128)

    def absorb_advance(block_index, running):
        running_max, running_sum, weighted = running
        block_start = block_index * block_width
        key_block = lax.dynamic_slice_in_dim(key_piece, block_start, block_width, 1).reshape(
            item_count, block_width, head_count, head_size
        )
        value_block = lax.dynamic_slice_in_dim(value_piece, block_start, block_width, 1).reshape(
            item_count, block_width, head_count, head_size
        )
        key_layout = lax.dynamic_slice_in_dim(layout, block_start, block_width, 1)
        key_valid = (block_start + jnp.arange(block_width, dtype=jnp.int32))[None, :] < lengths[
            :, None
        ]
        scores, onehot = block_scores(queries_heads, key_block, query_layout, key_layout, rel_table)
        key_mask = key_valid[:, None, None, :]
        masked = jnp.where(key_mask, scores, NEGATIVE)
        new_max = jnp.maximum(running_max, jnp.max(masked, axis=-1))
        shares = jnp.where(key_mask, jnp.exp(masked - new_max[..., None]), 0.0)
        factor = jnp.exp(running_max - new_max)
        running_sum = running_sum * factor + jnp.sum(shares, axis=-1)
        product = jnp.einsum(
            "shqk,skhe->sqhe",
            shares.astype(jnp.bfloat16),
            value_block,
            preferred_element_type=jnp.float32,
        )
        weighted = weighted * jnp.transpose(factor, (0, 2, 1))[..., None] + product
        return (new_max, running_sum, weighted)

    running_max, running_sum, weighted = lax.fori_loop(
        0, piece_rows // block_width, absorb_advance, start_state
    )
    log_total = running_max + jnp.log(running_sum)
    attended_full = weighted / jnp.transpose(running_sum, (0, 2, 1))[..., None]
    attended = attended_full.astype(jnp.bfloat16).reshape(token_rows, model_width)
    resid = hidden + jnp.dot(attended, output_weight, preferred_element_type=jnp.float32)
    normed_two, norm_two_back = jax.vjp(rms_norm, resid, gain_two.astype(jnp.float32))
    normed_two = normed_two.astype(jnp.bfloat16)
    pre_act = jnp.dot(normed_two, inner_weight, preferred_element_type=jnp.float32)
    activated, gelu_back = jax.vjp(gelu_exact, pre_act)
    activated = activated.astype(jnp.bfloat16)
    mixed = resid + jnp.dot(activated, outer_weight, preferred_element_type=jnp.float32)
    upstream_low = grad_out.reshape(token_rows, model_width)
    upstream = upstream_low.astype(jnp.float32)
    grad_outer = jnp.einsum(
        "rf,rd->fd", activated, upstream_low, preferred_element_type=jnp.float32
    )
    grad_activated = jnp.einsum(
        "rd,fd->rf", upstream_low, outer_weight, preferred_element_type=jnp.float32
    )
    (grad_pre,) = gelu_back(grad_activated)
    grad_pre = grad_pre.astype(jnp.bfloat16)
    grad_inner = jnp.einsum("rd,rf->df", normed_two, grad_pre, preferred_element_type=jnp.float32)
    grad_normed_two = jnp.einsum(
        "rf,df->rd", grad_pre, inner_weight, preferred_element_type=jnp.float32
    )
    grad_resid_part, grad_gain_two = norm_two_back(grad_normed_two)
    grad_resid = upstream + grad_resid_part
    grad_resid_low = grad_resid.astype(jnp.bfloat16)
    grad_output = jnp.einsum(
        "ra,rb->ab", attended, grad_resid_low, preferred_element_type=jnp.float32
    )
    grad_attended = jnp.einsum(
        "rb,ab->ra", grad_resid_low, output_weight, preferred_element_type=jnp.float32
    ).astype(jnp.bfloat16)
    grad_heads = grad_attended.reshape(head_shape)
    row_dot = jnp.transpose(
        jnp.sum(grad_heads.astype(jnp.float32) * attended_full, axis=-1), (0, 2, 1)
    )
    table_zero = jnp.zeros((bucket_count, head_count), jnp.float32)

    def pass_keys(key_pair):
        return passed_along(key_pair, "blk", 1)

    def pass_grads(grad_pair):
        return passed_along(grad_pair.astype(jnp.bfloat16), "blk", 1).astype(grad_pair.dtype)

    def visit_block(key_pair, owner_index):
        owner_start = owner_index * local_rows
        block_width = math.gcd(local_rows, 128)

        def visit_advance(block_index, running):
            grad_query, grad_pair, grad_table = running
            block_start = block_index * block_width
            key_start = owner_start + block_start
            block_pair = lax.dynamic_slice_in_dim(key_pair, block_start, block_width, 1)
            key_block = block_pair[:, :, 0].reshape(item_count, block_width, head_count, head_size)
            value_block = block_pair[:, :, 1].reshape(
                item_count, block_width, head_count, head_size
            )
            key_layout = lax.dynamic_slice_in_dim(layout, key_start, block_width, 1)
            key_valid = (key_start + jnp.arange(block_width, dtype=jnp.int32))[None, :] < lengths[
                :, None
            ]
            query_add, key_add, value_add, table_add = backward_block(
                queries_heads,
                grad_heads,
                log_total,
                row_dot,
                query_layout,
                key_block,
                value_block,
                key_layout,
                key_valid,
                rel_table,
            )
            pair_add = jnp.stack(
                [
                    key_add.reshape(item_count, block_width, model_width),
                    value_add.reshape(item_count, block_width, model_width),
                ],
                axis=2,
            )
            grad_pair = lax.dynamic_update_slice_in_dim(grad_pair, pair_add, block_start, 1)
            return (grad_query + query_add, grad_pair, grad_table + table_add)

        start_grads = (
            jnp.zeros(head_shape, jnp.float32),
            jnp.zeros((item_count, local_rows, 2, model_width), jnp.float32),
            table_zero,
        )
        return lax.fori_loop(0, local_rows // block_width, visit_advance, start_grads)

    own_pair = jnp.stack([key_items, value_items], axis=2)
    key_pair = pass_keys(own_pair)
    grad_query, grad_pair, grad_table = visit_block(
        key_pair, (group_index + group_size - 1) % group_size
    )

    def turn(step_index, running):
        grad_query, grad_pair, grad_table, key_pair = running
        key_pair = pass_keys(key_pair)
        owner_index = (group_index + 2 * group_size - 1 - step_index) % group_size
        query_add, pair_add, table_add = visit_block(key_pair, owner_index)
        return (
            grad_query + query_add,
            pass_grads(grad_pair) + pair_add,
            grad_table + table_add,
            key_pair,
        )

    grad_query, grad_pair, grad_table, key_pair = lax.fori_loop(
        1, group_size - 1, turn, (grad_query, grad_pair, grad_table, key_pair)
    )
    query_add, pair_add, table_add = visit_block(own_pair, group_index)
    grad_query = grad_query + query_add
    grad_pair = pass_grads(grad_pair) + pair_add
    grad_table = grad_table + table_add
    grad_key_full = grad_pair[:, :, 0]
    grad_value_full = grad_pair[:, :, 1]
    grad_query_low = grad_query.reshape(token_rows, model_width).astype(jnp.bfloat16)
    grad_key_low = grad_key_full.reshape(token_rows, model_width).astype(jnp.bfloat16)
    grad_value_low = grad_value_full.reshape(token_rows, model_width).astype(jnp.bfloat16)
    grad_wquery = jnp.einsum(
        "ra,rb->ab", normed, grad_query_low, preferred_element_type=jnp.float32
    )
    grad_wkey = jnp.einsum("ra,rb->ab", normed, grad_key_low, preferred_element_type=jnp.float32)
    grad_wvalue = jnp.einsum(
        "ra,rb->ab", normed, grad_value_low, preferred_element_type=jnp.float32
    )
    grad_normed = jnp.einsum(
        "rb,ab->ra", grad_query_low, query_weight, preferred_element_type=jnp.float32
    )
    grad_normed = grad_normed + jnp.einsum(
        "rb,ab->ra", grad_key_low, key_weight, preferred_element_type=jnp.float32
    )
    grad_normed = grad_normed + jnp.einsum(
        "rb,ab->ra", grad_value_low, value_weight, preferred_element_type=jnp.float32
    )
    grad_input_part, grad_gain_one = norm_one_back(grad_normed)
    grad_input = grad_resid + grad_input_part
    summed = (
        lax.psum_scatter(grad_gain_one, ("dp", "blk"), scatter_dimension=0, tiled=True),
        lax.psum_scatter(grad_wquery, ("dp", "blk"), scatter_dimension=0, tiled=True),
        lax.psum_scatter(grad_wkey, ("dp", "blk"), scatter_dimension=0, tiled=True),
        lax.psum_scatter(grad_wvalue, ("dp", "blk"), scatter_dimension=0, tiled=True),
        lax.psum_scatter(grad_output, ("dp", "blk"), scatter_dimension=0, tiled=True),
        lax.psum_scatter(grad_gain_two, ("dp", "blk"), scatter_dimension=0, tiled=True),
        lax.psum_scatter(grad_inner, ("dp", "blk"), scatter_dimension=0, tiled=True),
        lax.psum_scatter(grad_outer, ("dp", "blk"), scatter_dimension=0, tiled=True),
    )
    table_sum = lax.psum(grad_table, ("dp", "blk"))
    return (
        mixed.astype(jnp.bfloat16).reshape(item_shape),
        grad_input.astype(jnp.bfloat16).reshape(item_shape),
        summed[0],
        summed[1],
        summed[2],
        summed[3],
        summed[4],
        summed[5],
        summed[6],
        summed[7],
        table_sum,
    )


def solution(mesh):
    return jax.shard_map(
        on_device,
        mesh=mesh,
        in_specs=(
            P("dp", "blk", None),
            P("dp", None),
            P("dp"),
            P(("dp", "blk")),
            P(("dp", "blk"), None),
            P(("dp", "blk"), None),
            P(("dp", "blk"), None),
            P(("dp", "blk"), None),
            P(("dp", "blk")),
            P(("dp", "blk"), None),
            P(("dp", "blk"), None),
            P(),
            P("dp", "blk", None),
        ),
        out_specs=(
            P("dp", "blk", None),
            P("dp", "blk", None),
            P(("dp", "blk")),
            P(("dp", "blk"), None),
            P(("dp", "blk"), None),
            P(("dp", "blk"), None),
            P(("dp", "blk"), None),
            P(("dp", "blk")),
            P(("dp", "blk"), None),
            P(("dp", "blk"), None),
            P(),
        ),
        check_vma=False,
    )
```

profile of v0, /device:TPU:0, one launch (start us, length us, event | category | flops | bytes accessed | tf_op | source)
XLA Modules:
  0.0 1761.1 jit_solution(13452004537559919285)
XLA Ops:
  11.1 42.1 %all-reduce.5 = (bf16[768]{0:T(1024)(128)(2,1)S(1)}, bf16[768]{0:T(1024)(128)(2,1)S(1)}) all-reduce(bf16[768]{0:T(1024)(128)(2,1)S(1)} %dynamic-update-slice, bf16[768]{0:T(1024)(128)(2,1)S(1)} %dynamic-update-slice.1), channel_id=1, replica_groups=mesh['dp'=16,'blk'=2] {'dp','blk'}, use_global_device_ids=true, to_apply=%add | all-reduce | flops 1536 | bytes 6144
  58.2 9.6 all-gather.9.cloned.1.call-done
  72.3 51.6 %all-gather.15.cloned.1.call-done = bf16[768,768]{1,0:T(8,128)(2,1)} async-done(((bf16[24,768]{1,0:T(8,128)(2,1)}), bf16[768,768]{1,0:T(8,128)(2,1)}) %all-gather.15.cloned.1.call-update) | async-done | bytes 1179664 | tf_op jit(solution)/shard_map/all_gather | solution.py:103
  136.1 43.8 %all-gather.13.cloned.1.call-done = bf16[768,768]{1,0:T(8,128)(2,1)} async-done(((bf16[24,768]{1,0:T(8,128)(2,1)}), bf16[768,768]{1,0:T(8,128)(2,1)}) %all-gather.13.cloned.1.call-update) | async-done | bytes 1179664 | tf_op jit(solution)/shard_map/all_gather | solution.py:101
  200.4 48.7 %all-gather.11.cloned.1.call-done = bf16[2,1024,768]{1,2,0:T(8,128)(2,1)} async-done(((bf16[2,512,768]{1,2,0:T(8,128)(2,1)}), bf16[2,1024,768]{1,2,0:T(8,128)(2,1)}) %all-gather.11.cloned.1.call-update) | async-done | bytes 3145744 | tf_op jit(solution)/shard_map/all_gather | solution.py:145
  249.1 77.8 %all-gather.17.cloned.1.call-done = bf16[2,1024,768]{1,2,0:T(8,128)(2,1)} async-done(((bf16[2,512,768]{1,2,0:T(8,128)(2,1)}), bf16[2,1024,768]{1,2,0:T(8,128)(2,1)}) %all-gather.17.cloned.1.call-update) | async-done | bytes 3145744 | tf_op jit(solution)/shard_map/all_gather | solution.py:146
  326.9 294.8 %while.54 = (s32[]{:T(128)}, f32[2,12,512]{2,1,0:T(8,128)}, f32[2,12,512]{2,1,0:T(8,128)}, f32[2,512,12,64]{1,3,2,0:T(8,128)}, s32[2]{0:T(128)}, /*index=5*/bf16...) while((s32[]{:T(128)}, f32[2,12,512]{2,1,0:T(8,128)}, ...), condition=%wide.region_4.5_spmd.clone, body=%wide.region_1.4_spmd.clone.sunk | while | flops 529342848 | bytes 81864784 | solution.py:179
  328.1 5.9 fusion.217
  334.0 9.3 copy.207
  345.2 7.8 fusion.218
  363.2 5.9 fusion.217
  369.1 9.3 copy.207
  380.3 7.8 fusion.218
  394.0 5.1 bitcast_add_fusion.10
  400.4 5.9 fusion.217
  406.2 9.3 copy.207
  417.4 7.8 fusion.218
  437.8 5.9 fusion.217
  443.7 9.4 copy.207
  454.9 7.8 fusion.218
  468.6 5.0 bitcast_add_fusion.10
  474.9 5.9 fusion.217
  480.7 9.3 copy.207
  492.0 7.8 fusion.218
  505.6 5.1 bitcast_add_fusion.10
  512.0 5.9 fusion.217
  517.8 9.3 copy.207
  529.0 7.8 fusion.218
  549.0 5.9 fusion.217
  554.8 9.3 copy.207
  566.0 7.8 fusion.218
  586.0 5.9 fusion.217
  591.8 9.3 copy.207
  603.0 7.8 fusion.218
  622.6 7.7 fusion.100
  637.5 36.5 %multiply_convert_fusion = (bf16[1024,3072]{1,0:T(8,128)(2,1)}, f32[1024,3072]{1,0:T(8,128)}, f32[1024,3072]{1,0:T(8,128)}) fusion(bf16[768,3072]{1,0:T(8,128)(2,1)} %all-gather.21.cloned.1.call-done, f32[1024,768]{1,0:T(8,128)} %get-tuple-element.1056, f32[768]{0:T(1024)S(1)} %convert_element_type.387, f32[1024]{0:T(1024)S(1)} %fusion.94), kind=kOutput, calls=%fused_computation.112 | convolution fusion | flops 5038669824 | bytes 39328768 | tf_op jit(solution)/shard_map/dot_general | solution.py:188
  674.0 16.2 add_convert_fusion
  690.2 9.6 multiply_reduce_fusion
  718.5 166.9 %while.56 = (s32[]{:T(128)}, f32[2,512,12,64]{1,3,2,0:T(8,128)}, f32[2,512,2,768]{3,1,0,2:T(8,128)}, f32[32,12]{0,1:T(8,128)}, bf16[2,512,2,768]{1,3,0,2:T(8,128...) while((s32[]{:T(128)}, f32[2,512,12,64]{1,3,2,0:T(8,128)}, ...), condition=%wide.region_11.12_spmd.clone, body=%wide.region_10.11_spmd.clone.sunk | while | flops 1235551360 | bytes 150594448 | solution.py:271
  753.4 5.5 fusion.259
  779.7 5.2 bitcast_add_fusion.12
  795.3 5.5 fusion.259
  821.5 5.2 bitcast_add_fusion.12
  837.1 5.5 fusion.259
  863.4 5.2 bitcast_add_fusion.12
  878.9 5.5 fusion.259
  885.5 159.9 %while.55 = (s32[]{:T(128)}, f32[2,512,12,64]{1,3,2,0:T(8,128)}, bf16[2,512,2,768]{3,1,0,2:T(8,128)(2,1)}, f32[32,12]{0,1:T(8,128)S(1)}, bf16[2,512,2,768]{1,3,0...) while((s32[]{:T(128)}, f32[2,512,12,64]{1,3,2,0:T(8,128)}, ...), condition=%wide.region_9.10_spmd.clone, body=%wide.region_8.9_spmd.clone.sunk | while | flops 1235747968 | bytes 132494136 | solution.py:271
  918.3 6.4 fusion.240
  944.9 5.2 bitcast_add_fusion.11
  958.4 6.4 fusion.240
  985.0 5.2 bitcast_add_fusion.11
  998.6 6.4 fusion.240
  1025.2 5.2 bitcast_add_fusion.11
  1038.8 6.4 fusion.240
  1059.3 70.0 %collective-permute-done.1 = bf16[2,512,2,768]{3,1,0,2:T(8,128)(2,1)} collective-permute-done((bf16[2,512,2,768]{3,1,0,2:T(8,128)(2,1)}, bf16[2,512,2,768]{3,1,0,2:T(8,128)(2,1)}, u32[]{:S(2)}, u32[]{:S(2)}) %collective-permute-start.1) | collective-permute-done | bytes 3145760 | tf_op jit(solution)/shard_map/ppermute | solution.py:16
  1141.5 10.7 fusion.97
  1153.6 10.4 fusion.108
  1168.4 9.6 add_convert_fusion.2
  1183.5 39.5 %all-reduce.4 = (f32[768]{0:T(1024)S(1)}, f32[768]{0:T(1024)S(1)}, f32[32,12]{0,1:T(8,128)}) all-reduce(f32[768]{0:T(1024)S(1)} %get-tuple-element.952, f32[768]{0:T(1024)S(1)} %copy-done.54, f32[32,12]{0,1:T(8,128)S(1)} %add.573), channel_id=2, replica_groups=mesh['dp'=16,'blk'=2] {'dp','blk'}, use_global_device_ids=true, to_apply=%region_14.15.clone | all-reduce | flops 1920 | bytes 15360
  1229.0 33.6 %reduce-scatter.13.cloned.1.call-done = f32[24,768]{1,0:T(8,128)} async-done(((f32[768,768]{1,0:T(8,128)}), f32[24,768]{1,0:T(8,128)}) %reduce-scatter.13.cloned.1.call-update) | async-done | bytes 73744 | tf_op jit(solution)/shard_map/reduce_scatter | solution.py:326
  1262.5 103.9 %reduce-scatter.9.cloned.1.call-done = f32[24,768]{1,0:T(8,128)} async-done(((f32[768,768]{1,0:T(8,128)}), f32[24,768]{1,0:T(8,128)}) %reduce-scatter.9.cloned.1.call-update) | async-done | bytes 73744 | tf_op jit(solution)/shard_map/reduce_scatter | solution.py:324
  1366.5 104.6 %reduce-scatter.11.cloned.1.call-done = f32[24,768]{1,0:T(8,128)} async-done(((f32[768,768]{1,0:T(8,128)}), f32[24,768]{1,0:T(8,128)}) %reduce-scatter.11.cloned.1.call-update) | async-done | bytes 73744 | tf_op jit(solution)/shard_map/reduce_scatter | solution.py:325
  1471.1 141.2 %reduce-scatter.15.cloned.1.call-done = f32[24,3072]{1,0:T(8,128)} async-done(((f32[768,3072]{1,0:T(8,128)}), f32[24,3072]{1,0:T(8,128)}) %reduce-scatter.15.cloned.1.call-update) | async-done | bytes 294928 | tf_op jit(solution)/shard_map/reduce_scatter | solution.py:328
  1612.3 142.0 %reduce-scatter.17.cloned.1.call-done = f32[96,768]{1,0:T(8,128)} async-done(((f32[3072,768]{1,0:T(8,128)}), f32[96,768]{1,0:T(8,128)}) %reduce-scatter.17.cloned.1.call-update) | async-done | bytes 294928 | tf_op jit(solution)/shard_map/reduce_scatter | solution.py:329
  (565 shorter events, 457.6 us)
Async XLA Ops:
  7.2 60.6 %all-gather.9.cloned.1.call-start = ((), (), s32[]{:S(2)}) async-start(), calls=%async_computation.6 | async-start | bytes 1216512 | tf_op jit(solution)/shard_map/all_gather | solution.py:102
  7.9 115.9 %all-gather.15.cloned.1.call-start = ((), (), s32[]{:S(2)}) async-start(), calls=%async_computation.9 | async-start | bytes 1216512 | tf_op jit(solution)/shard_map/all_gather | solution.py:103
  8.7 171.2 %all-gather.13.cloned.1.call-start = ((), (), s32[]{:S(2)}) async-start(), calls=%async_computation.8 | async-start | bytes 1216512 | tf_op jit(solution)/shard_map/all_gather | solution.py:101
  9.4 239.7 %all-gather.11.cloned.1.call-start = ((), (), s32[]{:S(2)}) async-start(), calls=%async_computation.7 | async-start | bytes 4718592 | tf_op jit(solution)/shard_map/all_gather | solution.py:145
  53.2 80.6 %copy-start.40 = (f32[768]{0:T(1024)}, f32[768]{0:T(1024)S(1)}, u32[]{:S(2)}) copy-start(f32[768]{0:T(1024)S(1)} %convert_element_type.381) | copy-start | bytes 9220
  58.2 12.3 copy-start.30
  70.5 56.5 %copy-start.21 = (bf16[1024,768]{1,0:T(8,128)(2,1)}, bf16[1024,768]{1,0:T(8,128)(2,1)S(1)}, u32[]{:S(2)}) copy-start(bf16[1024,768]{1,0:T(8,128)(2,1)S(1)} %convolution_convert_fusion.3) | copy-start | bytes 4718596
  72.2 254.6 %all-gather.17.cloned.1.call-start = ((), (), s32[]{:S(2)}) async-start(), calls=%async_computation.10 | async-start | bytes 4718592 | tf_op jit(solution)/shard_map/all_gather | solution.py:146
  129.8 502.1 %all-gather.19.cloned.1.call-start = ((), (), s32[]{:S(2)}) async-start(), calls=%async_computation.11 | async-start | bytes 1216512 | tf_op jit(solution)/shard_map/all_gather | solution.py:104
  130.3 507.1 %all-gather.21.cloned.1.call-start = ((), (), s32[]{:S(2)}) async-start(), calls=%async_computation.12 | async-start | bytes 4866048 | tf_op jit(solution)/shard_map/all_gather | solution.py:106
  131.1 542.9 %all-gather.23.cloned.1.call-start = ((), (), s32[]{:S(2)}) async-start(), calls=%async_computation.13 | async-start | bytes 4866048 | tf_op jit(solution)/shard_map/all_gather | solution.py:107
  131.8 1097.1 %reduce-scatter.7.cloned.1.call-start = ((), (), s32[]{:S(2)}) async-start(), calls=%async_computation.14 | async-start | bytes 2433024 | tf_op jit(solution)/shard_map/reduce_scatter | solution.py:323
  131.9 48.0 %copy-start.31 = (bf16[1024,768]{1,0:T(8,128)(2,1)S(1)}, bf16[1024,768]{1,0:T(8,128)(2,1)}, u32[]{:S(2)}) copy-start(bf16[1024,768]{1,0:T(8,128)(2,1)} %copy-done.30) | copy-start | bytes 4718596
  133.8 566.0 %copy-start.46 = (f32[768]{0:T(1024)}, f32[768]{0:T(1024)S(1)}, u32[]{:S(2)}) copy-start(f32[768]{0:T(1024)S(1)} %convert_element_type.387) | copy-start | bytes 9220
  195.2 131.7 %copy-start.39 = (bf16[32,12]{0,1:T(8,128)(2,1)S(1)}, bf16[32,12]{0,1:T(8,128)(2,1)}, u32[]{:S(2)}) copy-start(bf16[32,12]{0,1:T(8,128)(2,1)} %param.30) | copy-start | bytes 2308
  199.1 686.3 %collective-permute-start = (bf16[2,512,2,768]{1,3,0,2:T(8,128)(2,1)}, bf16[2,512,2,768]{1,3,0,2:T(8,128)(2,1)}, u32[]{:S(2)}, u32[]{:S(2)}) collective-permute-start(bf16[2,512,2,768]{1,3,0,2:T(8,128)(2,1)} %pad_maximum_fusion.2), channel_id=1, source_target_pairs={{0,1},{1,0},{2,3},{3,2},{4,5},{5,4},{6,7},{7,6},{8,9},{9,8},{10,11... | collective-permute-start | bytes 9437192 | tf_op jit(solution)/shard_map/ppermute | solution.py:16
  393.3 5.7 copy-start.24
  426.2 5.3 copy-start
  430.4 6.1 copy-start.24
  467.9 5.7 copy-start.24
  500.7 5.0 copy-start
  505.0 5.8 copy-start.24
  542.0 5.7 copy-start.24
  579.0 5.7 copy-start.24
  616.0 5.7 copy-start.24
  636.8 63.0 %copy-start.48 = (f32[1024]{0:T(1024)}, f32[1024]{0:T(1024)S(1)}, u32[]{:S(2)}) copy-start(f32[1024]{0:T(1024)S(1)} %fusion.94) | copy-start | bytes 12292
  637.5 36.5 %copy-start.36 = (bf16[2,512,768]{2,1,0:T(8,128)(2,1)S(1)}, bf16[2,512,768]{2,1,0:T(8,128)(2,1)}, u32[]{:S(2)}) copy-start(bf16[2,512,768]{2,1,0:T(8,128)(2,1)} %param.31) | copy-start | bytes 4718596
  674.0 16.3 copy-start.26
  718.5 166.9 %copy-start.50 = (f32[32,12]{0,1:T(8,128)S(1)}, f32[32,12]{0,1:T(8,128)}, u32[]{:S(2)}) copy-start(f32[32,12]{0,1:T(8,128)} %custom-call.4) | copy-start | bytes 4612
  728.5 7.5 copy-start.8
  728.5 7.5 copy-start.15
  747.5 6.0 copy-start.51
  769.4 7.5 copy-start.8
  769.4 7.5 copy-start.15
  779.7 5.2 copy-start.2
  789.3 5.9 copy-start.51
  811.2 7.5 copy-start.8
  811.2 7.5 copy-start.15
  821.5 5.2 copy-start.2
  831.1 6.0 copy-start.51
  853.1 7.5 copy-start.8
  853.1 7.5 copy-start.15
  863.4 5.2 copy-start.2
  872.9 5.9 copy-start.51
  895.3 7.5 copy-start.9
  895.3 7.5 copy-start.16
  934.6 7.5 copy-start.9
  934.6 7.5 copy-start.16
  944.9 5.2 copy-start.4
  974.7 7.5 copy-start.9
  974.7 7.5 copy-start.16
  985.0 5.2 copy-start.4
  1014.9 7.5 copy-start.9
  1014.9 7.5 copy-start.16
  1025.2 5.2 copy-start.4
  1054.8 207.7 %reduce-scatter.13.cloned.1.call-start = ((), (), s32[]{:S(2)}) async-start(), calls=%async_computation.17 | async-start | bytes 2433024 | tf_op jit(solution)/shard_map/reduce_scatter | solution.py:326
  1054.9 74.4 %collective-permute-start.1 = (bf16[2,512,2,768]{3,1,0,2:T(8,128)(2,1)}, bf16[2,512,2,768]{3,1,0,2:T(8,128)(2,1)}, u32[]{:S(2)}, u32[]{:S(2)}) collective-permute-start(bf16[2,512,2,768]{3,1,0,2:T(8,128)(2,1)} %get-tuple-element.664), channel_id=1, source_target_pairs={{0,1},{1,0},{2,3},{3,2},{4,5},{5,4},{6,7},{7,6},{8,9},{9,8},{10,11... | collective-permute-start | bytes 9437192 | tf_op jit(solution)/shard_map/ppermute | solution.py:16
  1059.2 307.3 %reduce-scatter.9.cloned.1.call-start = ((), (), s32[]{:S(2)}) async-start(), calls=%async_computation.15 | async-start | bytes 2433024 | tf_op jit(solution)/shard_map/reduce_scatter | solution.py:324
  1138.6 332.6 %reduce-scatter.11.cloned.1.call-start = ((), (), s32[]{:S(2)}) async-start(), calls=%async_computation.16 | async-start | bytes 2433024 | tf_op jit(solution)/shard_map/reduce_scatter | solution.py:325
  1141.5 470.9 %reduce-scatter.15.cloned.1.call-start = ((), (), s32[]{:S(2)}) async-start(), calls=%async_computation.18 | async-start | bytes 9732096 | tf_op jit(solution)/shard_map/reduce_scatter | solution.py:328
  1152.2 602.1 %reduce-scatter.17.cloned.1.call-start = ((), (), s32[]{:S(2)}) async-start(), calls=%async_computation.19 | async-start | bytes 9732096 | tf_op jit(solution)/shard_map/reduce_scatter | solution.py:329
  1168.4 9.7 copy-start.35
  1168.4 9.6 copy-start.55
  1179.8 44.3 %copy-start.45 = (f32[1,4,2,128]{3,1,2,0:T(4,128)S(1)}, f32[1,4,2,128]{3,1,2,0:T(4,128)}, u32[]{:S(2)}) copy-start(f32[1,4,2,128]{3,1,2,0:T(4,128)} %copy-done.44) | copy-start | bytes 12292
  (90 other events, 276.4 us)
Sparse Core Ops, SparseCore 0:
  10.9 56.8 all-gather.8
  70.7 53.0 all-gather.14
  126.8 53.0 all-gather.12
  181.9 67.2 all-gather.10
  250.5 76.3 all-gather.16
  329.7 54.1 all-gather.18
  386.8 62.5 all-gather.20
  452.3 62.4 all-gather.22
  1055.0 102.8 reduce-scatter.6
  1164.4 98.0 reduce-scatter.12
  1268.4 98.0 reduce-scatter.8
  1373.0 98.0 reduce-scatter.10
  1477.6 134.7 reduce-scatter.14
  1619.7 134.5 reduce-scatter.16
where the time goes:
time: 1770 us; the launch traced here: 1760 us
  waiting for transfers between devices  831 us (47%)
  matrix products  476 us (27%)
  local copies, waits for them, and re-layouts  245 us (14%)
  other arithmetic  109 us (6%)
  blocking collectives  81.5 us (5%)
    reduce_scatter x1, waiting for transfers between devices, on_device(): lax.psum_scatter(grad_outer, ('dp', 'blk'), scatter_dimension=0, tiled=True)  142 us
    reduce_scatter x1, waiting for transfers between devices, on_device(): lax.psum_scatter(grad_inner, ('dp', 'blk'), scatter_dimension=0, tiled=True)  141 us
    reduce_scatter x1, waiting for transfers between devices, on_device(): lax.psum_scatter(grad_wvalue, ('dp', 'blk'), scatter_dimension=0, tiled=T...  105 us
    reduce_scatter x1, waiting for transfers between devices, on_device(): lax.psum_scatter(grad_wkey, ('dp', 'blk'), scatter_dimension=0, tiled=True)  104 us
    dot_general x16, matrix products, block_scores(): jnp.einsum('sqhe,skhe->shqk', query_block, key_block, preferred_element_t...  101 us
    unnamed x2, blocking collectives  81.5 us
    all_gather x1, waiting for transfers between devices, on_device(): value_piece = lax.all_gather(value_items, 'blk', axis=1, tiled=True)  77.8 us
    dot_general x16, matrix products, block_scores(): jnp.einsum('sbqk,bh->shqk', onehot, table, preferred_element_type=jnp.flo...  76.6 us
  transfers between devices with their start and end apart: 16, of which 11 were waited for; matrix products, arithmetic and copies ran while one was open for 36% of the time, Pallas kernels for 0%

commit v1 on v0

v1 whole, which is shorter than its diff:
```python
import functools

import jax
import jax.numpy as jnp
import numpy as np
from jax import lax
from jax.experimental import pallas as pl
from jax.experimental.pallas import tpu as pltpu
from jax.sharding import PartitionSpec as P

F32=jnp.float32; BF=jnp.bfloat16
SPAN=256
CH=256
def dot(a,b): return lax.dot_general(a,b,(((1,),(0,)),((),())),preferred_element_type=F32)
def eye_of(row, width, reverse):
    spots=lax.broadcasted_iota(jnp.int32,(width,row.shape[1]),0)
    if reverse: spots=width-1-spots
    return (spots==row).astype(F32).astype(BF)

def attend(n,L,S,R,E,steps,far,*refs):
    q,kf,vf,ks,vs,layq,layf,lays,mask,u=refs[:10]
    if far:
        shards=refs[10:13]; o,p,l=refs[13:16]; wholes=refs[16:19]
        kcat,qcat,vt,s_ref,ohq,send,recv,local=refs[19:]
        at,chains=gather_plan(shards,wholes,(send,recv),local)
        tick=ticker(spread(chains,GATHER_BEGIN,GATHER_LAG,2*steps),steps,at)
    else:
        o,p,l,kcat,qcat,vt,s_ref,ohq=refs[10:]
        tick=lambda u:None
    W=2*E
    spans=[L]*(n-1)+[S]
    @pl.when(pl.program_id(0)==0)
    def _():
        base=0
        for i,m in enumerate(spans):
            row=layf[i] if i<n-1 else lays[...]
            kcat[base:base+m,W:]=jnp.transpose(eye_of(row,SPAN,False).astype(F32)).astype(BF)
            ohq[i]=eye_of(layq[i],SPAN,False)
            base+=m
        vt[:,E:]=jnp.ones((2,vt.shape[1]-E,vt.shape[2]),BF)
    pair=pl.program_id(0)
    base=0
    for i,m in enumerate(spans):
        ch=min(CH,m)
        kcat[base:base+m,:W]=kf[i] if i<n-1 else ks[...]
        v=vf[i] if i<n-1 else vs[...]
        vtr=jnp.transpose(v.astype(F32)).astype(BF)
        vt[0,:E,:m]=vtr[:E]
        vt[1,:E,:m]=vtr[E:]
        qt=jnp.transpose(q[i].astype(F32)).astype(BF)
        outs=[]
        for h in range(2):
            if i==0: tick(h)
            urow=u[0,h:h+1,:]
            toep=pltpu.roll(jnp.broadcast_to(urow,(SPAN,2*SPAN)),0,1,stride=1,stride_axis=0)[:,:SPAN].astype(BF)
            qcat[h*E:(h+1)*E]=qt[h*E:(h+1)*E]
            qcat[(1-h)*E:(2-h)*E]=jnp.zeros((E,R),BF)
            qcat[W:]=dot(toep,ohq[i]).astype(BF)
            m8=jnp.full((8,R),-jnp.inf,F32)
            for c in range(0,m,ch):
                s=dot(kcat[base+c:base+c+ch],qcat[...])
                if 0<i<n-1: s=s+mask[i,c:c+ch,:]
                s_ref[c:c+ch]=s
                m8=jnp.maximum(m8,jnp.max(s.reshape(ch//8,8,R),axis=0))
            top=jnp.max(m8,axis=0,keepdims=True)
            for c in range(0,m,ch):
                p[0,h,base+c:base+c+ch]=jnp.exp(s_ref[c:c+ch]-top).astype(BF)
            full=dot(vt[h,:,:m],p[0,h,base:base+m])
            total=full[E:E+1]
            l[i,0,h:h+1]=total
            outs.append(full[:E]/total)
        o[i]=jnp.transpose(jnp.concatenate(outs,axis=0)).astype(BF)
        base+=m
    tick(2)

def attend_call(q,kf,vf,ks,vs,layq,layf,lays,mask,u,shards=()):
    n,R,D=q.shape; L=kf.shape[1]; S=ks.shape[0]; H=u.shape[0]*2; E=D//H; W=2*E
    KT=(n-1)*L+S
    full=lambda a: pl.BlockSpec(a.shape,lambda j:(0,)*a.ndim)
    return pl.pallas_call(functools.partial(attend,n,L,S,R,E,H//2,bool(shards)),
      grid=(H//2,),
      in_specs=[pl.BlockSpec((n,R,W),lambda j:(0,0,j)),
        pl.BlockSpec((n-1,L,W),lambda j:(0,0,j)),pl.BlockSpec((n-1,L,W),lambda j:(0,0,j)),
        pl.BlockSpec((S,W),lambda j:(0,j)),pl.BlockSpec((S,W),lambda j:(0,j)),
        full(layq),full(layf),full(lays),full(mask),pl.BlockSpec((1,2,2*SPAN),lambda j:(j,0,0))]+[pl.BlockSpec(memory_space=pl.ANY)]*len(shards),
      out_specs=[pl.BlockSpec((n,R,W),lambda j:(0,0,j)),
        pl.BlockSpec((1,2,KT,R),lambda j:(j,0,0,0)),
        pl.BlockSpec((n,1,2,R),lambda j:(0,j,0,0))]+[pl.BlockSpec(memory_space=pl.ANY)]*len(shards),
      out_shape=[jax.ShapeDtypeStruct((n,R,D),BF),jax.ShapeDtypeStruct((H//2,2,KT,R),BF),jax.ShapeDtypeStruct((n,H//2,2,R),F32)]
        +[jax.ShapeDtypeStruct((4,2,2,2)+s.shape,BF) for s in shards],
      scratch_shapes=[pltpu.VMEM((KT,W+SPAN),BF),pltpu.VMEM((W+SPAN,R),BF),pltpu.VMEM((2,E+16,L),BF),pltpu.VMEM((L,R),F32),pltpu.VMEM((n,SPAN,R),BF)]
        +([pltpu.SemaphoreType.DMA((5*GATHER_COPIES,))]*2+[pltpu.SemaphoreType.DMA((5,))] if shards else []),
      compiler_params=pltpu.CompilerParams(vmem_limit_bytes=56*2**20,dimension_semantics=("arbitrary",),**(dict(collective_id=2,has_side_effects=True) if shards else {})),
      name="attend",
    )(q,kf,vf,ks,vs,layq,layf,lays,mask,u,*shards)

def attend_back(n,L,S,R,E,steps,far,*refs):
    q,kf,vf,ks,vs,layq,layf,lays,o,do,p,l=refs[:12]
    if far:
        parts=refs[12:15]; dq,dkf,dvf,dks,dvs,t=refs[15:21]; totals=refs[21:24]
        kq,vaug,rhs,ds,ohq,nacc,qm,dm=refs[24:32]; send,recv,local=refs[-3:]
        at,chains=sum_plan(parts,totals,refs[32:-3],(send,recv),local)
        tick=ticker(spread(chains,SUM_BEGIN,SUM_LAG,2*steps),steps,at)
    else:
        dq,dkf,dvf,dks,dvs,t,kq,vaug,rhs,ds,ohq,nacc,qm,dm=refs[12:]
        tick=lambda u:None
    W=2*E
    spans=[L]*(n-1)+[S]
    @pl.when(pl.program_id(0)==0)
    def _():
        base=0
        for i,m in enumerate(spans):
            row=layf[i] if i<n-1 else lays[...]
            kq[:SPAN,base:base+m]=eye_of(row,SPAN,True)
            ohq[i]=jnp.transpose(eye_of(layq[i],SPAN,False).astype(F32)).astype(BF)
            base+=m
        vaug[:,W:]=(lax.broadcasted_iota(jnp.int32,(vaug.shape[0],W),1)<2).astype(F32).astype(BF)
        rhs[...]=jnp.zeros_like(rhs)
    nacc[...]=jnp.zeros_like(nacc)
    base=0
    lane=lax.broadcasted_iota(jnp.int32,(R,W),1)
    for i,m in enumerate(spans):
        ch=min(CH,m)
        kk=kf[i] if i<n-1 else ks[...]
        vaug[:m,:W]=vf[i] if i<n-1 else vs[...]
        kt=jnp.transpose(kk.astype(F32)).astype(BF)
        dot_=jnp.transpose(do[i].astype(F32))
        ot=jnp.transpose(o[i].astype(F32))
        scaled=[];
        for h in range(2):
            inv=1.0/l[i,0,h:h+1]
            scaled.append((dot_[h*E:(h+1)*E]*inv).astype(BF))
        sc=jnp.concatenate(scaled,axis=0)
        don=jnp.transpose(sc.astype(F32)).astype(BF)
        qq=q[i]
        zero=jnp.zeros((R,W),BF)
        for h in range(2):
            mine=(lane<E) if h==0 else (lane>=E)
            qm[h*R:(h+1)*R]=jnp.where(mine,qq,zero)
            dm[h*R:(h+1)*R]=jnp.where(mine,don,zero)
        dqs=[]
        for h in range(2):
            if i==0: tick(h)
            rhs[h*E:(h+1)*E]=scaled[h]
            rhs[(1-h)*E:(2-h)*E]=jnp.zeros((E,R),BF)
            delta=jnp.sum(scaled[h].astype(F32)*ot[h*E:(h+1)*E],axis=0,keepdims=True)
            hi=delta.astype(BF).astype(F32)
            lo=delta-hi
            spot=lax.broadcasted_iota(jnp.int32,(16,R),0)
            rhs[W:W+16]=jnp.where(spot==0,-hi,jnp.where(spot==1,-lo,0.0)).astype(BF)
            for c in range(0,m,ch):
                g=dot(vaug[c:c+ch],rhs[...])
                ds[c:c+ch,h*R:(h+1)*R]=(p[0,h,base+c:base+c+ch].astype(F32)*g).astype(BF)
            kq[SPAN:,base:base+m]=kt[h*E:(h+1)*E]
            both=dot(kq[:,base:base+m],ds[:m,h*R:(h+1)*R])
            dqs.append(both[SPAN:]*0.125)
            nacc[h]+=dot(both[:SPAN].astype(BF),ohq[i])
        dq[i]=jnp.transpose(jnp.concatenate(dqs,axis=0)).astype(BF)
        for c in range(0,m,ch):
            dk=dot(ds[c:c+ch],qm[...])
            dv=dot(p[0,0,base+c:base+c+ch],dm[:R])+dot(p[0,1,base+c:base+c+ch],dm[R:])
            if i<n-1:
                dkf[i,c:c+ch]=dk.astype(BF); dvf[i,c:c+ch]=dv.astype(BF)
            else:
                dks[c:c+ch]=dk.astype(BF); dvs[c:c+ch]=dv.astype(BF)
        base+=m
    for h in range(2):
        wide=jnp.concatenate([nacc[h],jnp.zeros((SPAN,SPAN),F32)],axis=1)
        rolled=pltpu.roll(wide,0,1,stride=1,stride_axis=0)
        t[0,h:h+1]=jnp.sum(rolled,axis=0,keepdims=True)
    tick(2)

def attend_back_call(q,kf,vf,ks,vs,layq,layf,lays,o,do,p,l,parts=()):
    n,R,D=q.shape; L=kf.shape[1]; S=ks.shape[0]; H=p.shape[0]*2; E=D//H; W=2*E
    KT=(n-1)*L+S
    full=lambda a: pl.BlockSpec(a.shape,lambda j:(0,)*a.ndim)
    rows=lambda: pl.BlockSpec((n,R,W),lambda j:(0,0,j))
    kb=lambda: pl.BlockSpec((n-1,L,W),lambda j:(0,0,j))
    sb=lambda: pl.BlockSpec((S,W),lambda j:(0,j))
    return pl.pallas_call(functools.partial(attend_back,n,L,S,R,E,H//2,bool(parts)),
      grid=(H//2,),
      in_specs=[rows(),kb(),kb(),sb(),sb(),full(layq),full(layf),full(lays),rows(),rows(),
        pl.BlockSpec((1,2,KT,R),lambda j:(j,0,0,0)),pl.BlockSpec((n,1,2,R),lambda j:(0,j,0,0))]+[pl.BlockSpec(memory_space=pl.ANY)]*len(parts),
      out_specs=[rows(),kb(),kb(),sb(),sb(),pl.BlockSpec((1,2,2*SPAN),lambda j:(j,0,0))]+[pl.BlockSpec(s.shape[4:],lambda j:(0,0)) for s in parts],
      out_shape=[jax.ShapeDtypeStruct((n,R,D),BF),jax.ShapeDtypeStruct(kf.shape,BF),jax.ShapeDtypeStruct(kf.shape,BF),
        jax.ShapeDtypeStruct(ks.shape,BF),jax.ShapeDtypeStruct(ks.shape,BF),jax.ShapeDtypeStruct((H//2,2,2*SPAN),F32)]
        +[jax.ShapeDtypeStruct(s.shape[4:],F32) for s in parts],
      scratch_shapes=[pltpu.VMEM((SPAN+E,KT),BF),pltpu.VMEM((L,2*W),BF),pltpu.VMEM((2*W,R),BF),pltpu.VMEM((L,2*R),BF),
        pltpu.VMEM((n,R,SPAN),BF),pltpu.VMEM((2,SPAN,SPAN),F32),pltpu.VMEM((2*R,W),BF),pltpu.VMEM((2*R,W),BF)]
        +sum((sum_scratch(s.shape[4],s.shape[5]//k) for s,k in zip(parts,(2,2,1)) for _ in range(k)),[])
        +([pltpu.SemaphoreType.DMA((5*SUM_COPIES,))]*2+[pltpu.SemaphoreType.DMA((5,))] if parts else []),
      compiler_params=pltpu.CompilerParams(vmem_limit_bytes=58*2**20,dimension_semantics=("arbitrary",),**(dict(collective_id=3,has_side_effects=True) if parts else {})),
      name="attend_back",
    )(q,kf,vf,ks,vs,layq,layf,lays,o,do,p,l,*parts)


MESH = pl.DeviceIdType.MESH


class Place:
    def __init__(self):
        dp = lax.axis_index("dp")
        self.x = lax.axis_index("blk")
        self.z, self.y, self.c = dp // 4, (dp // 2) % 2, dp % 2
        self.y1, self.x1 = (self.y + 1 - self.c) % 2, (self.x + self.c) % 2
        self.y2, self.x2 = (self.y + self.c) % 2, (self.x + 1 - self.c) % 2

    def device(self, z, y, c, x):
        return ((z * 2 + y) * 2 + c, x)

    def along_z(self, d):
        return self.device((self.z + d) % 4, self.y, self.c, self.x)

    def along_x(self):
        return self.device(self.z, self.y, self.c, 1 - self.x)

    def along_y(self):
        return self.device(self.z, 1 - self.y, self.c, self.x)

    def first(self):
        return self.device(self.z, self.y1, self.c, self.x1)

    def second(self):
        return self.device(self.z, self.y2, self.c, self.x2)

    def core(self):
        return self.device(self.z, self.y, 1 - self.c, self.x)

    def greet(self):
        barrier = pltpu.get_barrier_semaphore()
        partners = [self.along_z(d) for d in (1, 2, 3)] + [self.first(), self.second(), self.core()]
        for partner in partners:
            pl.semaphore_signal(barrier, inc=1, device_id=partner, device_id_type=MESH)
        pl.semaphore_wait(barrier, len(partners))


def remote(src, dst, sems, k, device):
    return pltpu.make_async_remote_copy(
        src_ref=src, dst_ref=dst, send_sem=sems[0].at[k], recv_sem=sems[1].at[k], device_id=device, device_id_type=MESH
    )


GATHER_COPIES = 10


def gather_stages(at, shard, whole, sems, local, base, cols=None):
    z, y, c, x = at.z, at.y, at.c, at.x
    cols = pl.ds(0, shard.shape[1]) if cols is None else cols
    shard = shard.at[:, cols]
    own = whole.at[z, y, c, x, :, cols]

    def group(yy, xx):
        return whole.at[:, yy, c, xx, :, cols]

    def copy(k):
        if k < 3:
            return remote(shard, own, sems, base + k, at.along_z(k + 1))
        view, device = {
            3: (group(y, x), at.first()),
            4: (group(y, x), at.second()),
            5: (group(y, x), at.core()),
            6: (group(at.y1, at.x1), at.second()),
            7: (group(at.y1, at.x1), at.core()),
            8: (group(at.y2, at.x2), at.core()),
            9: (group(1 - y, 1 - x), at.core()),
        }[k]
        return remote(view, view, sems, base + k, device)

    keep = pltpu.make_async_copy(shard, own, local)

    def one():
        keep.start()
        for k in range(3):
            copy(k).start()

    def two():
        keep.wait()
        for k in range(3):
            copy(k).wait_recv()
        for k in (3, 4, 5):
            copy(k).start()

    def three():
        copy(3).wait_recv()
        for k in (6, 7):
            copy(k).start()

    def four():
        copy(4).wait_recv()
        copy(8).start()
        copy(6).wait_recv()
        copy(9).start()

    def five():
        for k in (5, 7, 8, 9):
            copy(k).wait_recv()
        for k in range(10):
            copy(k).wait_send()

    return [one, two, three, four, five]


def start_kernel(count, tok_long, tok_short, *refs):
    shards, (xf, xs), wholes = refs[:count], refs[count : count + 2], refs[count + 2 : 2 * count + 2]
    send, recv, local = refs[2 * count + 2 :]
    at = Place()
    at.greet()
    sems, spare = (send, recv), GATHER_COPIES * count
    chains = [gather_stages(at, s, w, sems, local.at[i], GATHER_COPIES * i) for i, (s, w) in enumerate(zip(shards, wholes))]
    rows = tok_long.shape[1]
    long = remote(tok_long, xf.at[:, rows:], sems, spare, at.along_x())
    short = remote(tok_short, xs, sems, spare + 1, at.along_x())
    keep_long = pltpu.make_async_copy(tok_long, xf.at[:, :rows], local.at[count])
    keep_short = pltpu.make_async_copy(tok_short, xs, local.at[count + 1])

    def tokens_start():
        long.start()
        keep_long.start()

        @pl.when(at.x == 0)
        def _():
            short.start()
            keep_short.start()

    plan = spread(chains, range(count), (0, 1, 2, 3, 100), 200)
    for tick in sorted(plan):
        for stage in plan[tick]:
            stage()
        if tick == 0:
            tokens_start()
    long.wait()
    keep_long.wait()

    @pl.when(at.x == 0)
    def _():
        short.wait_send()
        keep_short.wait()

    @pl.when(at.x == 1)
    def _():
        short.wait_recv()


def start_call(tok_long, tok_short, shards):
    count = len(shards)
    n, rows, width = tok_long.shape
    outs = [jax.ShapeDtypeStruct((n, 2 * rows, width), BF), jax.ShapeDtypeStruct(tok_short.shape, BF)]
    outs += [jax.ShapeDtypeStruct((4, 2, 2, 2) + s.shape, s.dtype) for s in shards]
    anywhere = pl.BlockSpec(memory_space=pl.ANY)
    copies = GATHER_COPIES * count + 2
    return pl.pallas_call(
        functools.partial(start_kernel, count),
        in_specs=[anywhere] * (count + 2),
        out_specs=[anywhere] * (count + 2),
        out_shape=outs,
        scratch_shapes=[pltpu.SemaphoreType.DMA((copies,)), pltpu.SemaphoreType.DMA((copies,)), pltpu.SemaphoreType.DMA((count + 2,))],
        compiler_params=pltpu.CompilerParams(collective_id=0, has_side_effects=True),
        name="gather_first",
    )(tok_long, tok_short, *shards)


SUM_COPIES = 7


def sum_scratch(rows, columns):
    slab = (rows, columns)
    return [pltpu.VMEM((4, 2, 2) + slab, BF)] * 2 + [pltpu.VMEM((4,) + slab, BF)] * 3 + [pltpu.VMEM((3,) + slab, BF)]


def sum_stages(at, part, total, held, got_core, got_diag, got_one, got_two, got_z, sems, local, base, cols=None):
    z, y, c, x = at.z, at.y, at.c, at.x
    cols = pl.ds(0, total.shape[1]) if cols is None else cols

    def copy(k):
        if k > 3:
            d = k - 3
            return remote(held.at[(z + d) % 4, y, x], got_z.at[d - 1], sems, base + k, at.along_z(d))
        src, dst, device = [
            (part.at[:, :, 1 - c, :, :, cols], got_core, at.core()),
            (held.at[:, 1 - y, 1 - x], got_diag, at.second()),
            (held.at[:, at.y2, at.x2], got_two, at.second()),
            (held.at[:, at.y1, at.x1], got_one, at.first()),
        ][k]
        return remote(src, dst, sems, base + k, device)

    keep = pltpu.make_async_copy(part.at[:, :, c, :, :, cols], held, local)

    def one():
        copy(0).start()
        keep.start()

    def two():
        keep.wait()
        copy(0).wait_recv()

        def add(i, _):
            held[i] = (held[i].astype(F32) + got_core[i].astype(F32)).astype(BF)
            return 0

        lax.fori_loop(0, 4, add, 0)
        copy(1).start()
        copy(2).start()

    def three():
        copy(1).wait_recv()
        held[:, at.y1, at.x1] = (held[:, at.y1, at.x1].astype(F32) + got_diag[...].astype(F32)).astype(BF)
        copy(3).start()

    def four():
        copy(2).wait_recv()
        copy(3).wait_recv()
        mine = held[:, y, x].astype(F32) + got_one[...].astype(F32) + got_two[...].astype(F32)
        held[:, y, x] = mine.astype(BF)
        for k in (4, 5, 6):
            copy(k).start()

    def five():
        out = held[z, y, x].astype(F32)
        for d in (1, 2, 3):
            copy(3 + d).wait_recv()
            out = out + got_z[d - 1].astype(F32)
        total[:, cols] = out
        for k in range(7):
            copy(k).wait_send()

    return [one, two, three, four, five]


def small_stages(at, part, total, held, got, sems, base):
    def copy(k):
        device = [at.core, at.along_y, at.along_x][k]() if k < 3 else at.along_z(k - 2)
        return remote(held.at[min(k, 3)], got.at[k], sems, base + k, device)

    def one():
        held[0] = part[...]
        copy(0).start()

    def add(k):
        def run():
            copy(k).wait_recv()
            held[k + 1] = held[k] + got[k]
            for following in (k + 1,) if k < 2 else (3, 4, 5):
                copy(following).start()

        return run

    def five():
        parts = [held[3]]
        for d in (1, 2, 3):
            copy(2 + d).wait_recv()
            parts.append(got[2 + d])
        out = jnp.zeros_like(parts[0])
        for spot in range(4):
            for d in range(4):
                out = out + jnp.where((at.z - d + 4) % 4 == spot, parts[d], 0.0)
        total[...] = out
        for k in range(6):
            copy(k).wait_send()

    return [one, add(0), add(1), add(2), five]


def sum_kernel(count, *refs):
    parts, small_part = refs[:count], refs[count]
    totals, small_total = refs[count + 1 : 2 * count + 1], refs[2 * count + 1]
    scratch = refs[2 * count + 2 :]
    small_held, small_got, send, recv, local = scratch[-5:]
    at = Place()
    at.greet()
    sems = (send, recv)
    chains = [
        sum_stages(at, parts[i], totals[i], *scratch[6 * i : 6 * i + 6], sems, local.at[i], SUM_COPIES * i)
        for i in range(count)
    ]
    chains.append(small_stages(at, small_part, small_total, small_held, small_got, sems, SUM_COPIES * count))
    for turn in range(count + 5):
        for i in range(count + 1):
            if 0 <= turn - i < 5:
                chains[i][turn - i]()


def sum_call(parts, small):
    count = len(parts)
    scratch = sum((sum_scratch(*p.shape[4:]) for p in parts), [])
    scratch += [pltpu.VMEM((4,) + small.shape, F32), pltpu.VMEM((6,) + small.shape, F32)]
    copies = SUM_COPIES * count + 6
    scratch += [pltpu.SemaphoreType.DMA((copies,)), pltpu.SemaphoreType.DMA((copies,)), pltpu.SemaphoreType.DMA((count,))]
    anywhere = pl.BlockSpec(memory_space=pl.ANY)
    vmem = pl.BlockSpec(memory_space=pltpu.VMEM)
    return pl.pallas_call(
        functools.partial(sum_kernel, count),
        in_specs=[anywhere] * count + [vmem],
        out_specs=[vmem] * (count + 1),
        out_shape=[jax.ShapeDtypeStruct(p.shape[4:], F32) for p in parts] + [jax.ShapeDtypeStruct(small.shape, F32)],
        scratch_shapes=scratch,
        compiler_params=pltpu.CompilerParams(collective_id=1, has_side_effects=True, vmem_limit_bytes=56 * 2**20),
        name="sum_gradients",
    )(*parts, small)


GATHER_BEGIN, GATHER_LAG = (0, 1, 5, 9, 13), (0, 3, 5, 7, 100)
SUM_BEGIN, SUM_LAG = (1, 5, 9, 13, 16), (-100, 0, 2, 4, 7)


def spread(chains, begins, lags, ticks):
    plan = {}
    for i, (begin, stages) in enumerate(zip(begins, chains)):
        for lag, stage in zip(lags, stages):
            plan.setdefault(min(max(begin + lag, 0), ticks), []).append((begin + lag, -i, stage))
    return {tick: [stage for _, _, stage in sorted(group, key=lambda e: e[:2])] for tick, group in plan.items()}


def halves(width):
    return [pl.ds(0, width // 2), pl.ds(width // 2, width // 2)]


def ticker(plan, steps, at):
    def tick(u):
        for t in sorted(plan):
            if t == 2 * steps and u == 2 or t < 2 * steps and t % 2 == u:

                @pl.when(pl.program_id(0) == min(t // 2, steps - 1))
                def _(t=t):
                    if t == 0:
                        at.greet()
                    for stage in plan[t]:
                        stage()

    return tick


def gather_plan(shards, wholes, sems, local):
    at = Place()
    chains = []
    for shard, whole, parts in zip(shards, wholes, (1, 2, 2)):
        for cols in [None] if parts == 1 else halves(shard.shape[1]):
            chains.append(gather_stages(at, shard, whole, sems, local.at[len(chains)], GATHER_COPIES * len(chains), cols))
    return at, chains


def sum_plan(parts, totals, scratch, sems, local):
    at = Place()
    chains = []
    for part, total, count in zip(parts, totals, (2, 2, 1)):
        for cols in [None] if count == 1 else halves(total.shape[1]):
            i = len(chains)
            chains.append(sum_stages(at, part, total, *scratch[6 * i : 6 * i + 6], sems, local.at[i], SUM_COPIES * i, cols))
    return at, chains


EPSILON = 1e-06
THRESHOLDS = (12, 16, 23, 32, 46, 64, 91)
BOTH = ("dp", "blk")


def bucket_np(relative):
    magnitude = np.abs(relative)
    larger = 8 + sum((magnitude >= limit).astype(np.int64) for limit in THRESHOLDS)
    return np.where(magnitude < 8, magnitude, larger) + 16 * (relative > 0)


def bucket_rows(distance, buckets):
    return (bucket_np(distance)[:, None] == np.arange(buckets)[None, :]).astype(np.float32)


def norm_parts(x, gain):
    back = lax.rsqrt(jnp.mean(x * x, axis=-1, keepdims=True) + EPSILON)
    return (x * back * gain).astype(BF), back


def norm_back(d, x, back, gain):
    a = gain * d
    grad_gain = jnp.sum(d * x * back, axis=0)
    return back * a - x * back**3 * jnp.mean(a * x, axis=-1, keepdims=True), grad_gain


def mm(a, b, dims):
    return lax.dot_general(a, b, (dims, ((), ())), preferred_element_type=F32)


def gather_weights(gain_one, wq, wk, wv, wo, gain_two, wi, wt):
    full = lambda a: lax.all_gather(a, BOTH, axis=0, tiled=True)
    packed = full(jnp.concatenate([wq, wk, wv, wo, wi], axis=1))
    width = wq.shape[1]
    gains = full(jnp.stack([gain_one, gain_two], axis=1))
    return packed[:, : 3 * width], packed[:, 3 * width : 4 * width], packed[:, 4 * width :], full(wt), gains[:, 0], gains[:, 1]


def scatter_sums(dqkv, dwo, dwi, dwt, dg1, dg2):
    take = lambda a: lax.psum_scatter(a, BOTH, scatter_dimension=0, tiled=True)
    width = dwo.shape[1]
    packed = take(jnp.concatenate([dqkv, dwo, dwi], axis=1).astype(BF)).astype(F32)
    gains = take(jnp.stack([dg1, dg2], axis=1))
    parts = [packed[:, i * width : (i + 1) * width] for i in range(4)]
    return parts, packed[:, 4 * width :], take(dwt.astype(BF)).astype(F32), gains[:, 0], gains[:, 1]


def on_device(tokens, layout, lengths, gain_one, wq, wk, wv, wo, gain_two, wi, wt, table, grad_out):
    n, R, D = tokens.shape
    H = table.shape[1]
    G = lax.axis_size("blk")
    me = lax.axis_index("blk")
    L = layout.shape[1]
    S = L // 8
    order = jnp.argsort(-lengths, stable=True)
    place = jnp.argsort(order)
    tok = tokens[order]
    gout = grad_out[order]
    lay = layout[order]
    lens = lengths[order]

    def from_step(x, s):
        return lax.ppermute(x, "blk", [(i, (i - s) % G) for i in range(G)])

    near = G == 2 and lax.axis_size("dp") == 16
    first = tok[-1, :S]
    columns = lambda a, count: jnp.pad(a, ((0, 0), (0, count - a.shape[1])))
    if near:
        gains = columns(jnp.stack([gain_one, gain_two], axis=1), 128)
        xf, xs, *firsts = start_call(tok[:-1], first, [gains, wq, wk, wv])
        rows_of = lambda a: a.reshape(-1, a.shape[-1])
        gains, wq_all, wk_all, wv_all = [rows_of(a) for a in firsts]
        g1, g2 = gains[:, 0], gains[:, 1]
    else:
        pieces = [tok[:-1]] + [from_step(tok[:-1], s) for s in range(1, G)]
        xf = jnp.concatenate(pieces, axis=1)
        xs = jnp.where(me == 0, first, sum(lax.ppermute(first, "blk", [(0, i)]) for i in range(1, G)))
        wqkv, wo_all, wi_all, wt_all, g1, g2 = gather_weights(gain_one, wq, wk, wv, wo, gain_two, wi, wt)
        wq_all, wk_all, wv_all = [wqkv[:, i * D : (i + 1) * D] for i in range(3)]
    lay_turned = jnp.roll(lay, -me * R, axis=1)
    layq = lay_turned[:, None, :R]
    layf = lay_turned[:-1, None, :]
    lays = lay[-1:, :S]
    spots = (jnp.arange(L) + me * R) % L
    mask = jnp.where(spots[None, :, None] < lens[:-1, None, None], 0.0, -1e30).astype(F32)

    g1 = g1.astype(F32)
    g2 = g2.astype(F32)
    hidden = tok.reshape(n * R, D).astype(F32)
    normed, r1 = norm_parts(hidden, g1)
    xkeys = jnp.concatenate([xf.reshape((n - 1) * L, D), xs], axis=0)
    nkeys, _ = norm_parts(xkeys.astype(F32), g1)
    q = (mm(normed, wq_all, ((1,), (0,))).astype(BF) * jnp.asarray(0.125, BF)).reshape(n, R, D)
    k = mm(nkeys, wk_all, ((1,), (0,))).astype(BF)
    v = mm(nkeys, wv_all, ((1,), (0,))).astype(BF)
    cut = (n - 1) * L
    kf, ks = k[:cut].reshape(n - 1, L, D), k[cut:]
    vf, vs = v[:cut].reshape(n - 1, L, D), v[cut:]
    lane = np.arange(2 * SPAN)
    turned = np.where(lane >= SPAN, lane - 2 * SPAN, lane)
    urow = mm(table, bucket_rows(-turned, table.shape[0]).astype(BF), ((0,), (1,))).reshape(H // 2, 2, 2 * SPAN)
    o, p, l, *rest = attend_call(q, kf, vf, ks, vs, layq, layf, lays, mask, urow, [wo, wi, wt] if near else [])
    if near:
        wo_all, wi_all, wt_all = [rows_of(a) for a in rest]

    attended = o.reshape(n * R, D)
    resid = hidden + mm(attended, wo_all, ((1,), (0,)))
    normed_two, r2 = norm_parts(resid, g2)
    pre = mm(normed_two, wi_all, ((1,), (0,)))
    act, act_back = jax.vjp(lambda x: jax.nn.gelu(x, approximate=False), pre)
    act = act.astype(BF)
    mixed = (resid + mm(act, wt_all, ((1,), (0,)))).astype(BF)
    up = gout.reshape(n * R, D)
    dwt = mm(act, up, ((0,), (0,)))
    (dpre,) = act_back(mm(up, wt_all, ((1,), (1,))))
    dpre = dpre.astype(BF)
    dwi = mm(normed_two, dpre, ((0,), (0,)))
    dn2 = mm(dpre, wi_all, ((1,), (1,)))
    dresid, dg2 = norm_back(dn2, resid, r2, g2)
    dresid = dresid + up.astype(F32)
    low = dresid.astype(BF)
    dwo = mm(attended, low, ((0,), (0,)))
    datt = mm(low, wo_all, ((1,), (1,))).astype(BF).reshape(n, R, D)

    slabs = lambda a: a.astype(BF).reshape(4, 2, 2, 2, -1, a.shape[-1])
    parts = [slabs(dwt), slabs(dwi), slabs(dwo)] if near else []
    dq, dkf, dvf, dks, dvs, t, *rest = attend_back_call(q, kf, vf, ks, vs, layq, layf, lays, o, datt, p, l, parts)
    dtable = jnp.einsum(
        "hj,jb->bh", t.reshape(H, 2 * SPAN), bucket_rows(SPAN - 1 - lane, table.shape[0]), precision=lax.Precision.HIGHEST
    )
    dq = dq.reshape(n * R, D)
    dk = jnp.concatenate([dkf.reshape(cut, D), dks], axis=0)
    dv = jnp.concatenate([dvf.reshape(cut, D), dvs], axis=0)
    dnk = mm(dk, wk_all, ((1,), (1,))) + mm(dv, wv_all, ((1,), (1,)))
    dnf = dnk[:cut].reshape(n - 1, L, D)
    dns = dnk[cut:].astype(BF)
    far = sum(
        lax.ppermute(dnf[:, s * R : (s + 1) * R].astype(BF), "blk", [(i, (i + s) % G) for i in range(G)]).astype(F32)
        for s in range(1, G)
    )
    back = jnp.where(
        me == 0, dnk[cut:] + sum(lax.ppermute(dns, "blk", [(i, 0)]).astype(F32) for i in range(1, G)), 0.0
    )
    extra = jnp.concatenate([dnf[:, :R] + far, jnp.pad(back, ((0, R - S), (0, 0)))[None]], axis=0).reshape(n * R, D)
    dn1 = mm(dq, wq_all, ((1,), (1,))) + extra
    dwq = mm(normed, dq, ((0,), (0,)))
    dwk = mm(nkeys, dk, ((0,), (0,)))
    dwv = mm(nkeys, dv, ((0,), (0,)))
    dx, dg1 = norm_back(dn1, hidden, r1, g1)
    gtok = (dresid + dx).astype(BF)
    if near:
        gwt, gwi, gwo = rest
        small = jnp.concatenate([dg1, dg2, dtable.reshape(-1)]).reshape(-1, 128)
        small = jnp.pad(small, ((0, -small.shape[0] % 8), (0, 0)))
        *parts, small = sum_call([slabs(dwq), slabs(dwk), slabs(dwv)], small)
        parts.append(gwo)
        small = small.reshape(-1)
        mine = (lax.axis_index("dp") * G + me) * (D // 32)
        gg1, gg2 = [lax.dynamic_slice_in_dim(small, mine + i * D, D // 32) for i in range(2)]
        dtable = small[2 * D : 2 * D + table.size].reshape(table.shape)
    else:
        parts, gwi, gwt, gg1, gg2 = scatter_sums(jnp.concatenate([dwq, dwk, dwv], axis=1), dwo, dwi, dwt, dg1, dg2)
        dtable = lax.psum(dtable, BOTH)
    return (
        mixed.reshape(n, R, D)[place],
        gtok.reshape(n, R, D)[place],
        gg1,
        parts[0],
        parts[1],
        parts[2],
        parts[3],
        gg2,
        gwi,
        gwt,
        dtable,
    )


def solution(mesh):
    rows = P(BOTH, None)
    items = P("dp", "blk", None)
    return jax.shard_map(
        on_device,
        mesh=mesh,
        in_specs=(items, P("dp", None), P("dp"), P(BOTH), rows, rows, rows, rows, P(BOTH), rows, rows, P(), items),
        out_specs=(items, items, P(BOTH), rows, rows, rows, rows, P(BOTH), rows, rows, P()),
        check_vma=False,
    )
```

time: 1770 us -> 411 us (0.23)
  waiting for transfers between devices: 831 us -> 0.01 us
  matrix products: 476 us -> 121 us
  Pallas kernels: 0 us -> 227 us
  local copies, waits for them, and re-layouts: 245 us -> 35.7 us
  other arithmetic: 109 us -> 17.4 us
  blocking collectives: 81.5 us -> 0 us
    reduce_scatter x6 -> x0, waiting for transfers between devices: 525 us -> none  [the longest x1 142 us: on_device(): lax.psum_scatter(grad_outer, ('dp', 'blk'), scatter_dimension=0, tiled=True)]
    dot_general x98 -> x20, matrix products: 476 us -> 121 us  [the longest x19 120 us: mm(): return lax.dot_general(a, b, (dims, ((), ())), preferred_element_type=F32)]
    all_gather x8 -> x0, waiting for transfers between devices: 231 us -> none  [the longest x1 77.8 us: on_device(): value_piece = lax.all_gather(value_items, 'blk', axis=1, tiled=True)]
    pallas_call x0 -> x4, Pallas kernels: none -> 227 us  [the longest x1 67.5 us: attend_back_call(): pl.pallas_call(functools.partial(attend_back, n, L, S, R, E, H // 2, bool...]
    unnamed x2 -> x0, blocking collectives: 81.5 us -> none
    dot_general x8 -> x0, local copies, waits for them, and re-layouts: 74.4 us -> none  [block_scores(): jnp.einsum('sbqk,bh->shqk', onehot, table, preferred_element_type=jnp.flo...]
    ppermute x2, waiting for transfers between devices: 70 us -> 0.01 us  [the longest x1 0.01 us: on_device(): lax.ppermute(dns, 'blk', [(i, 0)]).astype(F32)]
    dynamic_update_slice x16 -> x0, local copies, waits for them, and re-layouts: 41.2 us -> none  [visit_advance(): lax.dynamic_update_slice_in_dim(grad_pair, pair_add, block_start, 1)]
  transfers between devices with their start and end apart: 16 -> 2, of which waited for: 11 -> 0; matrix products, arithmetic and copies ran while one was open for 36% -> 5% of each run, Pallas kernels for 0% -> 0%
where the time goes in v1:
time: 411 us; the launch traced here: 406 us
  Pallas kernels  227 us (55%)
  matrix products  121 us (29%)
  local copies, waits for them, and re-layouts  35.7 us (9%)
  other arithmetic  17.4 us (4%)
    dot_general x19, matrix products, mm(): return lax.dot_general(a, b, (dims, ((), ())), preferred_element_type=F32)  120 us
    pallas_call x1, Pallas kernels, attend_back_call(): pl.pallas_call(functools.partial(attend_back, n, L, S, R, E, H // 2, bool...  67.5 us
    pallas_call x1, Pallas kernels, attend_call(): pl.pallas_call(functools.partial(attend, n, L, S, R, E, H // 2, bool(shar...  67.1 us
    pallas_call x1, Pallas kernels, start_call(): pl.pallas_call(functools.partial(start_kernel, count), in_specs=[anywhere...  56.7 us
    pallas_call x1, Pallas kernels, sum_call(): pl.pallas_call(functools.partial(sum_kernel, count), in_specs=[anywhere]...  36.1 us
    unnamed x122, local copies, waits for them, and re-layouts  11 us
  transfers between devices with their start and end apart: 2, of which 0 were waited for; matrix products, arithmetic and copies ran while one was open for 5% of the time, Pallas kernels for 0%

profile of v1, /device:TPU:0, one launch (start us, length us, event | category | flops | bytes accessed | tf_op | source)
XLA Modules:
  0.0 405.6 jit_solution(14269560192678701323)
XLA Ops:
  0.7 0.8 neg.13
  1.5 0.6 sort.34
  3.2 1.3 gather_fusion.1
  5.1 0.6 gather_fusion
  5.8 1.0 slice.83.tok_long
  6.8 0.7 slice_bitcast_fusion.3.tok_short
  7.6 0.6 pad.12.refs_0_
  8.2 56.7 %gather_first.1 = (bf16[1,1024,768]{2,1,0:T(8,128)(2,1)}, bf16[128,768]{1,0:T(8,128)(2,1)}, bf16[4,2,2,2,24,128]{5,4,3,2,1,0:T(8,128)(2,1)}, bf16[4,2,2,2,24,768...) custom-call(bf16[1,512,768]{2,1,0:T(8,128)(2,1)} %slice.83.tok_long, ...), custom_call_target="tpu_custom_call" | custom-call | tf_op jit(solution)/shard_map/gather_first/pallas_call | solution.py:351
  64.9 1.9 fusion.6
  66.8 1.1 fusion.41
  68.2 3.4 convolution_convert_fusion.2
  71.6 1.3 slice_bitcast_fusion.1.refs_2_
  72.9 0.7 slice.89.refs_4_
  74.0 1.6 convolution_convert_fusion.3
  75.7 1.2 slice_bitcast_fusion.2.refs_1_
  76.9 0.7 slice.88.refs_3_
  78.0 0.6 gather_fusion.2
  81.0 0.8 reshape.312.refs_9_
  81.8 3.8 fusion.19
  85.6 1.1 fusion.27.refs_8_
  86.7 67.1 %attend.1 = (bf16[2,512,768]{2,1,0:T(8,128)(2,1)}, bf16[6,2,1152,512]{3,2,1,0:T(8,128)(2,1)}, f32[2,6,2,512]{3,2,1,0:T(2,128)}, bf16[4,2,2,2,24,768]{5,4,3,2,1,0...) custom-call(bf16[2,512,768]{2,1,0:T(8,128)(2,1)} %bitcast.106, ...), custom_call_target="tpu_custom_call" | custom-call | tf_op jit(solution)/shard_map/attend/pallas_call | solution.py:80
  153.8 4.9 %multiply_reduce_fusion.2 = (f32[1024]{0:T(1024)S(1)}, f32[1024,768]{1,0:T(8,128)}) fusion(bf16[1024,768]{1,0:T(8,128)(2,1)} %bitcast.113, bf16[768,768]{1,0:T(8,128)(2,1)} %bitcast.150, bf16[2,512,768]{2,1,0:T(8,128)(2,1)S(1)} %gather_fusion), kind=kOutput, calls=%fused_computation.57 | convolution fusion | flops 1211104256 | bytes 7475200 | tf_op jit(solution)/shard_map/dot_general | solution.py:578
  158.9 2.1 gather_fusion.4
  160.9 37.0 %multiply_convert_fusion = (bf16[1024,3072]{1,0:T(8,128)(2,1)}, f32[1024,3072]{1,0:T(8,128)}, f32[1024,3072]{1,0:T(8,128)}) fusion(bf16[768,3072]{1,0:T(8,128)(2,1)} %bitcast.137, f32[1024,768]{1,0:T(8,128)} %get-tuple-element.113, f32[768]{0:T(1024)S(1)} %convert_reduce_fusion, f32[1024]{0:T(1024)S(1)} %get-tuple-element.111), kind=kOutput, calls=%fused_computation.9 | convolution fusion | flops 5038669824 | bytes 39328768 | tf_op jit(solution)/shard_map/dot_general | solution.py:578
  197.9 15.7 %add_convert_fusion = bf16[1024,3072]{1,0:T(8,128)(2,1)} fusion(f32[1024,3072]{1,0:T(8,128)} %get-tuple-element.103, f32[1024,3072]{1,0:T(8,128)} %get-tuple-element.114, bf16[1024,768]{1,0:T(8,128)(2,1)S(1)} %bitcast.109, bf16[3072,768]{1,0:T(8,128)(2,1)} %bitcast.133), kind=kOutput, calls=%fused_computation.8 | convolution fusion | flops 4875878400 | bytes 37748736 | tf_op jit(solution)/shard_map/dot_general | solution.py:578
  213.6 9.9 %multiply_reduce_fusion = (f32[768]{0:T(1024)}, f32[1024]{0:T(1024)S(1)}, f32[1024,768]{1,0:T(8,128)S(1)}) fusion(f32[1024,768]{1,0:T(8,128)S(1)} %copy-done.9, f32[1024]{0:T(1024)S(1)} %get-tuple-element.111, f32[768]{0:T(1024)S(1)} %convert_reduce_fusion, bf16[1024,3072]{1,0:T(8,128)(2,1)} %add_convert_fusion, bf16[768,3072]{1,0:T(8,128)(2,1)} %bitcast.138), kind=kOutput, calls=%fused_computation.52 | convolution fusion | flops 4836554752 | bytes 17315840 | tf_op jit(solution)/shard_map/dot_general | solution.py:578
  223.5 7.1 %convolution_convert_fusion = bf16[768,3072]{1,0:T(8,128)(2,1)} fusion(bf16[1024,3072]{1,0:T(8,128)(2,1)S(1)} %copy-done.49, f32[1024,768]{1,0:T(8,128)S(1)} %copy-done.9, f32[768]{0:T(1024)S(1)} %convert_reduce_fusion, f32[1024]{0:T(1024)S(1)} %get-tuple-element.111), kind=kOutput, calls=%fused_computation.23 | convolution fusion | flops 4836556800 | bytes 14162944 | tf_op jit(solution)/shard_map/dot_general | solution.py:578
  230.6 1.2 convert_add_fusion
  232.0 2.5 convolution_convert_fusion.8
  234.5 0.6 copy-done.44
  235.1 2.6 convolution_convert_fusion.4
  237.7 6.9 %convolution_convert_fusion.1 = bf16[3072,768]{1,0:T(8,128)(2,1)} fusion(bf16[1024,3072]{1,0:T(8,128)(2,1)S(1)} %bitcast.155, bf16[1024,768]{1,0:T(8,128)(2,1)S(1)} %bitcast.110), kind=kOutput, calls=%fused_computation.24 | convolution fusion | flops 4834197504 | bytes 12582912 | tf_op jit(solution)/shard_map/dot_general | solution.py:578
  244.6 67.5 %attend_back.1 = (bf16[2,512,768]{2,1,0:T(8,128)(2,1)}, bf16[1,1024,768]{2,1,0:T(8,128)(2,1)}, bf16[1,1024,768]{2,1,0:T(8,128)(2,1)}, bf16[128,768]{1,0:T(8,128)...) custom-call(bf16[2,512,768]{2,1,0:T(8,128)(2,1)} %bitcast.107, ...), custom_call_target="tpu_custom_call" | custom-call | tf_op jit(solution)/shard_map/attend_back/pallas_call | solution.py:180
  312.2 3.2 fusion.20
  315.5 1.6 convolution_add_fusion
  317.4 1.7 copy-done.7
  319.1 1.1 slice.107
  320.2 1.0 collective-permute-start
  321.3 1.7 collective-permute-start.1
  323.1 3.0 convolution_convert_fusion.6
  326.1 2.9 convolution_convert_fusion.7
  329.0 6.1 %add_convert_fusion.1 = bf16[1024,768]{1,0:T(8,128)(2,1)} fusion(f32[1024,768]{1,0:T(8,128)S(1)} %copy-done.9, bf16[1024,3072]{1,0:T(8,128)(2,1)S(1)} %bitcast.157, bf16[3072,768]{1,0:T(8,128)(2,1)S(1)} %bitcast.136), kind=kOutput, calls=%fused_computation.55 | convolution fusion | flops 4833411072 | bytes 15728640 | tf_op jit(solution)/shard_map/dot_general | solution.py:578
  335.2 0.6 reshape.332
  335.9 4.0 bitcast_convert_fusion
  340.5 0.7 pad_clamp_fusion
  341.2 1.8 gather_fusion.3
  343.0 1.0 add_select_fusion.1
  344.2 1.8 slice_add_fusion
  346.3 1.1 copy-done.4
  347.5 1.5 copy-done.37
  349.3 3.6 fusion.18
  352.9 0.6 pad.14.refs_3_
  353.5 36.1 %sum_gradients.1 = (f32[24,768]{1,0:T(8,128)}, f32[24,768]{1,0:T(8,128)}, f32[24,768]{1,0:T(8,128)}, f32[16,128]{1,0:T(8,128)}) custom-call(bf16[4,2,2,2,24,768]{5,4,3,2,1,0:T(8,128)(2,1)} %bitcast.126, bf16[4,2,2,2,24,768]{5,4,3,2,1,0:T(8,128)(2,1)} %bitcast.125, bf16[4,2,2,2,24,768]{5,4,3,2,1,0:T(8,128)(2,1)} %bitcast.124, f32[16,128]{1,0:T(8,128)} %pad.14.refs_3_), custom_call_target="tpu_custom_call" | custom-call | tf_op jit(solution)/shard_map/sum_gradients/pallas_call | solution.py:490
  389.6 0.7 slice.70
  390.4 0.7 copy.42
  391.1 5.3 %fusion.15 = bf16[1024,768]{1,0:T(8,128)(2,1)} fusion(f32[1024,768]{1,0:T(8,128)} %copy-done.6, bf16[2,512,768]{2,1,0:T(8,128)(2,1)S(1)} %copy-done.4, f32[1024]{0:T(1024)S(1)} %broadcast_multiply_fusion, f32[1024]{0:T(1024)S(1)} %multiply_multiply_fusion.5, f32[768]{0:T(1024)S(1)} %copy-done.28, f32[1024]{0:T(1024)S(1)} %bitcast.130, ...), kind=kLoop, calls=%fused_computation.48 | loop fusion | flops 7077888 | bytes 12598272 | tf_op jit(solution)/shard_map/convert_element_type | solution.py:700
  396.4 3.4 gather_fusion.5
  399.8 1.4 fusion.42
  401.2 0.6 copy.54
  401.8 0.6 copy.55
  402.4 0.6 copy.56
  403.1 0.6 copy.57
  403.7 0.7 copy.58
  404.4 0.7 copy.59
  (148 shorter events, 7.6 us)
Async XLA Ops:
  0.6 4.5 %copy-start = (bf16[2,512,768]{2,1,0:T(8,128)(2,1)S(1)}, bf16[2,512,768]{2,1,0:T(8,128)(2,1)}, u32[]{:S(2)}) copy-start(bf16[2,512,768]{2,1,0:T(8,128)(2,1)} %param.15) | copy-start | bytes 4718596
  0.7 6.8 %copy-start.48 = (bf16[24]{0:T(256)(128)(2,1)S(1)}, bf16[24]{0:T(256)(128)(2,1)}, u32[]{:S(2)}) copy-start(bf16[24]{0:T(256)(128)(2,1)} %param.18) | copy-start | bytes 148
  0.7 6.8 %copy-start.47 = (bf16[24]{0:T(256)(128)(2,1)S(1)}, bf16[24]{0:T(256)(128)(2,1)}, u32[]{:S(2)}) copy-start(bf16[24]{0:T(256)(128)(2,1)} %param.23) | copy-start | bytes 148
  4.5 62.3 %copy-start.29 = (s32[2,1024]{1,0:T(2,128)}, s32[2,1024]{1,0:T(2,128)S(1)}, u32[]{:S(2)}) copy-start(s32[2,1024]{1,0:T(2,128)S(1)} %fusion.29) | copy-start | bytes 24580
  5.8 148.0 %copy-start.3 = (bf16[2,512,768]{2,1,0:T(8,128)(2,1)}, bf16[2,512,768]{2,1,0:T(8,128)(2,1)S(1)}, u32[]{:S(2)}) copy-start(bf16[2,512,768]{2,1,0:T(8,128)(2,1)S(1)} %gather_fusion) | copy-start | bytes 4718596
  66.8 6.7 %copy-start.32 = (f32[1152]{0:T(1024)}, f32[1152]{0:T(1024)S(1)}, u32[]{:S(2)}) copy-start(f32[1152]{0:T(1024)S(1)} %add_rsqrt_fusion) | copy-start | bytes 13828
  68.1 12.2 %copy-start.27 = (f32[768]{0:T(1024)}, f32[768]{0:T(1024)S(1)}, u32[]{:S(2)}) copy-start(f32[768]{0:T(1024)S(1)} %convert_reduce_fusion.1) | copy-start | bytes 9220
  71.6 2.0 copy-start.11
  71.6 2.0 copy-start.19
  71.6 2.4 copy-start.42
  75.7 2.3 copy-start.2
  75.7 3.5 slice-start
  76.9 3.9 copy-start.22
  76.9 3.9 copy-start.36
  80.8 4.8 %copy-start.13 = (bf16[2,512,768]{2,1,0:T(8,128)(2,1)}, bf16[2,512,768]{2,1,0:T(8,128)(2,1)S(1)}, u32[]{:S(2)}) copy-start(bf16[2,512,768]{2,1,0:T(8,128)(2,1)S(1)} %fusion.11) | copy-start | bytes 4718596
  197.9 15.7 %copy-start.9 = (f32[1024,768]{1,0:T(8,128)S(1)}, f32[1024,768]{1,0:T(8,128)}, u32[]{:S(2)}) copy-start(f32[1024,768]{1,0:T(8,128)} %get-tuple-element.113) | copy-start | bytes 9437188
  213.6 9.9 %copy-start.49 = (bf16[1024,3072]{1,0:T(8,128)(2,1)S(1)}, bf16[1024,3072]{1,0:T(8,128)(2,1)}, u32[]{:S(2)}) copy-start(bf16[1024,3072]{1,0:T(8,128)(2,1)} %add_convert_fusion) | copy-start | bytes 18874372
  230.6 1.4 copy-start.10
  230.6 7.1 %slice-start.3 = ((s8[6291456]{0:T(1024)(128)(4,1)}), s8[4194304]{0:T(1024)(128)(4,1)S(1)}, s32[]{:S(2)}) async-start(s8[6291456]{0:T(1024)(128)(4,1)} %bitcast.154), calls=%async_computation.3 | async-start | bytes 8388608
  232.0 2.5 copy-start.6
  232.0 3.1 copy-start.44
  232.0 5.7 %slice-start.4 = ((s8[6291456]{0:T(1024)(128)(4,1)}), s8[2097152]{0:T(1024)(128)(4,1)S(1)}, s32[]{:S(2)}) async-start(s8[6291456]{0:T(1024)(128)(4,1)} %bitcast.154), calls=%async_computation.4 | async-start | bytes 4194304
  244.6 67.5 %copy-start.43 = (bf16[4,2,2,2,24,768]{5,4,3,2,1,0:T(8,128)(2,1)S(1)}, bf16[4,2,2,2,24,768]{5,4,3,2,1,0:T(8,128)(2,1)}, u32[]{:S(2)}) copy-start(bf16[4,2,2,2,24,768]{5,4,3,2,1,0:T(8,128)(2,1)} %get-tuple-element.43) | copy-start | bytes 3538948
  312.2 3.3 copy-start.39
  312.2 3.3 copy-start.41
  312.2 3.3 copy-start.46
  317.1 4.1 %copy-start.8 = (f32[1152,768]{1,0:T(8,128)}, f32[1152,768]{1,0:T(8,128)S(1)}, u32[]{:S(2)}) copy-start(f32[1152,768]{1,0:T(8,128)S(1)} %convolution_add_fusion) | copy-start | bytes 10616836
  317.1 5.9 %copy-start.12 = (bf16[1,1024,768]{2,1,0:T(8,128)(2,1)S(1)}, bf16[1,1024,768]{2,1,0:T(8,128)(2,1)}, u32[]{:S(2)}) copy-start(bf16[1,1024,768]{2,1,0:T(8,128)(2,1)} %get-tuple-element.41) | copy-start | bytes 4718596
  317.2 5.9 %copy-start.20 = (bf16[128,768]{1,0:T(8,128)(2,1)S(1)}, bf16[128,768]{1,0:T(8,128)(2,1)}, u32[]{:S(2)}) copy-start(bf16[128,768]{1,0:T(8,128)(2,1)} %get-tuple-element.42) | copy-start | bytes 589828
  317.2 5.9 %copy-start.28 = (f32[768]{0:T(1024)S(1)}, f32[768]{0:T(1024)}, u32[]{:S(2)}) copy-start(f32[768]{0:T(1024)} %copy-done.27) | copy-start | bytes 9220
  317.2 5.9 %copy-start.33 = (f32[1152]{0:T(1024)S(1)}, f32[1152]{0:T(1024)}, u32[]{:S(2)}) copy-start(f32[1152]{0:T(1024)} %copy-done.32) | copy-start | bytes 13828
  317.4 1.7 copy-start.7
  320.2 23.9 %collective-permute-start = (bf16[1,512,768]{2,1,0:T(8,128)(2,1)}, bf16[1,512,768]{2,1,0:T(8,128)(2,1)}, u32[]{:S(2)}, u32[]{:S(2)}) collective-permute-start(bf16[1,512,768]{2,1,0:T(8,128)(2,1)} %slice.107), channel_id=1, source_target_pairs={{0,1},{1,0},{2,3},{3,2},{4,5},{5,4},{6,7},{7,6},{8,9},{9,8},{10,11... | collective-permute-start | bytes 2359304 | tf_op jit(solution)/shard_map/ppermute | solution.py:688
  321.3 4.8 %copy-start.38 = (bf16[1,1024,768]{2,1,0:T(8,128)(2,1)S(1)}, bf16[1,1024,768]{2,1,0:T(8,128)(2,1)}, u32[]{:S(2)}) copy-start(bf16[1,1024,768]{2,1,0:T(8,128)(2,1)} %get-tuple-element.53) | copy-start | bytes 4718596
  321.3 4.7 %copy-start.45 = (bf16[128,768]{1,0:T(8,128)(2,1)S(1)}, bf16[128,768]{1,0:T(8,128)(2,1)}, u32[]{:S(2)}) copy-start(bf16[128,768]{1,0:T(8,128)(2,1)} %get-tuple-element.54) | copy-start | bytes 589828
  321.3 21.7 %collective-permute-start.1 = (bf16[128,768]{1,0:T(8,128)(2,1)S(1)}, bf16[128,768]{1,0:T(8,128)(2,1)S(1)}, u32[]{:S(2)}, u32[]{:S(2)}) collective-permute-start(bf16[128,768]{1,0:T(8,128)(2,1)S(1)} %slice.108), channel_id=1, source_target_pairs={{1,0},{3,2},{5,4},{7,6},{9,8},{11,10},{13,12},{15,14},{17,16},{19,... | collective-permute-start | bytes 589832 | tf_op jit(solution)/shard_map/ppermute | solution.py:692
  323.0 6.0 %slice-start.1 = ((s8[4718592]{0:T(1024)(128)(4,1)}), s8[4194304]{0:T(1024)(128)(4,1)S(1)}, s32[]{:S(2)}) async-start(s8[4718592]{0:T(1024)(128)(4,1)} %bitcast.134), calls=%async_computation.1 | async-start | bytes 8388608
  323.1 6.0 %slice-start.5 = ((s8[6291456]{0:T(1024)(128)(4,1)}), s8[2097152]{0:T(1024)(128)(4,1)S(1)}, s32[]{:S(2)}) async-start(s8[6291456]{0:T(1024)(128)(4,1)} %bitcast.156), calls=%async_computation.5 | async-start | bytes 4194304
  326.1 3.0 slice-start.2
  326.1 3.0 slice-start.6
  329.0 6.2 %copy-start.30 = (f32[6,2,512]{2,1,0:T(2,128)S(1)}, f32[6,2,512]{2,1,0:T(2,128)}, u32[]{:S(2)}) copy-start(f32[6,2,512]{2,1,0:T(2,128)} %get-tuple-element.57) | copy-start | bytes 73732
  329.0 6.8 %copy-start.14 = (bf16[2,512,768]{2,1,0:T(8,128)(2,1)S(1)}, bf16[2,512,768]{2,1,0:T(8,128)(2,1)}, u32[]{:S(2)}) copy-start(bf16[2,512,768]{2,1,0:T(8,128)(2,1)} %copy-done.13) | copy-start | bytes 4718596
  335.8 4.0 copy-start.18
  335.8 4.0 copy-start.21
  335.8 4.6 %copy-start.31 = (f32[1,4,2,128]{3,2,1,0:T(2,128)S(1)}, f32[1,4,2,128]{3,2,1,0:T(2,128)}, u32[]{:S(2)}) copy-start(f32[1,4,2,128]{3,2,1,0:T(2,128)} %get-tuple-element.108) | copy-start | bytes 12292
  335.8 5.4 %copy-start.15 = (bf16[1024,768]{1,0:T(8,128)(2,1)S(1)}, bf16[1024,768]{1,0:T(8,128)(2,1)}, u32[]{:S(2)}) copy-start(bf16[1024,768]{1,0:T(8,128)(2,1)} %add_convert_fusion.1) | copy-start | bytes 4718596
  341.2 1.8 copy-start.34
  345.9 1.6 copy-start.4
  346.0 3.0 copy-start.37
  346.0 3.3 copy-start.40
  346.3 6.5 %copy-start.5 = (f32[2,512,768]{2,1,0:T(8,128)}, f32[2,512,768]{2,1,0:T(8,128)S(1)}, u32[]{:S(2)}) copy-start(f32[2,512,768]{2,1,0:T(8,128)S(1)} %pad_maximum_fusion) | copy-start | bytes 9437188
  349.3 3.6 copy-start.35
  391.1 14.1 %copy-start.1 = (bf16[2,512,768]{2,1,0:T(8,128)(2,1)S(1)}, bf16[2,512,768]{2,1,0:T(8,128)(2,1)}, u32[]{:S(2)}) copy-start(bf16[2,512,768]{2,1,0:T(8,128)(2,1)} %param.15) | copy-start | bytes 4718596
  396.4 4.8 %copy-start.26 = (f32[24,768]{1,0:T(8,128)S(1)}, f32[24,768]{1,0:T(8,128)}, u32[]{:S(2)}) copy-start(f32[24,768]{1,0:T(8,128)} %get-tuple-element.133) | copy-start | bytes 221188
  396.4 5.4 %copy-start.25 = (f32[24,768]{1,0:T(8,128)S(1)}, f32[24,768]{1,0:T(8,128)}, u32[]{:S(2)}) copy-start(f32[24,768]{1,0:T(8,128)} %get-tuple-element.134) | copy-start | bytes 221188
  396.4 6.1 %copy-start.24 = (f32[24,768]{1,0:T(8,128)S(1)}, f32[24,768]{1,0:T(8,128)}, u32[]{:S(2)}) copy-start(f32[24,768]{1,0:T(8,128)} %get-tuple-element.135) | copy-start | bytes 221188
  396.4 6.7 %copy-start.23 = (f32[24,768]{1,0:T(8,128)S(1)}, f32[24,768]{1,0:T(8,128)}, u32[]{:S(2)}) copy-start(f32[24,768]{1,0:T(8,128)} %get-tuple-element.136) | copy-start | bytes 221188
  396.4 7.3 %copy-start.17 = (f32[24,3072]{1,0:T(8,128)S(1)}, f32[24,3072]{1,0:T(8,128)}, u32[]{:S(2)}) copy-start(f32[24,3072]{1,0:T(8,128)} %get-tuple-element.138) | copy-start | bytes 884740
  396.4 8.0 %copy-start.16 = (f32[96,768]{1,0:T(8,128)S(1)}, f32[96,768]{1,0:T(8,128)}, u32[]{:S(2)}) copy-start(f32[96,768]{1,0:T(8,128)} %get-tuple-element.139) | copy-start | bytes 884740

commit v2 on v1

v2 whole, which is shorter than its diff:
```python
import functools
import math

import jax
import jax.numpy as jnp
import numpy as np
from jax import lax
from jax.experimental import pallas as pl
from jax.experimental.pallas import tpu as pltpu
from jax.sharding import PartitionSpec as P

F32=jnp.float32; BF=jnp.bfloat16
SPAN=256
CH=256
def dot(a,b): return lax.dot_general(a,b,(((1,),(0,)),((),())),preferred_element_type=F32)
def eye_of(row, width, reverse):
    spots=lax.broadcasted_iota(jnp.int32,(width,row.shape[1]),0)
    if reverse: spots=width-1-spots
    return (spots==row).astype(F32).astype(BF)

def attend(n,L,S,R,E, q,kf,vf,ks,vs,layq,layf,lays,mask,u,o,p,l, kcat,qcat,vt,s_ref,ohq):
    W=2*E
    spans=[L]*(n-1)+[S]
    @pl.when(pl.program_id(0)==0)
    def _():
        base=0
        for i,m in enumerate(spans):
            row=layf[i] if i<n-1 else lays[...]
            kcat[base:base+m,W:]=jnp.transpose(eye_of(row,SPAN,False).astype(F32)).astype(BF)
            ohq[i]=eye_of(layq[i],SPAN,False)
            base+=m
        vt[:,E:]=jnp.ones((2,vt.shape[1]-E,vt.shape[2]),BF)
    pair=pl.program_id(0)
    base=0
    for i,m in enumerate(spans):
        ch=min(CH,m)
        kcat[base:base+m,:W]=kf[i] if i<n-1 else ks[...]
        v=vf[i] if i<n-1 else vs[...]
        vtr=jnp.transpose(v.astype(F32)).astype(BF)
        vt[0,:E,:m]=vtr[:E]
        vt[1,:E,:m]=vtr[E:]
        qt=jnp.transpose(q[i].astype(F32)).astype(BF)
        outs=[]
        for h in range(2):
            urow=u[pl.ds(0,1),h,:] if False else u[0,h:h+1,:]
            toep=pltpu.roll(jnp.broadcast_to(urow,(SPAN,2*SPAN)),0,1,stride=1,stride_axis=0)[:,:SPAN].astype(BF)
            qcat[h*E:(h+1)*E]=qt[h*E:(h+1)*E]
            qcat[(1-h)*E:(2-h)*E]=jnp.zeros((E,R),BF)
            qcat[W:]=dot(toep,ohq[i]).astype(BF)
            m8=jnp.full((8,R),-jnp.inf,F32)
            for c in range(0,m,ch):
                s=dot(kcat[base+c:base+c+ch],qcat[...])
                if 0<i<n-1: s=s+mask[i,c:c+ch,:]
                s_ref[c:c+ch]=s
                m8=jnp.maximum(m8,jnp.max(s.reshape(ch//8,8,R),axis=0))
            top=jnp.max(m8,axis=0,keepdims=True)
            for c in range(0,m,ch):
                p[0,h,base+c:base+c+ch]=jnp.exp(s_ref[c:c+ch]-top).astype(BF)
            full=dot(vt[h,:,:m],p[0,h,base:base+m])
            total=full[E:E+1]
            l[i,0,h:h+1]=total
            outs.append(full[:E]/total)
        o[i]=jnp.transpose(jnp.concatenate(outs,axis=0)).astype(BF)
        base+=m

def attend_call(q,kf,vf,ks,vs,layq,layf,lays,mask,u):
    n,R,D=q.shape; L=kf.shape[1]; S=ks.shape[0]; H=u.shape[0]*2; E=D//H; W=2*E
    KT=(n-1)*L+S
    full=lambda a: pl.BlockSpec(a.shape,lambda j:(0,)*a.ndim)
    return pl.pallas_call(functools.partial(attend,n,L,S,R,E),
      grid=(H//2,),
      in_specs=[pl.BlockSpec((n,R,W),lambda j:(0,0,j)),
        pl.BlockSpec((n-1,L,W),lambda j:(0,0,j)),pl.BlockSpec((n-1,L,W),lambda j:(0,0,j)),
        pl.BlockSpec((S,W),lambda j:(0,j)),pl.BlockSpec((S,W),lambda j:(0,j)),
        full(layq),full(layf),full(lays),full(mask),pl.BlockSpec((1,2,2*SPAN),lambda j:(j,0,0))],
      out_specs=[pl.BlockSpec((n,R,W),lambda j:(0,0,j)),
        pl.BlockSpec((1,2,KT,R),lambda j:(j,0,0,0)),
        pl.BlockSpec((n,1,2,R),lambda j:(0,j,0,0))],
      out_shape=[jax.ShapeDtypeStruct((n,R,D),BF),jax.ShapeDtypeStruct((H//2,2,KT,R),BF),jax.ShapeDtypeStruct((n,H//2,2,R),F32)],
      scratch_shapes=[pltpu.VMEM((KT,W+SPAN),BF),pltpu.VMEM((W+SPAN,R),BF),pltpu.VMEM((2,E+16,L),BF),pltpu.VMEM((L,R),F32),pltpu.VMEM((n,SPAN,R),BF)],
      compiler_params=pltpu.CompilerParams(vmem_limit_bytes=56*2**20,dimension_semantics=("arbitrary",)),
      name="attend",
    )(q,kf,vf,ks,vs,layq,layf,lays,mask,u)

def attend_back(n,L,S,R,E, q,kf,vf,ks,vs,layq,layf,lays,o,do,p,l, dq,dkf,dvf,dks,dvs,t, kq,vaug,rhs,ds,ohq,nacc,qm,dm):
    W=2*E
    spans=[L]*(n-1)+[S]
    @pl.when(pl.program_id(0)==0)
    def _():
        base=0
        for i,m in enumerate(spans):
            row=layf[i] if i<n-1 else lays[...]
            kq[:SPAN,base:base+m]=eye_of(row,SPAN,True)
            ohq[i]=jnp.transpose(eye_of(layq[i],SPAN,False).astype(F32)).astype(BF)
            base+=m
        vaug[:,W:]=(lax.broadcasted_iota(jnp.int32,(vaug.shape[0],W),1)<2).astype(F32).astype(BF)
        rhs[...]=jnp.zeros_like(rhs)
    nacc[...]=jnp.zeros_like(nacc)
    base=0
    lane=lax.broadcasted_iota(jnp.int32,(R,W),1)
    for i,m in enumerate(spans):
        ch=min(CH,m)
        kk=kf[i] if i<n-1 else ks[...]
        vaug[:m,:W]=vf[i] if i<n-1 else vs[...]
        kt=jnp.transpose(kk.astype(F32)).astype(BF)
        dot_=jnp.transpose(do[i].astype(F32))
        ot=jnp.transpose(o[i].astype(F32))
        scaled=[];
        for h in range(2):
            inv=1.0/l[i,0,h:h+1]
            scaled.append((dot_[h*E:(h+1)*E]*inv).astype(BF))
        sc=jnp.concatenate(scaled,axis=0)
        don=jnp.transpose(sc.astype(F32)).astype(BF)
        qq=q[i]
        zero=jnp.zeros((R,W),BF)
        for h in range(2):
            mine=(lane<E) if h==0 else (lane>=E)
            qm[h*R:(h+1)*R]=jnp.where(mine,qq,zero)
            dm[h*R:(h+1)*R]=jnp.where(mine,don,zero)
        dqs=[]
        for h in range(2):
            rhs[h*E:(h+1)*E]=scaled[h]
            rhs[(1-h)*E:(2-h)*E]=jnp.zeros((E,R),BF)
            delta=jnp.sum(scaled[h].astype(F32)*ot[h*E:(h+1)*E],axis=0,keepdims=True)
            hi=delta.astype(BF).astype(F32)
            lo=delta-hi
            spot=lax.broadcasted_iota(jnp.int32,(16,R),0)
            rhs[W:W+16]=jnp.where(spot==0,-hi,jnp.where(spot==1,-lo,0.0)).astype(BF)
            for c in range(0,m,ch):
                g=dot(vaug[c:c+ch],rhs[...])
                ds[c:c+ch,h*R:(h+1)*R]=(p[0,h,base+c:base+c+ch].astype(F32)*g).astype(BF)
            kq[SPAN:,base:base+m]=kt[h*E:(h+1)*E]
            both=dot(kq[:,base:base+m],ds[:m,h*R:(h+1)*R])
            dqs.append(both[SPAN:]*0.125)
            nacc[h]+=dot(both[:SPAN].astype(BF),ohq[i])
        dq[i]=jnp.transpose(jnp.concatenate(dqs,axis=0)).astype(BF)
        for c in range(0,m,ch):
            dk=dot(ds[c:c+ch],qm[...])
            dv=dot(p[0,0,base+c:base+c+ch],dm[:R])+dot(p[0,1,base+c:base+c+ch],dm[R:])
            if i<n-1:
                dkf[i,c:c+ch]=dk.astype(BF); dvf[i,c:c+ch]=dv.astype(BF)
            else:
                dks[c:c+ch]=dk.astype(BF); dvs[c:c+ch]=dv.astype(BF)
        base+=m
    for h in range(2):
        wide=jnp.concatenate([nacc[h],jnp.zeros((SPAN,SPAN),F32)],axis=1)
        rolled=pltpu.roll(wide,0,1,stride=1,stride_axis=0)
        t[0,h:h+1]=jnp.sum(rolled,axis=0,keepdims=True)

def attend_back_call(q,kf,vf,ks,vs,layq,layf,lays,o,do,p,l):
    n,R,D=q.shape; L=kf.shape[1]; S=ks.shape[0]; H=p.shape[0]*2; E=D//H; W=2*E
    KT=(n-1)*L+S
    full=lambda a: pl.BlockSpec(a.shape,lambda j:(0,)*a.ndim)
    rows=lambda: pl.BlockSpec((n,R,W),lambda j:(0,0,j))
    kb=lambda: pl.BlockSpec((n-1,L,W),lambda j:(0,0,j))
    sb=lambda: pl.BlockSpec((S,W),lambda j:(0,j))
    return pl.pallas_call(functools.partial(attend_back,n,L,S,R,E),
      grid=(H//2,),
      in_specs=[rows(),kb(),kb(),sb(),sb(),full(layq),full(layf),full(lays),rows(),rows(),
        pl.BlockSpec((1,2,KT,R),lambda j:(j,0,0,0)),pl.BlockSpec((n,1,2,R),lambda j:(0,j,0,0))],
      out_specs=[rows(),kb(),kb(),sb(),sb(),pl.BlockSpec((1,2,2*SPAN),lambda j:(j,0,0))],
      out_shape=[jax.ShapeDtypeStruct((n,R,D),BF),jax.ShapeDtypeStruct(kf.shape,BF),jax.ShapeDtypeStruct(kf.shape,BF),
        jax.ShapeDtypeStruct(ks.shape,BF),jax.ShapeDtypeStruct(ks.shape,BF),jax.ShapeDtypeStruct((H//2,2,2*SPAN),F32)],
      scratch_shapes=[pltpu.VMEM((SPAN+E,KT),BF),pltpu.VMEM((L,2*W),BF),pltpu.VMEM((2*W,R),BF),pltpu.VMEM((L,2*R),BF),
        pltpu.VMEM((n,R,SPAN),BF),pltpu.VMEM((2,SPAN,SPAN),F32),pltpu.VMEM((2*R,W),BF),pltpu.VMEM((2*R,W),BF)],
      compiler_params=pltpu.CompilerParams(vmem_limit_bytes=56*2**20,dimension_semantics=("arbitrary",)),
      name="attend_back",
    )(q,kf,vf,ks,vs,layq,layf,lays,o,do,p,l)


EPSILON = 1e-06
FORWARD_PIECES = 2
FORWARD_WAYS = (0,) * 9
FORWARD_AT = (
    (-9, -8, -7, -6, -5),
    (-8, -7, -6, -5, -4),
    (-7, -6, -5, -4, -3),
    (-6, -5, -4, -3, -2),
    (-5, -4, -3, -2, 6),
    (-4, -3, -2, 6, 12),
    (-3, -2, 6, 12, 18),
    (-2, 6, 12, 18, 24),
)
FF_SUMS = 3
FF_SUM = (0, 2)
FF_SUM_LAG = (0, 3, 7, 11, 16)
BACK_SUM = (2, 2, 4)


MESH = pl.DeviceIdType.MESH


class Place:
    def __init__(self, mostly_y=False):
        dp = lax.axis_index("dp")
        self.x = lax.axis_index("blk")
        self.z, self.y, self.c = dp // 4, (dp // 2) % 2, dp % 2
        c = 1 if mostly_y else self.c
        self.y1, self.x1 = (self.y + 1 - c) % 2, (self.x + c) % 2
        self.y2, self.x2 = (self.y + c) % 2, (self.x + 1 - c) % 2

    def device(self, z, y, c, x):
        return ((z * 2 + y) * 2 + c, x)

    def along_z(self, d):
        return self.device((self.z + d) % 4, self.y, self.c, self.x)

    def along_x(self):
        return self.device(self.z, self.y, self.c, 1 - self.x)

    def along_y(self):
        return self.device(self.z, 1 - self.y, self.c, self.x)

    def first(self):
        return self.device(self.z, self.y1, self.c, self.x1)

    def second(self):
        return self.device(self.z, self.y2, self.c, self.x2)

    def core(self):
        return self.device(self.z, self.y, 1 - self.c, self.x)

    def greet(self):
        barrier = pltpu.get_barrier_semaphore()
        partners = [self.along_z(d) for d in (1, 2, 3)] + [self.first(), self.second(), self.core()]
        for partner in partners:
            pl.semaphore_signal(barrier, inc=1, device_id=partner, device_id_type=MESH)
        pl.semaphore_wait(barrier, len(partners))


def remote(src, dst, sems, k, device):
    return pltpu.make_async_remote_copy(
        src_ref=src, dst_ref=dst, send_sem=sems[0].at[k], recv_sem=sems[1].at[k], device_id=device, device_id_type=MESH
    )


GATHER_COPIES = 10


def gather_stages(at, shard, whole, sems, local, base, cols=None, plane=None):
    z, y, c, x = at.z, at.y, at.c, at.x
    cols = pl.ds(0, shard.shape[1]) if cols is None else cols
    shard = shard.at[:, cols]
    own = whole.at[z if plane is None else 0, y, c, x]
    keep = pltpu.make_async_copy(shard, own, local)

    def group(yy, xx):
        return whole.at[:, yy, c, xx]

    def copy(k):
        if k < 3:
            return remote(shard, own, sems, base + k, at.along_z(k + 1))
        view, device = {
            3: (group(y, x), at.first()),
            4: (group(y, x), at.second()),
            5: (group(y, x), at.core()),
            6: (group(at.y1, at.x1), at.second()),
            7: (group(at.y1, at.x1), at.core()),
            8: (group(at.y2, at.x2), at.core()),
            9: (group(1 - y, 1 - x), at.core()),
        }[k]
        return remote(view, view, sems, base + k, device)

    def one():
        def start():
            keep.start()
            for k in range(3):
                copy(k).start()

        start() if plane is None else pl.when(z == plane)(start)

    def two():
        if plane is None:
            keep.wait()
            for k in range(3):
                copy(k).wait_recv()
        else:
            pl.when(z == plane)(keep.wait)
            d = (z - plane + 4) % 4
            arrival = remote(shard, own, sems, base + d - 1, at.along_z(1))
            pl.when(z != plane)(arrival.wait_recv)
        for k in (3, 4, 5):
            copy(k).start()

    def three():
        copy(3).wait_recv()
        for k in (6, 7):
            copy(k).start()

    def four():
        copy(4).wait_recv()
        copy(8).start()
        copy(6).wait_recv()
        copy(9).start()

    def five():
        for k in (5, 7, 8, 9):
            copy(k).wait_recv()
        for k in range(3, 10):
            copy(k).wait_send()

        def sent():
            for k in range(3):
                copy(k).wait_send()

        sent() if plane is None else pl.when(z == plane)(sent)

    return [one, two, three, four, five]


def gather_stages_x(at, shard, whole, sems, local, base):
    z, y, c, x = at.z, at.y, at.c, at.x
    own = whole.at[z, y, c, x]
    keep = pltpu.make_async_copy(shard, own, local)

    def copy(k):
        if k == 0:
            return remote(shard, own, sems, base, at.along_x())
        view, device = {
            1: (whole.at[z, y, c], at.along_z(1)),
            2: (whole.at[z, y, c], at.along_z(2)),
            3: (whole.at[z, y, c], at.along_z(3)),
            4: (whole.at[:, y, c], at.along_y()),
            5: (whole.at[:, y, c], at.core()),
            6: (whole.at[:, 1 - y, c], at.core()),
        }[k]
        return remote(view, view, sems, base + k, device)

    def step(arrivals, starts):
        def run():
            for k in arrivals:
                copy(k).wait_recv()
            for k in starts:
                copy(k).start()

        return run

    def one():
        keep.start()
        copy(0).start()

    def two():
        keep.wait()
        step((0,), (1, 2, 3))()

    def five():
        step((5, 6), ())()
        for k in range(7):
            copy(k).wait_send()

    return [one, two, step((1, 2, 3), (4, 5)), step((4,), (6,)), five]


def small_stages(at, part, total, held, got, sems, base):
    def copy(k):
        device = [at.core, at.along_y, at.along_x][k]() if k < 3 else at.along_z(k - 2)
        return remote(held.at[min(k, 3)], got.at[k], sems, base + k, device)

    def one():
        held[0] = part[...]
        copy(0).start()

    def add(k):
        def run():
            copy(k).wait_recv()
            held[k + 1] = held[k] + got[k]
            for following in (k + 1,) if k < 2 else (3, 4, 5):
                copy(following).start()

        return run

    def five():
        parts = [held[3]]
        for d in (1, 2, 3):
            copy(2 + d).wait_recv()
            parts.append(got[2 + d])
        out = jnp.zeros_like(parts[0])
        for spot in range(4):
            for d in range(4):
                out = out + jnp.where((at.z - d + 4) % 4 == spot, parts[d], 0.0)
        total[...] = out
        for k in range(6):
            copy(k).wait_send()

    return [one, add(0), add(1), add(2), five]


def norm_rows(x):
    return lax.rsqrt(jnp.mean(x * x, axis=1, keepdims=True) + EPSILON)


def dot_nt(a, b):
    return lax.dot_general(a, b, (((1,), (1,)), ((), ())), preferred_element_type=F32)


def flipped(a):
    return jnp.transpose(a.astype(F32)).astype(BF)


TICKS = 6


def feed_forward_plan(sums):
    events = []
    for i, (stages, j) in enumerate(sums):
        for s, lag in enumerate(FF_SUM_LAG):
            events.append((TICKS * (j + 1) + FF_SUM[i % 2] + lag, stages[s]))
    plan = {}
    for when, stage in sorted(events, key=lambda e: e[0]):
        plan.setdefault(when, []).append(stage)
    return plan


def feed_forward(R, blocks, *refs):
    flag, att_, tok_, up_, wo_, grow = refs[:6]
    given = refs[6:8]
    refs = list(refs[8:])
    take = lambda k: [refs.pop(0) for _ in range(k)]
    mixed, dres, datt, dwo = take(4)
    last = FF_SUMS
    handed = [take(2) for _ in range(last, blocks)]
    (dgain,) = take(1)
    totals_in = take(last)
    (total_out,) = take(1)
    att, tok, up, wo, wbi, wbt, n2, n2t, resid, acc, dn2, act_t, dpre_s, parts_in, parts_out = take(15)
    sum_scratch = [take(5) for _ in range(2 * last)]
    send, recv, local = take(3)
    rows, width = att.shape
    block = wbi.shape[2]
    piece = rows // 4
    pieces = [pl.ds(i, piece) for i in range(0, rows, piece)]
    step = pl.program_id(0)
    slot = lax.rem(step, 2)
    at = Place()
    sems = (send, recv)

    sums = []
    for j in range(last):
        for which, (part, total) in enumerate([(parts_in.at[j], totals_in[j]), (parts_out.at[j], total_out)]):
            i = len(sums)
            chain = Sum(at, part, total, sum_scratch[i], sems, None, Sum.COPIES * i, None, j if which else None)
            sums.append((chain.stages, j))
    plan = feed_forward_plan(sums)

    def local_copy(a, b, k):
        return pltpu.make_async_copy(a, b, local.at[k])

    def weights(j):
        hidden = pl.ds(j * block, block)
        return [local_copy(given[0].at[:, hidden], wbi.at[j % 2], 4), local_copy(given[1].at[hidden], wbt.at[j % 2], 5)]

    def tick(t):
        for when in plan:
            if when < TICKS * blocks and when % TICKS == t:

                @pl.when(step == when // TICKS)
                def _(when=when):
                    for stage in plan[when]:
                        stage()

    @pl.when(step == 0)
    def _():
        loads = [local_copy(a, b, i) for i, (a, b) in enumerate([(tok_, tok), (att_, att), (wo_, wo), (up_, up)])]
        for load in loads + weights(0):
            load.start()
        at.greet()
        for load in loads:
            load.wait()
        for a in (tok, up):
            a[:R], a[R:] = swapped(flag, a[:R], a[R:])
        for b in pieces:
            x = tok[b].astype(F32) + dot(att[b], wo[...])
            resid[b] = x
            normed = (x * norm_rows(x) * grow[1:2]).astype(BF)
            n2[b] = normed
            n2t[:, b] = flipped(normed)
            acc[b] = x
            dn2[b] = jnp.zeros_like(x)

    for j in range(blocks):

        @pl.when(step == j)
        def _(j=j):
            for load in weights(j):
                load.wait()
            if j + 1 < blocks:
                for load in weights(j + 1):
                    load.start()

    for i, b in enumerate(pieces):
        tick(i)
        pre = dot(n2[b], wbi[slot])
        dact = dot_nt(up[b], wbt[slot])
        half = 0.5 + 0.5 * lax.erf(pre * 0.7071067811865476)
        act = (pre * half).astype(BF)
        dpre = (dact * (half + pre * (jnp.exp(-0.5 * pre * pre) * 0.3989422804014327))).astype(BF)
        acc[b] += dot(act, wbt[slot])
        dn2[b] += dot_nt(dpre, wbi[slot])
        act_t[:, b] = flipped(act)
        dpre_s[b] = dpre
    tick(4)
    grad_in = dot(n2t[...], dpre_s[...])
    tick(5)
    grad_out = dot(act_t[...], up[...])

    into_slabs(grad_in, parts_in.at[step])
    count = parts_out.shape[5]
    for i in range(8):
        parts_out[step, 0, i // 4, i // 2 % 2, i % 2] = grad_out[count * i : count * (i + 1)].astype(BF)
    hand = [
        [local_copy(parts_in.at[j], handed[j - last][0], 6 + 2 * j), local_copy(parts_out.at[j], handed[j - last][1], 7 + 2 * j)]
        for j in range(last, blocks)
    ]
    for j in range(last, blocks):

        @pl.when(step == j)
        def _(j=j):
            for copy in hand[j - last]:
                copy.start()

    @pl.when(step == blocks - 1)
    def _():
        rest = [stage for t in sorted(plan) if t >= TICKS * blocks for stage in plan[t]]

        def some(count):
            for _ in range(min(count, len(rest))):
                rest.pop(0)()

        ends = []
        some(2)
        for i, b in enumerate(pieces):
            n2[b] = acc[b].astype(BF)
        n2[:R], n2[R:] = swapped(flag, n2[:R], n2[R:])
        ends.append(local_copy(n2, mixed, 2))
        ends[-1].start()
        total = None
        for b in pieces:
            x, d = resid[b], dn2[b]
            back = norm_rows(x)
            a = grow[1:2] * d
            part = jnp.sum(d * x * back, axis=0, keepdims=True)
            total = part if total is None else total + part
            g = up[b].astype(F32) + back * a - x * (back * back * back) * jnp.mean(a * x, axis=1, keepdims=True)
            dn2[b] = g
            g = g.astype(BF)
            up[b] = g
            tok[b] = dot_nt(g, wo[...]).astype(BF)
            act_t[:width, b] = flipped(att[b])
            some(1)
        dgain[...] = total
        ends += [local_copy(dn2, dres, 3), local_copy(tok, datt, 4)]
        ends[-1].start()
        ends[-2].start()
        dpre_s[:width, :width] = dot(act_t[:width], up[...]).astype(BF)
        ends.append(local_copy(dpre_s.at[pl.ds(0, width), pl.ds(0, width)], dwo, 5))
        ends[-1].start()
        some(100)
        for end in ends + sum(hand, []):
            end.wait()


def feed_forward_call(flag, att, tokens, up, wo, grow, wi, wt):
    rows, D = tokens.shape
    R = rows // 2
    blocks = 4
    last = FF_SUMS
    block = wi.shape[1] // blocks
    share_in, share_out = (D // 32, block), (wt.shape[0] // 32, D)
    anywhere = pl.BlockSpec(memory_space=pl.ANY)
    whole = lambda shape: pl.BlockSpec(shape, lambda j: (0,) * len(shape))
    vmem = lambda *s: pltpu.VMEM(s, BF)
    wide = lambda *s: pltpu.VMEM(s, F32)
    slab_in, slab_out = (4, 2, 2, 2) + share_in, (1, 2, 2, 2) + share_out
    outs = [((rows, D), BF), ((rows, D), F32), ((rows, D), BF), ((D, D), BF)] + [(slab_in, BF), (slab_out, BF)] * (blocks - last)
    small = [((1, D), F32)] + [(share_in, F32)] * last + [(share_out, F32)]
    copies = max(Sum.COPIES * 2 * last, 1)
    scratch = [vmem(rows, D)] * 3 + [vmem(D, D), vmem(2, D, block), vmem(2, block, D), vmem(rows, D), vmem(D, rows)]
    scratch += [wide(rows, D)] * 3 + [vmem(block, rows), vmem(rows, block), vmem(blocks, *slab_in), vmem(blocks, *slab_out)]
    scratch += (Sum.scratch(4, *share_in, 0) + Sum.scratch(1, *share_out, 0)) * last
    scratch += [pltpu.SemaphoreType.DMA((copies,))] * 2 + [pltpu.SemaphoreType.DMA((6 + 2 * blocks,))]
    return pl.pallas_call(
        functools.partial(feed_forward, R, blocks),
        grid=(blocks,),
        in_specs=[whole(flag.shape)] + [anywhere] * 4 + [whole(grow.shape)] + [anywhere] * 2,
        out_specs=[anywhere] * len(outs) + [whole(s) for s, _ in small],
        out_shape=[jax.ShapeDtypeStruct(*s) for s in outs + small],
        scratch_shapes=scratch,
        compiler_params=pltpu.CompilerParams(
            vmem_limit_bytes=60 * 2**20, dimension_semantics=("arbitrary",), collective_id=2, has_side_effects=True
        ),
        name="feed_forward",
    )(flag, att, tokens, up, wo, grow, wi, wt)


def turn_plan(chains, places):
    plan = {}
    for chain, at in zip(chains, places):
        for place, stage in zip(at, chain):
            plan.setdefault(place, []).insert(0, stage)
    return plan


def together(*chains):
    def stage(s):
        def run():
            for chain in chains:
                chain[s]()

        return run

    return [stage(s) for s in range(len(chains[0]))]


def unslab(slabs, flat):
    rows = slabs.shape[4]
    for i in range(16):
        pair = [slabs[i // 4, i // 2 % 2, i % 2, x] for x in range(2)]
        flat[2 * rows * i : 2 * rows * (i + 1)] = jnp.concatenate(pair, axis=0)


def normed_rows(x, gain):
    x = x.astype(F32)
    return (x * norm_rows(x) * gain).astype(BF)


def block_chain(ats, shard_in, shard_out, j, whole_in, whole_out, sems, local, k):
    width = whole_in.shape[5]
    return [
        gather_stages(ats[0], shard_in, whole_in, sems, local.at[k], GATHER_COPIES * k, pl.ds(j * width, width)),
        gather_stages(ats[1], shard_out, whole_out, sems, local.at[k + 1], GATHER_COPIES * (k + 1), None, j),
    ]


def swapped(flag, a, b):
    turn = flag[0:1, 0:1] > 0
    return jnp.where(turn, b, a), jnp.where(turn, a, b)


def forward_kernel(R, L, S, E, pairs, *refs):
    flag, tokens, layt, lays, u = refs[:5]
    shards = refs[5:12]
    refs = list(refs[12:])
    take = lambda k: [refs.pop(0) for _ in range(k)]
    o, pa, pb, cs, grow = take(5)
    kept = take(7)
    wholes = take(6)
    kcat, qcat, vt, s_ref, ohq, xfar, xshort, flat, normed, tok, held, stats = take(12)
    q, kf, vf, ks, vs, nkt, nst = inner = take(7)
    slabs = take(4)
    send, recv, local = take(3)
    W = 2 * E
    D = tok.shape[2]
    at = Place()
    sems = (send, recv)
    ways = [(at, Place(True))[i] for i in FORWARD_WAYS]
    targets = slabs + wholes[3:]
    chains = []
    for i, cols in [(i, None) for i in range(5)] + [(i, cols) for i in (5, 6) for cols in pieces_of(shards[i].shape[1])]:
        k = len(chains)
        view = targets[i] if cols is None else targets[i].at[:, :, :, :, :, cols]
        chains.append(gather_stages(ways[k], shards[i], view, sems, local.at[k], GATHER_COPIES * k, cols))
    count = len(chains)
    chains = [together(chains[0], chains[1])] + chains[2:]
    plan = turn_plan(chains, FORWARD_AT)
    spare = GATHER_COPIES * count
    long = remote(tok.at[0], xfar, sems, spare, at.along_x())
    short = remote(tok.at[1, pl.ds(0, S)], xshort, sems, spare + 1, at.along_x())
    out = lambda i, a, b: pltpu.make_async_copy(a, b, local.at[count + i])
    weights_out = [out(i, slabs[1 + i], wholes[i]) for i in range(3)]
    kept_out = [out(3 + i, a, b) for i, (a, b) in enumerate(zip(inner, kept))]

    def send_tokens():
        long.start()
        pl.when(at.x == 0)(short.start)

    def turn(t):
        for stage in plan.get(t, []):
            stage()

    step = pl.program_id(0)
    pair = lax.rem(step, pairs)

    @pl.when(step == 0)
    def _():
        at.greet()
        turn(-9)
        tok[0], tok[1] = swapped(flag, tokens[0], tokens[1])
        send_tokens()
        for i, (base, row) in enumerate([(0, layt[0]), (L, lays[...])]):
            kcat[base : base + row.shape[1], W:] = jnp.transpose(eye_of(row, SPAN, False).astype(F32)).astype(BF)
            ohq[i] = eye_of(layt[i, :, :R], SPAN, False)
        vt[:, E:] = jnp.ones((2, vt.shape[1] - E, vt.shape[2]), BF)
        for t in range(-8, -4):
            turn(t)
        gslab = slabs[0]
        columns = jnp.concatenate(
            [gslab[i // 8, i // 4 % 2, i // 2 % 2, i % 2].astype(F32) for i in range(32)], axis=0
        )
        grow[...] = jnp.transpose(columns)[:8]
        gain = grow[0:1]
        weights_out[0].start()
        unslab(slabs[1], flat.at[0])
        for i in range(2):
            normed[i] = normed_rows(tok[i], gain)
            q[i] = (dot(normed[i], flat[0]).astype(BF).astype(F32) * 0.125).astype(BF)
        turn(-4)
        weights_out[1].start()
        unslab(slabs[2], flat.at[0])
        kf[:R] = dot(normed[0], flat[0]).astype(BF)
        turn(-3)
        weights_out[2].start()
        unslab(slabs[3], flat.at[1])
        vf[:R] = dot(normed[0], flat[1]).astype(BF)
        kept_out[0].start()
        turn(-2)

    @pl.when(step == pairs)
    def _():
        nkt[:, :R] = flipped(normed[0])
        nst[...] = flipped(normed[1])
        long.wait()

        @pl.when(at.x == 0)
        def _():
            short.wait_send()

        @pl.when(at.x == 1)
        def _():
            short.wait_recv()

        @pl.when(at.x == 0)
        def _():
            xshort[...] = tok[1, :S]

        gain = grow[0:1]
        normed[0] = normed_rows(xfar[...], gain)
        normed[1, :S] = normed_rows(xshort[...], gain)
        kf[R:] = dot(normed[0], flat[0]).astype(BF)
        vf[R:] = dot(normed[0], flat[1]).astype(BF)
        ks[...] = dot(normed[1, :S], flat[0]).astype(BF)
        vs[...] = dot(normed[1, :S], flat[1]).astype(BF)
        nkt[:, R:L] = flipped(normed[0])
        nkt[:, L:] = flipped(normed[1, :S])
        for copy in kept_out[1:]:
            copy.start()

    steps = 2 * pairs

    def tick(spot):
        for t in sorted(plan):
            if t >= 2 * steps and spot == 2 or 0 <= t < 2 * steps and t % 2 == spot:

                @pl.when(step == min(t // 2, steps - 1))
                def _(t=t):
                    turn(t)

    here = pl.ds(pl.multiple_of(pair * W, W), W)

    def attend_to(i, base, m, keys, values, into, ticking):
        ch = min(CH, m)
        kcat[base : base + m, :W] = keys
        vt[0, :E, :m], vt[1, :E, :m] = jnp.split(flipped(values), 2, axis=0)
        qt = flipped(q[i, :, here])
        found = []
        for h in range(2):
            if ticking:
                tick(h)
            toep = pltpu.roll(jnp.broadcast_to(u[0, h : h + 1], (SPAN, 2 * SPAN)), 0, 1, stride=1, stride_axis=0)
            qcat[h * E : (h + 1) * E] = qt[h * E : (h + 1) * E]
            qcat[(1 - h) * E : (2 - h) * E] = jnp.zeros((E, R), BF)
            qcat[W:] = dot(toep[:, :SPAN].astype(BF), ohq[i]).astype(BF)
            top = jnp.full((8, R), -jnp.inf, F32)
            for c in range(0, m, ch):
                s = dot(kcat[base + c : base + c + ch], qcat[...])
                s_ref[c : c + ch] = s
                top = jnp.maximum(top, jnp.max(s.reshape(ch // 8, 8, R), axis=0))
            top = jnp.max(top, axis=0, keepdims=True)
            for c in range(0, m, ch):
                into[h, c : c + ch] = jnp.exp(s_ref[c : c + ch] - top).astype(BF)
            full = dot(vt[h, :, :m], into[h, :m])
            found.append((top, full[E : E + 1], full[:E]))
        return found

    def heads(parts):
        return jnp.transpose(jnp.concatenate(parts, axis=0)).astype(BF)

    @pl.when(step < pairs)
    def _():
        found = attend_to(0, 0, R, kf[:R, here], vf[:R, here], pa.at[0], True)
        for h, (top, total, full) in enumerate(found):
            stats[pair, 2 * h : 2 * h + 1] = top
            stats[pair, 2 * h + 1 : 2 * h + 2] = total
            held[pair, h * E : (h + 1) * E] = full

    @pl.when(step >= pairs)
    def _():
        m = L - R
        found = attend_to(0, R, m, kf[R:, here], vf[R:, here], pb.at[0, :, pl.ds(0, m)], True)
        parts = []
        for h, (top, total, full) in enumerate(found):
            first, first_total = stats[pair, 2 * h : 2 * h + 1], stats[pair, 2 * h + 1 : 2 * h + 2]
            most = jnp.maximum(first, top)
            a, b = jnp.exp(first - most), jnp.exp(top - most)
            back = 1.0 / (a * first_total + b * total)
            cs[0, 0, h : h + 1] = a * back
            cs[1, 0, h : h + 1] = b * back
            parts.append(held[pair, h * E : (h + 1) * E] * (a * back) + full * (b * back))
        o[0] = heads(parts)
        found = attend_to(1, L, S, ks[:, here], vs[:, here], pb.at[0, :, pl.ds(m, S)], False)
        for h, (top, total, full) in enumerate(found):
            cs[2, 0, h : h + 1] = 1.0 / total
        o[1] = heads([full / total for _, total, full in found])

    tick(2)

    @pl.when(step == steps - 1)
    def _():
        for copy in weights_out + kept_out:
            copy.wait()


def pieces_of(width):
    return [pl.ds(i * width // FORWARD_PIECES, width // FORWARD_PIECES) for i in range(FORWARD_PIECES)]


def forward_call(flag, tokens, layt, lays, u, shards, S):
    n, R, D = tokens.shape
    L = layt.shape[2]
    pairs = u.shape[0]
    E = D // (2 * pairs)
    W = 2 * E
    KT = L + S
    whole = lambda shape: pl.BlockSpec(shape, lambda j: (0,) * len(shape))
    anywhere = pl.BlockSpec(memory_space=pl.ANY)
    vmem = lambda *s: pltpu.VMEM(s, BF)
    wide = lambda *s: pltpu.VMEM(s, F32)
    early = lambda j: jnp.minimum(j, pairs - 1)
    late = lambda j: jnp.maximum(j - pairs, 0)
    kept = [(n, R, D), (L, D), (L, D), (S, D), (S, D), (D, KT), (D, R)]
    chains = 5 + 2 * FORWARD_PIECES
    copies = GATHER_COPIES * chains + 2
    gathered = [(4, 2, 2, 2) + s.shape for s in shards]
    filled = gathered[1:]
    blocked = [
        ((n, R, D), BF, pl.BlockSpec((n, R, W), lambda j: (0, 0, late(j)))),
        ((pairs, 2, R, R), BF, pl.BlockSpec((1, 2, R, R), lambda j: (early(j), 0, 0, 0))),
        ((pairs, 2, KT - R, R), BF, pl.BlockSpec((1, 2, KT - R, R), lambda j: (late(j), 0, 0, 0))),
        ((3, pairs, 2, R), F32, pl.BlockSpec((3, 1, 2, R), lambda j: (0, late(j), 0, 0))),
        ((8, D), F32, whole((8, D))),
    ]
    return pl.pallas_call(
        functools.partial(forward_kernel, R, L, S, E, pairs),
        grid=(2 * pairs,),
        in_specs=[whole(flag.shape), whole(tokens.shape), whole(layt.shape), whole(lays.shape)]
        + [pl.BlockSpec((1, 2, 2 * SPAN), lambda j: (lax.rem(j, pairs), 0, 0))]
        + [anywhere] * 7,
        out_specs=[b[2] for b in blocked] + [anywhere] * (len(kept) + len(filled)),
        out_shape=[jax.ShapeDtypeStruct(*b[:2]) for b in blocked] + [jax.ShapeDtypeStruct(s, BF) for s in kept + filled],
        scratch_shapes=[vmem(KT, W + SPAN), vmem(W + SPAN, R), vmem(2, E + 16, R), wide(R, R), vmem(n, SPAN, R)]
        + [vmem(R, D), vmem(S, D), vmem(2, D, D), vmem(n, R, D), vmem(n, R, D), wide(pairs, W, R), wide(pairs, 8, R)]
        + [vmem(*s) for s in kept]
        + [vmem(*s) for s in gathered[:4]]
        + [pltpu.SemaphoreType.DMA((copies,))] * 2
        + [pltpu.SemaphoreType.DMA((chains + 10,))],
        compiler_params=pltpu.CompilerParams(
            vmem_limit_bytes=60 * 2**20, dimension_semantics=("arbitrary",), collective_id=0, has_side_effects=True
        ),
        name="forward",
    )(flag, tokens, layt, lays, u, *shards)


class Sum:
    COPIES = 7

    def __init__(self, at, part, total, scratch, sems, local, base, cols=None, plane=None):
        self.at, self.part, self.total, self.sems, self.base, self.plane = at, part, total, sems, base, plane
        self.cols = pl.ds(0, total.shape[1]) if cols is None else cols
        self.acc, self.got_diag, self.got_one, self.got_two, self.got_z = scratch[:5]
        self.held = scratch[5] if len(scratch) > 5 else None
        if self.held is not None:
            self.keep = pltpu.make_async_copy(part.at[:, :, at.c, :, :, self.cols], self.held, local)
        self.stages = [self.one, self.two, self.three, self.four, self.five]

    @staticmethod
    def scratch(depth, rows, columns, held):
        slab = (rows, columns)
        shapes = [(depth, 2, 2) + slab] + [(depth,) + slab] * 3 + [(3,) + slab] + [(depth, 2, 2) + slab] * held
        return [pltpu.VMEM(s, BF) for s in shapes]

    def send(self, k):
        at, acc = self.at, self.acc
        if k > 3:
            d = k - 3
            src, dst, device = acc.at[(at.z + d) % 4, at.y, at.x], self.got_z.at[d - 1], at.along_z(d)
        else:
            src, dst, device = [
                (self.part.at[:, :, 1 - at.c, :, :, self.cols], acc, at.core()),
                (acc.at[:, 1 - at.y, 1 - at.x], self.got_diag, at.second()),
                (acc.at[:, at.y2, at.x2], self.got_two, at.second()),
                (acc.at[:, at.y1, at.x1], self.got_one, at.first()),
            ][k]
        return remote(src, dst, self.sems, self.base + k, device)

    def to_plane(self):
        at = self.at
        d = (self.plane - at.z + 4) % 4
        k = self.base + 3 + d
        return pltpu.make_async_remote_copy(
            src_ref=self.acc.at[0, at.y, at.x],
            dst_ref=self.got_z.at[d - 1],
            send_sem=self.sems[0].at[k],
            recv_sem=self.sems[1].at[k],
            device_id=at.device(self.plane, at.y, at.c, at.x),
            device_id_type=MESH,
        )

    def one(self):
        self.send(0).start()
        if self.held is not None:
            self.keep.start()

    def two(self):
        at, acc = self.at, self.acc
        if self.held is not None:
            self.keep.wait()
        self.send(0).wait_recv()

        def add(i, _):
            for yy in range(2):
                own = self.held[i, yy] if self.held is not None else self.part[i, yy, at.c, :, :, self.cols]
                acc[i, yy] = (acc[i, yy].astype(F32) + own.astype(F32)).astype(BF)
            return 0

        lax.fori_loop(0, acc.shape[0], add, 0)
        self.send(1).start()
        self.send(2).start()

    def three(self):
        at, acc = self.at, self.acc
        self.send(1).wait_recv()
        acc[:, at.y1, at.x1] = (acc[:, at.y1, at.x1].astype(F32) + self.got_diag[...].astype(F32)).astype(BF)
        self.send(3).start()

    def four(self):
        at, acc = self.at, self.acc
        self.send(2).wait_recv()
        self.send(3).wait_recv()
        mine = acc[:, at.y, at.x].astype(F32) + self.got_one[...].astype(F32) + self.got_two[...].astype(F32)
        acc[:, at.y, at.x] = mine.astype(BF)
        if self.plane is None:
            for k in (4, 5, 6):
                self.send(k).start()
        else:

            @pl.when(at.z != self.plane)
            def _():
                self.to_plane().start()

    def five(self):
        at = self.at

        def collect():
            out = self.acc[at.z if self.plane is None else 0, at.y, at.x].astype(F32)
            for d in (1, 2, 3):
                arrival = remote(self.got_z.at[d - 1], self.got_z.at[d - 1], self.sems, self.base + 3 + d, at.along_z(d))
                arrival.wait_recv()
                out = out + self.got_z[d - 1].astype(F32)
            self.total[:, self.cols] = out

        for k in range(4):
            self.send(k).wait_send()
        if self.plane is None:
            collect()
            for k in (4, 5, 6):
                self.send(k).wait_send()
        else:
            pl.when(at.z == self.plane)(collect)

            @pl.when(at.z != self.plane)
            def _():
                self.to_plane().wait_send()


def into_slabs(flat, slabs):
    rows = slabs.shape[4]
    for i in range(32):
        slabs[i // 8, i // 4 % 2, i // 2 % 2, i % 2] = flat[rows * i : rows * (i + 1)].astype(BF)


def backward_kernel(R, L, S, E, pairs, planes, *refs):
    flag, q, kf, vf, ks, vs, o, do, pa, pb, cs, layt, lays = refs[:13]
    refs = list(refs[13:])
    take = lambda k: [refs.pop(0) for _ in range(k)]
    parts = take(len(planes))
    nkt_, nst_, wq, wk, wv, tok, dres, grow, dg2 = take(9)
    gtok, small_total = take(2)
    totals = take(3 + len(planes))
    kq, vaug, rhs, ds, ohq, nacc, qm, dm, held = take(9)
    dq, dk, dv, nkt, nst, ws, toks, dress = take(8)
    far, fars, gfar, gshort, ends = take(5)
    tsum, small, small_held, small_got = take(4)
    send, recv, local = take(3)
    W = 2 * E
    D = ws.shape[1]
    at = Place()
    sems = (send, recv)
    sums = []

    def summed(part, total, held, plane=None):
        i = len(sums)
        sums.append(Sum(at, part, total, take(5 + held), sems, local.at[i], Sum.COPIES * i, None, plane))

    for part, total, plane in zip(parts, totals, planes):
        summed(part, total, 1, plane)
    early = len(sums)
    mats = take(3)
    for part, total in zip(mats, totals[early:]):
        summed(part, total, 0)
    base = Sum.COPIES * len(sums)
    small_chain = small_stages(at, small, small_total, small_held, small_got, sems, base)
    long = remote(far, gfar, sems, base + 6, at.along_x())
    short = remote(fars, gshort, sems, base + 7, at.along_x())
    loads = [(w, ws.at[i]) for i, w in enumerate((wq, wk, wv))] + [(nkt_, nkt), (nst_, nst), (tok, toks), (dres, dress)]
    loads = [pltpu.make_async_copy(a, b, local.at[len(sums) + i]) for i, (a, b) in enumerate(loads)]

    step = pl.program_id(0)
    pair = lax.rem(step, pairs)
    steps = 2 * pairs
    plan = {}
    for i in range(early):
        for s in range(5):
            when = 0 if s == 0 else int(BACK_SUM[0] + BACK_SUM[1] * i + BACK_SUM[2] * (s - 1))
            plan.setdefault(when, []).insert(0, sums[i].stages[s])

    def tick(spot):
        for t in plan:
            if t < 2 * steps and t % 2 == spot:

                @pl.when(step == t // 2)
                def _(t=t):
                    for stage in plan[t]:
                        stage()

    @pl.when(step == 0)
    def _():
        at.greet()
        for load in loads:
            load.start()
        for i, (base, row) in enumerate([(0, layt[0]), (L, lays[...])]):
            kq[:SPAN, base : base + row.shape[1]] = eye_of(row, SPAN, True)
            ohq[i] = jnp.transpose(eye_of(layt[i, :, :R], SPAN, False).astype(F32)).astype(BF)
        vaug[:, W:] = (lax.broadcasted_iota(jnp.int32, (R, W), 1) < 2).astype(F32).astype(BF)
        rhs[...] = jnp.zeros_like(rhs)

    @pl.when(step == pairs)
    def _():
        for load in loads[:3]:
            load.wait()
        far[...] = (dot_nt(dk[R:L], ws[1]) + dot_nt(dv[R:L], ws[2])).astype(BF)
        long.start()
        ends[...] = dot_nt(dk[L:], ws[1]) + dot_nt(dv[L:], ws[2])
        fars[...] = ends[...].astype(BF)
        pl.when(at.x == 1)(short.start)

    nacc[...] = jnp.zeros_like(nacc)
    lane = lax.broadcasted_iota(jnp.int32, (R, W), 1)
    spot = lax.broadcasted_iota(jnp.int32, (16, R), 0)
    here = pl.ds(pl.multiple_of(pair * W, W), W)

    def attend_to(i, base, m, keys, values, p, scale, ticking):
        ch = min(CH, m)
        vaug[:m, :W] = values
        kt = flipped(keys)
        dot_, ot = jnp.transpose(do[i].astype(F32)), jnp.transpose(o[i].astype(F32))
        scaled = [(dot_[h * E : (h + 1) * E] * cs[scale, 0, h : h + 1]).astype(BF) for h in range(2)]
        don = flipped(jnp.concatenate(scaled, axis=0))
        qq = q[i]
        zero = jnp.zeros((R, W), BF)
        for h in range(2):
            mine = (lane < E) if h == 0 else (lane >= E)
            qm[h * R : (h + 1) * R] = jnp.where(mine, qq, zero)
            dm[h * R : (h + 1) * R] = jnp.where(mine, don, zero)
        dqs = []
        for h in range(2):
            if ticking:
                tick(h)
            rhs[h * E : (h + 1) * E] = scaled[h]
            rhs[(1 - h) * E : (2 - h) * E] = jnp.zeros((E, R), BF)
            delta = jnp.sum(scaled[h].astype(F32) * ot[h * E : (h + 1) * E], axis=0, keepdims=True)
            hi = delta.astype(BF).astype(F32)
            rhs[W : W + 16] = jnp.where(spot == 0, -hi, jnp.where(spot == 1, hi - delta, 0.0)).astype(BF)
            for c in range(0, m, ch):
                g = dot(vaug[c : c + ch], rhs[...])
                ds[c : c + ch, h * R : (h + 1) * R] = (p[h, c : c + ch].astype(F32) * g).astype(BF)
            kq[SPAN:, base : base + m] = kt[h * E : (h + 1) * E]
            both = dot(kq[:, base : base + m], ds[:m, h * R : (h + 1) * R])
            dqs.append(both[SPAN:] * 0.125)
            nacc[h] += dot(both[:SPAN].astype(BF), ohq[i])
        for c in range(0, m, ch):
            dk[base + c : base + c + ch, here] = dot(ds[c : c + ch], qm[...]).astype(BF)
            both = dot(p[0, c : c + ch], dm[:R]) + dot(p[1, c : c + ch], dm[R:])
            dv[base + c : base + c + ch, here] = both.astype(BF)
        return jnp.concatenate(dqs, axis=0)

    def diagonals(h):
        wide = jnp.concatenate([nacc[h], jnp.zeros((SPAN, SPAN), F32)], axis=1)
        return jnp.sum(pltpu.roll(wide, 0, 1, stride=1, stride_axis=0), axis=0, keepdims=True)

    @pl.when(step < pairs)
    def _():
        m = L - R
        held[pair] = attend_to(0, R, m, kf[R:], vf[R:], pb.at[0, :, pl.ds(0, m)], 1, True)
        dq[1, :, here] = flipped(attend_to(1, L, S, ks[...], vs[...], pb.at[0, :, pl.ds(m, S)], 2, False))
        for h in range(2):
            tsum[2 * pair + h] = diagonals(h)

    @pl.when(step >= pairs)
    def _():
        dq[0, :, here] = flipped(held[pair] + attend_to(0, 0, R, kf[:R], vf[:R], pa.at[0], 0, True))
        for h in range(2):
            tsum[2 * pair + h] = tsum[2 * pair + h] + diagonals(h)

    @pl.when(step == steps - 1)
    def _():
        rest = [stage for t in sorted(plan) if t >= 2 * steps for stage in plan[t]]

        def some(count):
            for _ in range(min(count, len(rest))):
                rest.pop(0)()

        for load in loads[3:]:
            load.wait()
        later = sums[early:]
        into_slabs(dot(nkt[...], dv[...]), mats[2])
        later[2].one()
        some(2)
        into_slabs(dot(nkt[...], dk[...]), mats[1])
        later[1].one()
        some(2)
        into_slabs(dot(nkt[:, :R], dq[0]) + dot(nst[...], dq[1]), mats[0])
        later[0].one()
        some(100)
        later[2].two()
        toks[0], toks[1] = swapped(flag, toks[0], toks[1])
        own = [dot_nt(dq[0], ws[0]) + dot_nt(dk[:R], ws[1]) + dot_nt(dv[:R], ws[2]), dot_nt(dq[1], ws[0])]
        later[1].two()
        later[2].three()
        long.wait()
        pl.when(at.x == 1)(short.wait_send)
        pl.when(at.x == 0)(short.wait_recv)
        gain = grow[0:1]
        keys = jnp.where(at.x == 0, ends[...] + gshort[...].astype(F32), 0.0)
        total = jnp.zeros((1, D), F32)
        for i in range(2):
            d = own[i] + (gfar[...].astype(F32) if i == 0 else jnp.concatenate([keys, jnp.zeros((R - S, D), F32)], axis=0))
            x = toks[i].astype(F32)
            back = norm_rows(x)
            a = gain * d
            total = total + jnp.sum(d * x * back, axis=0, keepdims=True)
            part = back * a - x * (back * back * back) * jnp.mean(a * x, axis=1, keepdims=True)
            toks[i] = (dress[i * R : (i + 1) * R] + part).astype(BF)
        toks[0], toks[1] = swapped(flag, toks[0], toks[1])
        finish = pltpu.make_async_copy(toks, gtok, local.at[len(sums) + len(loads)])
        finish.start()
        small[...] = jnp.zeros_like(small)
        lines = D // 128
        for i in range(lines):
            small[i : i + 1] = total[:, 128 * i : 128 * (i + 1)]
            small[lines + i : lines + i + 1] = dg2[:, 128 * i : 128 * (i + 1)]
        for h in range(2 * pairs):
            for i in range(4):
                spots = 2 * lines + 4 * h + i
                small[spots : spots + 1] = tsum[h, :, 128 * i : 128 * (i + 1)]
        small_chain[0]()
        later[0].two()
        later[1].three()
        small_chain[1]()
        later[2].four()
        later[0].three()
        small_chain[2]()
        later[1].four()
        small_chain[3]()
        later[0].four()
        for s in later[::-1]:
            s.five()
        small_chain[4]()
        finish.wait()


def backward_call(flag, q, kf, vf, ks, vs, o, do, pa, pb, cs, layt, lays, parts, planes, nkt, nst, wq, wk, wv, tok, dres, grow, dg2):
    n, R, D = q.shape
    L, S = kf.shape[0], ks.shape[0]
    pairs = pa.shape[0]
    E = D // (2 * pairs)
    W = 2 * E
    KT = L + S
    whole = lambda a: pl.BlockSpec(a.shape, lambda j: (0,) * len(a.shape))
    anywhere = pl.BlockSpec(memory_space=pl.ANY)
    early = lambda j: jnp.minimum(j, pairs - 1)
    late = lambda j: jnp.maximum(j - pairs, 0)
    rows = pl.BlockSpec((n, R, W), lambda j: (0, 0, lax.rem(j, pairs)))
    keys = lambda a: pl.BlockSpec((a.shape[0], W), lambda j: (0, lax.rem(j, pairs)))
    shares = [p_.shape[4:] for p_ in parts] + [(D // 32, D)] * 3
    lines = -(-(2 * D // 128 + 8 * pairs) // 8) * 8
    outs = [jax.ShapeDtypeStruct((n, R, D), BF), jax.ShapeDtypeStruct((lines, 128), F32)]
    outs += [jax.ShapeDtypeStruct(s, F32) for s in shares]
    vmem = lambda *s: pltpu.VMEM(s, BF)
    wide = lambda *s: pltpu.VMEM(s, F32)
    scratch = [vmem(SPAN + E, KT), vmem(R, 2 * W), vmem(2 * W, R), vmem(R, 2 * R), vmem(n, R, SPAN)]
    scratch += [wide(2, SPAN, SPAN), vmem(2 * R, W), vmem(2 * R, W), wide(pairs, W, R)]
    scratch += [vmem(n, R, D), vmem(KT, D), vmem(KT, D), vmem(D, KT), vmem(D, R)]
    scratch += [vmem(3, D, D), vmem(n, R, D), wide(n * R, D)]
    scratch += [vmem(R, D), vmem(S, D), vmem(R, D), vmem(S, D), wide(S, D)]
    scratch += [wide(2 * pairs, 1, 2 * SPAN), wide(lines, 128), wide(4, lines, 128), wide(6, lines, 128)]
    chunks = [(p_.shape[0],) + p_.shape[4:] for p_ in parts]
    copies = Sum.COPIES * (len(chunks) + 3) + 8
    scratch += [pltpu.SemaphoreType.DMA((copies,)), pltpu.SemaphoreType.DMA((copies,)), pltpu.SemaphoreType.DMA((len(chunks) + 12,))]
    scratch += sum([Sum.scratch(*s, 1) for s in chunks], [])
    scratch += [vmem(4, 2, 2, 2, D // 32, D)] * 3
    scratch += sum([Sum.scratch(4, *s, 0) for s in shares[len(parts):]], [])
    return pl.pallas_call(
        functools.partial(backward_kernel, R, L, S, E, pairs, planes),
        grid=(2 * pairs,),
        in_specs=[whole(flag), rows, keys(kf), keys(vf), keys(ks), keys(vs), rows, rows]
        + [pl.BlockSpec((1, 2, R, R), lambda j: (late(j), 0, 0, 0)), pl.BlockSpec((1, 2, KT - R, R), lambda j: (early(j), 0, 0, 0))]
        + [pl.BlockSpec((3, 1, 2, R), lambda j: (0, lax.rem(j, pairs), 0, 0)), whole(layt), whole(lays)]
        + [anywhere] * (len(parts) + 7)
        + [whole(grow), whole(dg2)],
        out_specs=[anywhere] + [whole(s) for s in outs[1:]],
        out_shape=outs,
        scratch_shapes=scratch,
        compiler_params=pltpu.CompilerParams(
            vmem_limit_bytes=60 * 2**20, dimension_semantics=("arbitrary",), collective_id=1, has_side_effects=True
        ),
        name="backward",
    )(flag, q, kf, vf, ks, vs, o, do, pa, pb, cs, layt, lays, *parts, nkt, nst, wq, wk, wv, tok, dres, grow, dg2)


EPSILON = 1e-06
THRESHOLDS = (12, 16, 23, 32, 46, 64, 91)
BOTH = ("dp", "blk")


def bucket_np(relative):
    magnitude = np.abs(relative)
    larger = 8 + sum((magnitude >= limit).astype(np.int64) for limit in THRESHOLDS)
    return np.where(magnitude < 8, magnitude, larger) + 16 * (relative > 0)


def bucket_rows(distance, buckets):
    return (bucket_np(distance)[:, None] == np.arange(buckets)[None, :]).astype(np.float32)


def norm_parts(x, gain):
    back = lax.rsqrt(jnp.mean(x * x, axis=-1, keepdims=True) + EPSILON)
    return (x * back * gain).astype(BF), back


def norm_back(d, x, back, gain):
    a = gain * d
    grad_gain = jnp.sum(d * x * back, axis=0)
    return back * a - x * back**3 * jnp.mean(a * x, axis=-1, keepdims=True), grad_gain


def mm(a, b, dims):
    return lax.dot_general(a, b, (dims, ((), ())), preferred_element_type=F32)


def gather_weights(gain_one, wq, wk, wv, wo, gain_two, wi, wt):
    full = lambda a: lax.all_gather(a, BOTH, axis=0, tiled=True)
    packed = full(jnp.concatenate([wq, wk, wv, wo, wi], axis=1))
    width = wq.shape[1]
    gains = full(jnp.stack([gain_one, gain_two], axis=1))
    return packed[:, : 3 * width], packed[:, 3 * width : 4 * width], packed[:, 4 * width :], full(wt), gains[:, 0], gains[:, 1]


def scatter_sums(dqkv, dwo, dwi, dwt, dg1, dg2):
    take = lambda a: lax.psum_scatter(a, BOTH, scatter_dimension=0, tiled=True)
    width = dwo.shape[1]
    packed = take(jnp.concatenate([dqkv, dwo, dwi], axis=1).astype(BF)).astype(F32)
    gains = take(jnp.stack([dg1, dg2], axis=1))
    parts = [packed[:, i * width : (i + 1) * width] for i in range(4)]
    return parts, packed[:, 4 * width :], take(dwt.astype(BF)).astype(F32), gains[:, 0], gains[:, 1]


def on_any_device(tokens, layout, lengths, gain_one, wq, wk, wv, wo, gain_two, wi, wt, table, grad_out):
    n, R, D = tokens.shape
    H = table.shape[1]
    G = lax.axis_size("blk")
    me = lax.axis_index("blk")
    L = layout.shape[1]
    S = L // 8
    order = jnp.argsort(-lengths, stable=True)
    place = jnp.argsort(order)
    tok = tokens[order]
    gout = grad_out[order]
    lay = layout[order]
    lens = lengths[order]

    def from_step(x, s):
        return lax.ppermute(x, "blk", [(i, (i - s) % G) for i in range(G)])

    pieces = [tok[:-1]] + [from_step(tok[:-1], s) for s in range(1, G)]
    xf = jnp.concatenate(pieces, axis=1)
    first = tok[-1, :S]
    xs = jnp.where(me == 0, first, sum(lax.ppermute(first, "blk", [(0, i)]) for i in range(1, G)))
    lay_turned = jnp.roll(lay, -me * R, axis=1)
    layq = lay_turned[:, None, :R]
    layf = lay_turned[:-1, None, :]
    lays = lay[-1:, :S]
    spots = (jnp.arange(L) + me * R) % L
    mask = jnp.where(spots[None, :, None] < lens[:-1, None, None], 0.0, -1e30).astype(F32)

    wqkv, wo_all, wi_all, wt_all, g1, g2 = gather_weights(gain_one, wq, wk, wv, wo, gain_two, wi, wt)
    g1 = g1.astype(F32)
    g2 = g2.astype(F32)
    hidden = tok.reshape(n * R, D).astype(F32)
    normed, r1 = norm_parts(hidden, g1)
    xkeys = jnp.concatenate([xf.reshape((n - 1) * L, D), xs], axis=0)
    nkeys, _ = norm_parts(xkeys.astype(F32), g1)
    q = (mm(normed, wqkv[:, :D], ((1,), (0,))).astype(BF) * jnp.asarray(0.125, BF)).reshape(n, R, D)
    k = mm(nkeys, wqkv[:, D : 2 * D], ((1,), (0,))).astype(BF)
    v = mm(nkeys, wqkv[:, 2 * D :], ((1,), (0,))).astype(BF)
    cut = (n - 1) * L
    kf, ks = k[:cut].reshape(n - 1, L, D), k[cut:]
    vf, vs = v[:cut].reshape(n - 1, L, D), v[cut:]
    lane = np.arange(2 * SPAN)
    turned = np.where(lane >= SPAN, lane - 2 * SPAN, lane)
    urow = mm(table, bucket_rows(-turned, table.shape[0]).astype(BF), ((0,), (1,))).reshape(H // 2, 2, 2 * SPAN)
    o, p, l = attend_call(q, kf, vf, ks, vs, layq, layf, lays, mask, urow)

    attended = o.reshape(n * R, D)
    resid = hidden + mm(attended, wo_all, ((1,), (0,)))
    normed_two, r2 = norm_parts(resid, g2)
    pre = mm(normed_two, wi_all, ((1,), (0,)))
    act, act_back = jax.vjp(lambda x: jax.nn.gelu(x, approximate=False), pre)
    act = act.astype(BF)
    mixed = (resid + mm(act, wt_all, ((1,), (0,)))).astype(BF)
    up = gout.reshape(n * R, D)
    dwt = mm(act, up, ((0,), (0,)))
    (dpre,) = act_back(mm(up, wt_all, ((1,), (1,))))
    dpre = dpre.astype(BF)
    dwi = mm(normed_two, dpre, ((0,), (0,)))
    dn2 = mm(dpre, wi_all, ((1,), (1,)))
    dresid, dg2 = norm_back(dn2, resid, r2, g2)
    dresid = dresid + up.astype(F32)
    low = dresid.astype(BF)
    dwo = mm(attended, low, ((0,), (0,)))
    datt = mm(low, wo_all, ((1,), (1,))).astype(BF).reshape(n, R, D)

    dq, dkf, dvf, dks, dvs, t = attend_back_call(q, kf, vf, ks, vs, layq, layf, lays, o, datt, p, l)
    dtable = jnp.einsum(
        "hj,jb->bh", t.reshape(H, 2 * SPAN), bucket_rows(SPAN - 1 - lane, table.shape[0]), precision=lax.Precision.HIGHEST
    )
    dq = dq.reshape(n * R, D)
    dk = jnp.concatenate([dkf.reshape(cut, D), dks], axis=0)
    dv = jnp.concatenate([dvf.reshape(cut, D), dvs], axis=0)
    dnk = mm(dk, wqkv[:, D : 2 * D], ((1,), (1,))) + mm(dv, wqkv[:, 2 * D :], ((1,), (1,)))
    dnf = dnk[:cut].reshape(n - 1, L, D)
    dns = dnk[cut:].astype(BF)
    far = sum(
        lax.ppermute(dnf[:, s * R : (s + 1) * R].astype(BF), "blk", [(i, (i + s) % G) for i in range(G)]).astype(F32)
        for s in range(1, G)
    )
    near = jnp.where(
        me == 0, dnk[cut:] + sum(lax.ppermute(dns, "blk", [(i, 0)]).astype(F32) for i in range(1, G)), 0.0
    )
    extra = jnp.concatenate([dnf[:, :R] + far, jnp.pad(near, ((0, R - S), (0, 0)))[None]], axis=0).reshape(n * R, D)
    dn1 = mm(dq, wqkv[:, :D], ((1,), (1,))) + extra
    dwq = mm(normed, dq, ((0,), (0,)))
    dwk = mm(nkeys, dk, ((0,), (0,)))
    dwv = mm(nkeys, dv, ((0,), (0,)))
    dx, dg1 = norm_back(dn1, hidden, r1, g1)
    gtok = (dresid + dx).astype(BF)
    parts, gwi, gwt, gg1, gg2 = scatter_sums(jnp.concatenate([dwq, dwk, dwv], axis=1), dwo, dwi, dwt, dg1, dg2)
    dtable = lax.psum(dtable, BOTH)
    return (
        mixed.reshape(n, R, D)[place],
        gtok.reshape(n, R, D)[place],
        gg1,
        parts[0],
        parts[1],
        parts[2],
        parts[3],
        gg2,
        gwi,
        gwt,
        dtable,
    )


def on_device(tokens, layout, lengths, gain_one, wq, wk, wv, wo, gain_two, wi, wt, table, grad_out):
    n, R, D = tokens.shape
    H = table.shape[1]
    G = lax.axis_size("blk")
    me = lax.axis_index("blk")
    L = layout.shape[1]
    S = L // 8
    swap = lengths[0] < lengths[1]
    flag = jnp.broadcast_to(swap.astype(jnp.int32), (8, 128))
    lay = jnp.where(swap, layout[::-1], layout)
    layt = jnp.where(me == 0, lay, jnp.roll(lay, R, axis=1))[:, None, :]
    lays = lay[1:, :S]
    lane = np.arange(2 * SPAN)
    turned = np.where(lane >= SPAN, lane - 2 * SPAN, lane)
    urow = mm(table, bucket_rows(-turned, table.shape[0]).astype(BF), ((0,), (1,))).reshape(H // 2, 2, 2 * SPAN)
    gains = jnp.pad(jnp.stack([gain_one, gain_two], axis=1), ((0, 0), (0, 126)))
    o, pa, pb, cs, grow, q, kf, vf, ks, vs, nkt, nst, *wholes = forward_call(
        flag, tokens, layt, lays, urow, [gains, wq, wk, wv, wo, wi, wt], S
    )
    flat = lambda a: a.reshape(-1, a.shape[-1])
    wq_all, wk_all, wv_all, wo_all, wi_all, wt_all = [flat(a) for a in wholes]
    rows = lambda a: a.reshape(n * R, D)
    mixed, dresid, datt, dwo, *handed = feed_forward_call(
        flag, rows(o), rows(tokens), rows(grad_out), wo_all, grow, wi_all, wt_all
    )
    count = 2 * (4 - FF_SUMS)
    dg2, done = handed[count], handed[count + 1 :]
    planes = sum([(None, j) for j in range(FF_SUMS, 4)], ()) + (None,)
    gtok, small, *sums = backward_call(
        flag, q, kf, vf, ks, vs, o, datt.reshape(n, R, D), pa, pb, cs, layt, lays,
        handed[:count] + [dwo.reshape(4, 2, 2, 2, -1, D)], planes,
        nkt, nst, wq_all, wk_all, wv_all, tokens, dresid, grow, dg2,
    )
    gwo, gwq, gwk, gwv = sums[count:]
    gwi = jnp.concatenate(done[:FF_SUMS] + sums[0:count:2], axis=1)
    gwt = done[FF_SUMS]
    for j in range(FF_SUMS, 4):
        gwt = jnp.where(lax.axis_index("dp") // 4 == j, sums[2 * (j - FF_SUMS) + 1], gwt)
    small = small.reshape(-1)
    mine = (lax.axis_index("dp") * G + me) * (D // 32)
    gg1, gg2 = [lax.dynamic_slice_in_dim(small, mine + i * D, D // 32) for i in range(2)]
    t = small[2 * D : 2 * D + H * 2 * SPAN].reshape(H, 2 * SPAN)
    dtable = jnp.einsum(
        "hj,jb->bh", t, bucket_rows(SPAN - 1 - lane, table.shape[0]), precision=lax.Precision.HIGHEST
    )
    return mixed.reshape(n, R, D), gtok, gg1, gwq, gwk, gwv, gwo, gg2, gwi, gwt, dtable


def solution(mesh):
    rows = P(BOTH, None)
    items = P("dp", "blk", None)
    known = dict(mesh.shape) == {"dp": 16, "blk": 2}

    def body(tokens, *rest):
        return (on_device if known and tokens.shape[0] == 2 else on_any_device)(tokens, *rest)

    return jax.shard_map(
        body,
        mesh=mesh,
        in_specs=(items, P("dp", None), P("dp"), P(BOTH), rows, rows, rows, rows, P(BOTH), rows, rows, P(), items),
        out_specs=(items, items, P(BOTH), rows, rows, rows, rows, P(BOTH), rows, rows, P()),
        check_vma=False,
    )
```

time: 411 us -> 294 us (0.72); the launches traced: 406 us -> 293 us
  matrix products: 121 us -> 1.89 us
  Pallas kernels: 227 us -> 270 us
  local copies, waits for them, and re-layouts: 35.7 us -> 15 us
  other arithmetic: 17.4 us -> 3.09 us
    dot_general x19 -> x1, matrix products: 120 us -> 1.03 us  [mm(): return lax.dot_general(a, b, (dims, ((), ())), preferred_element_type=F32)]
    pallas_call x4 -> x3, Pallas kernels: 227 us -> 270 us  [the longest x1 110 us: forward_call(): pl.pallas_call(functools.partial(forward_kernel, R, L, S, E, pairs), grid...]
    gather x6 -> x0, local copies, waits for them, and re-layouts: 9.79 us -> none  [the longest x1 3.39 us: on_device(): gtok.reshape(n, R, D)[place]]
    convert_element_type x4 -> x0, other arithmetic: 5.81 us -> none  [the longest x1 5.31 us: on_device(): gtok = (dresid + dx).astype(BF)]
    unnamed x122 -> x30, local copies, waits for them, and re-layouts: 11 us -> 5.7 us
  transfers between devices with their start and end apart: 2 -> 0, of which waited for: 0 -> 0; matrix products, arithmetic and copies ran while one was open for 5% -> 0% of each run, Pallas kernels for 0% -> 0%
where the time goes in v2:
time: 294 us; the launch traced here: 293 us
  Pallas kernels  270 us (92%)
  local copies, waits for them, and re-layouts  15 us (5%)
  other arithmetic  3.09 us (1%)
    pallas_call x1, Pallas kernels, forward_call(): pl.pallas_call(functools.partial(forward_kernel, R, L, S, E, pairs), grid...  110 us
    pallas_call x1, Pallas kernels, backward_call(): pl.pallas_call(functools.partial(backward_kernel, R, L, S, E, pairs, plan...  97.8 us
    pallas_call x1, Pallas kernels, feed_forward_call(): pl.pallas_call(functools.partial(feed_forward, R, blocks), grid=(blocks,)...  62.6 us

profile of v2, /device:TPU:0, one launch (start us, length us, event | category | flops | bytes accessed | tf_op | source)
XLA Modules:
  0.0 292.8 jit_solution(12310798538116928200)
XLA Ops:
  0.6 0.0 copy-start
  0.7 1.3 fusion.3
  3.3 2.8 rev.3
  6.2 0.6 copy.31.refs_2_.refs_11_
  6.8 0.5 slice.29.refs_3_.refs_12_
  7.3 0.6 broadcast_in_dim.6.refs_0_
  7.9 0.0 copy-done
  7.9 1.0 convolution_bitcast_fusion
  8.9 0.6 reshape.70.refs_4_
  9.6 0.7 pad_maximum_fusion.1
  10.2 0.1 copy.30
  10.3 0.6 pad.4.refs_5_
  10.9 110.0 %forward.1 = (bf16[2,512,768]{2,1,0:T(8,128)(2,1)}, bf16[6,2,512,512]{3,2,1,0:T(8,128)(2,1)}, bf16[6,2,640,512]{3,2,1,0:T(8,128)(2,1)}, f32[3,6,2,512]{3,2,1,0:T...) custom-call(s32[8,128]{1,0:T(8,128)} %broadcast_in_dim.6.refs_0_, ...), custom_call_target="tpu_custom_call" | custom-call | tf_op jit(solution)/shard_map/forward/pallas_call | solution.py:851
  120.9 62.6 %feed_forward.1 = (bf16[1024,768]{1,0:T(8,128)(2,1)}, f32[1024,768]{1,0:T(8,128)}, bf16[1024,768]{1,0:T(8,128)(2,1)}, bf16[768,768]{1,0:T(8,128)(2,1)}, bf16[4,2...) custom-call(s32[8,128]{1,0:T(8,128)} %broadcast_in_dim.6.refs_0_, ...), custom_call_target="tpu_custom_call" | custom-call | tf_op jit(solution)/shard_map/feed_forward/pallas_call | solution.py:581
  183.6 0.0 copy-start.3
  183.6 0.0 copy-start.5
  183.6 0.0 copy-start.6
  183.6 0.0 copy-start.7
  183.6 0.0 copy-start.4
  183.6 97.8 %backward.1 = (bf16[2,512,768]{2,1,0:T(8,128)(2,1)}, f32[64,128]{1,0:T(8,128)}, f32[24,768]{1,0:T(8,128)}, f32[96,768]{1,0:T(8,128)}, f32[24,768]{1,0:T(8,128)},...) custom-call(s32[8,128]{1,0:T(8,128)} %broadcast_in_dim.6.refs_0_, ...), custom_call_target="tpu_custom_call" | custom-call | tf_op jit(solution)/shard_map/backward/pallas_call | solution.py:1221
  281.5 0.0 copy-start.1
  281.5 0.0 copy-done.3
  281.5 0.8 broadcast_select_fusion
  282.3 0.0 copy-done.5
  282.3 0.0 copy-done.6
  282.3 0.0 copy-done.7
  282.3 1.6 pad_maximum_fusion
  283.9 0.8 slice.26
  284.7 0.0 copy-done.4
  284.7 0.9 fusion.4
  285.6 1.4 fusion.1
  286.9 0.0 copy-done.1
  286.9 0.0 copy-start.2
  286.9 1.1 copy.39
  288.1 0.8 copy-done.2
  288.9 0.0 copy-start.11
  288.9 0.0 copy-start.10
  288.9 0.0 copy-start.9
  288.9 0.0 copy-start.8
  288.9 1.1 copy.40
  290.1 0.0 copy-done.11
  290.1 0.6 copy.41
  290.7 0.0 copy-done.10
  290.7 0.6 copy.42
  291.3 0.0 copy-done.9
  291.3 0.6 copy.43
  292.0 0.0 copy-done.8
  292.0 0.6 copy.44
  (4 shorter events, 0.0 us)
Async XLA Ops:
  0.6 7.2 %copy-start = (bf16[32,12]{0,1:T(8,128)(2,1)S(1)}, bf16[32,12]{0,1:T(8,128)(2,1)}, u32[]{:S(2)}) copy-start(bf16[32,12]{0,1:T(8,128)(2,1)} %param.26) | copy-start | bytes 2308
  183.6 97.9 %copy-start.3 = (f32[96,768]{1,0:T(8,128)S(1)}, f32[96,768]{1,0:T(8,128)}, u32[]{:S(2)}) copy-start(f32[96,768]{1,0:T(8,128)} %get-tuple-element.84) | copy-start | bytes 884740
  183.6 98.7 %copy-start.5 = (f32[24,768]{1,0:T(8,128)S(1)}, f32[24,768]{1,0:T(8,128)}, u32[]{:S(2)}) copy-start(f32[24,768]{1,0:T(8,128)} %get-tuple-element.79) | copy-start | bytes 221188
  183.6 98.7 %copy-start.6 = (f32[24,768]{1,0:T(8,128)S(1)}, f32[24,768]{1,0:T(8,128)}, u32[]{:S(2)}) copy-start(f32[24,768]{1,0:T(8,128)} %get-tuple-element.80) | copy-start | bytes 221188
  183.6 98.7 %copy-start.7 = (f32[24,768]{1,0:T(8,128)S(1)}, f32[24,768]{1,0:T(8,128)}, u32[]{:S(2)}) copy-start(f32[24,768]{1,0:T(8,128)} %get-tuple-element.81) | copy-start | bytes 221188
  183.6 101.1 %copy-start.4 = (f32[512,32]{1,0:T(8,128)S(1)}, f32[512,32]{1,0:T(8,128)}, u32[]{:S(2)}) copy-start(f32[512,32]{1,0:T(8,128)} %constant.42.clone) | copy-start | bytes 196612
  281.5 5.4 %copy-start.1 = (bf16[1024,768]{1,0:T(8,128)(2,1)S(1)}, bf16[1024,768]{1,0:T(8,128)(2,1)}, u32[]{:S(2)}) copy-start(bf16[1024,768]{1,0:T(8,128)(2,1)} %get-tuple-element.53) | copy-start | bytes 4718596
  286.9 2.0 copy-start.2
  288.9 1.2 copy-start.11
  288.9 1.8 copy-start.10
  288.9 2.4 copy-start.9
  288.9 3.1 %copy-start.8 = (f32[24,768]{1,0:T(8,128)S(1)}, f32[24,768]{1,0:T(8,128)}, u32[]{:S(2)}) copy-start(f32[24,768]{1,0:T(8,128)} %get-tuple-element.108) | copy-start | bytes 221188

commit v3 on v2

--- a/solution.py
+++ b/solution.py
@@ -169,17 +169,19 @@
 
 
 EPSILON = 1e-06
-FORWARD_PIECES = 2
-FORWARD_WAYS = (0,) * 9
+FORWARD_PIECES = 3
+FORWARD_WAYS = (0,) * 11
 FORWARD_AT = (
     (-9, -8, -7, -6, -5),
     (-8, -7, -6, -5, -4),
     (-7, -6, -5, -4, -3),
     (-6, -5, -4, -3, -2),
-    (-5, -4, -3, -2, 6),
-    (-4, -3, -2, 6, 12),
-    (-3, -2, 6, 12, 18),
-    (-2, 6, 12, 18, 24),
+    (-5, -4, -3, -2, 4),
+    (-4, -3, -2, 4, 8),
+    (-3, -2, 4, 8, 12),
+    (-2, 4, 8, 12, 16),
+    (4, 8, 12, 16, 20),
+    (8, 12, 16, 20, 24),
 )
 FF_SUMS = 3
 FF_SUM = (0, 2)
@@ -581,7 +583,7 @@
     return pl.pallas_call(
         functools.partial(feed_forward, R, blocks),
         grid=(blocks,),
-        in_specs=[whole(flag.shape)] + [anywhere] * 4 + [whole(grow.shape)] + [anywhere] * 2,
+        in_specs=[pl.BlockSpec(memory_space=pltpu.SMEM)] + [anywhere] * 4 + [whole(grow.shape)] + [anywhere] * 2,
         out_specs=[anywhere] * len(outs) + [whole(s) for s, _ in small],
         out_shape=[jax.ShapeDtypeStruct(*s) for s in outs + small],
         scratch_shapes=scratch,
@@ -631,20 +633,26 @@
     ]
 
 
-def swapped(flag, a, b):
-    turn = flag[0:1, 0:1] > 0
+def swapped(lengths, a, b):
+    turn = lengths[0] < lengths[1]
     return jnp.where(turn, b, a), jnp.where(turn, a, b)
 
 
+def coordinates(at, lengths, layout, R, S):
+    long, short = swapped(lengths, layout[0:1], layout[1:2])
+    keys = jnp.where(at.x == 0, long, jnp.concatenate([long[:, R:], long[:, :R]], axis=1))
+    return keys, short[:, :S], keys[:, :R], jnp.where(at.x == 0, short[:, :R], short[:, R:])
+
+
 def forward_kernel(R, L, S, E, pairs, *refs):
-    flag, tokens, layt, lays, u = refs[:5]
+    flag, tokens, layout, table, basis = refs[:5]
     shards = refs[5:12]
     refs = list(refs[12:])
     take = lambda k: [refs.pop(0) for _ in range(k)]
     o, pa, pb, cs, grow = take(5)
     kept = take(7)
     wholes = take(6)
-    kcat, qcat, vt, s_ref, ohq, xfar, xshort, flat, normed, tok, held, stats = take(12)
+    kcat, qcat, vt, s_ref, ohq, xfar, xshort, flat, normed, tok, held, stats, u = take(13)
     q, kf, vf, ks, vs, nkt, nst = inner = take(7)
     slabs = take(4)
     send, recv, local = take(3)
@@ -686,9 +694,13 @@
         turn(-9)
         tok[0], tok[1] = swapped(flag, tokens[0], tokens[1])
         send_tokens()
-        for i, (base, row) in enumerate([(0, layt[0]), (L, lays[...])]):
+        long_keys, short_keys, *queries = coordinates(at, flag, layout, R, S)
+        for i, (base, row) in enumerate([(0, long_keys), (L, short_keys)]):
             kcat[base : base + row.shape[1], W:] = jnp.transpose(eye_of(row, SPAN, False).astype(F32)).astype(BF)
-            ohq[i] = eye_of(layt[i, :, :R], SPAN, False)
+            ohq[i] = eye_of(queries[i], SPAN, False)
+        rows = lax.dot_general(table[...], basis[...], (((0,), (0,)), ((), ())), preferred_element_type=F32)
+        for h in range(2 * pairs):
+            u[h] = rows[h : h + 1]
         vt[:, E:] = jnp.ones((2, vt.shape[1] - E, vt.shape[2]), BF)
         for t in range(-8, -4):
             turn(t)
@@ -765,7 +777,7 @@
         for h in range(2):
             if ticking:
                 tick(h)
-            toep = pltpu.roll(jnp.broadcast_to(u[0, h : h + 1], (SPAN, 2 * SPAN)), 0, 1, stride=1, stride_axis=0)
+            toep = pltpu.roll(jnp.broadcast_to(u[2 * pair + h], (SPAN, 2 * SPAN)), 0, 1, stride=1, stride_axis=0)
             qcat[h * E : (h + 1) * E] = qt[h * E : (h + 1) * E]
             qcat[(1 - h) * E : (2 - h) * E] = jnp.zeros((E, R), BF)
             qcat[W:] = dot(toep[:, :SPAN].astype(BF), ohq[i]).astype(BF)
@@ -823,10 +835,10 @@
     return [pl.ds(i * width // FORWARD_PIECES, width // FORWARD_PIECES) for i in range(FORWARD_PIECES)]
 
 
-def forward_call(flag, tokens, layt, lays, u, shards, S):
+def forward_call(flag, tokens, layout, table, basis, shards, S):
     n, R, D = tokens.shape
-    L = layt.shape[2]
-    pairs = u.shape[0]
+    L = layout.shape[1]
+    pairs = table.shape[1] // 2
     E = D // (2 * pairs)
     W = 2 * E
     KT = L + S
@@ -851,13 +863,13 @@
     return pl.pallas_call(
         functools.partial(forward_kernel, R, L, S, E, pairs),
         grid=(2 * pairs,),
-        in_specs=[whole(flag.shape), whole(tokens.shape), whole(layt.shape), whole(lays.shape)]
-        + [pl.BlockSpec((1, 2, 2 * SPAN), lambda j: (lax.rem(j, pairs), 0, 0))]
+        in_specs=[pl.BlockSpec(memory_space=pltpu.SMEM)]
+        + [whole(a.shape) for a in (tokens, layout, table, basis)]
         + [anywhere] * 7,
         out_specs=[b[2] for b in blocked] + [anywhere] * (len(kept) + len(filled)),
         out_shape=[jax.ShapeDtypeStruct(*b[:2]) for b in blocked] + [jax.ShapeDtypeStruct(s, BF) for s in kept + filled],
         scratch_shapes=[vmem(KT, W + SPAN), vmem(W + SPAN, R), vmem(2, E + 16, R), wide(R, R), vmem(n, SPAN, R)]
-        + [vmem(R, D), vmem(S, D), vmem(2, D, D), vmem(n, R, D), vmem(n, R, D), wide(pairs, W, R), wide(pairs, 8, R)]
+        + [vmem(R, D), vmem(S, D), vmem(2, D, D), vmem(n, R, D), vmem(n, R, D), wide(pairs, W, R), wide(pairs, 8, R), wide(2 * pairs, 1, 2 * SPAN)]
         + [vmem(*s) for s in kept]
         + [vmem(*s) for s in gathered[:4]]
         + [pltpu.SemaphoreType.DMA((copies,))] * 2
@@ -866,7 +878,7 @@
             vmem_limit_bytes=60 * 2**20, dimension_semantics=("arbitrary",), collective_id=0, has_side_effects=True
         ),
         name="forward",
-    )(flag, tokens, layt, lays, u, *shards)
+    )(flag, tokens, layout, table, basis, *shards)
 
 
 class Sum:
@@ -988,8 +1000,8 @@
 
 
 def backward_kernel(R, L, S, E, pairs, planes, *refs):
-    flag, q, kf, vf, ks, vs, o, do, pa, pb, cs, layt, lays = refs[:13]
-    refs = list(refs[13:])
+    flag, q, kf, vf, ks, vs, o, do, pa, pb, cs, layout = refs[:12]
+    refs = list(refs[12:])
     take = lambda k: [refs.pop(0) for _ in range(k)]
     parts = take(len(planes))
     nkt_, nst_, wq, wk, wv, tok, dres, grow, dg2 = take(9)
@@ -1046,9 +1058,10 @@
         at.greet()
         for load in loads:
             load.start()
-        for i, (base, row) in enumerate([(0, layt[0]), (L, lays[...])]):
+        long_keys, short_keys, *queries = coordinates(at, flag, layout, R, S)
+        for i, (base, row) in enumerate([(0, long_keys), (L, short_keys)]):
             kq[:SPAN, base : base + row.shape[1]] = eye_of(row, SPAN, True)
-            ohq[i] = jnp.transpose(eye_of(layt[i, :, :R], SPAN, False).astype(F32)).astype(BF)
+            ohq[i] = jnp.transpose(eye_of(queries[i], SPAN, False).astype(F32)).astype(BF)
         vaug[:, W:] = (lax.broadcasted_iota(jnp.int32, (R, W), 1) < 2).astype(F32).astype(BF)
         rhs[...] = jnp.zeros_like(rhs)
 
@@ -1187,7 +1200,7 @@
         finish.wait()
 
 
-def backward_call(flag, q, kf, vf, ks, vs, o, do, pa, pb, cs, layt, lays, parts, planes, nkt, nst, wq, wk, wv, tok, dres, grow, dg2):
+def backward_call(flag, q, kf, vf, ks, vs, o, do, pa, pb, cs, layout, parts, planes, nkt, nst, wq, wk, wv, tok, dres, grow, dg2):
     n, R, D = q.shape
     L, S = kf.shape[0], ks.shape[0]
     pairs = pa.shape[0]
@@ -1221,9 +1234,9 @@
     return pl.pallas_call(
         functools.partial(backward_kernel, R, L, S, E, pairs, planes),
         grid=(2 * pairs,),
-        in_specs=[whole(flag), rows, keys(kf), keys(vf), keys(ks), keys(vs), rows, rows]
+        in_specs=[pl.BlockSpec(memory_space=pltpu.SMEM), rows, keys(kf), keys(vf), keys(ks), keys(vs), rows, rows]
         + [pl.BlockSpec((1, 2, R, R), lambda j: (late(j), 0, 0, 0)), pl.BlockSpec((1, 2, KT - R, R), lambda j: (early(j), 0, 0, 0))]
-        + [pl.BlockSpec((3, 1, 2, R), lambda j: (0, lax.rem(j, pairs), 0, 0)), whole(layt), whole(lays)]
+        + [pl.BlockSpec((3, 1, 2, R), lambda j: (0, lax.rem(j, pairs), 0, 0)), whole(layout)]
         + [anywhere] * (len(parts) + 7)
         + [whole(grow), whole(dg2)],
         out_specs=[anywhere] + [whole(s) for s in outs[1:]],
@@ -1233,7 +1246,7 @@
             vmem_limit_bytes=60 * 2**20, dimension_semantics=("arbitrary",), collective_id=1, has_side_effects=True
         ),
         name="backward",
-    )(flag, q, kf, vf, ks, vs, o, do, pa, pb, cs, layt, lays, *parts, nkt, nst, wq, wk, wv, tok, dres, grow, dg2)
+    )(flag, q, kf, vf, ks, vs, o, do, pa, pb, cs, layout, *parts, nkt, nst, wq, wk, wv, tok, dres, grow, dg2)
 
 
 EPSILON = 1e-06
@@ -1396,29 +1409,24 @@
     me = lax.axis_index("blk")
     L = layout.shape[1]
     S = L // 8
-    swap = lengths[0] < lengths[1]
-    flag = jnp.broadcast_to(swap.astype(jnp.int32), (8, 128))
-    lay = jnp.where(swap, layout[::-1], layout)
-    layt = jnp.where(me == 0, lay, jnp.roll(lay, R, axis=1))[:, None, :]
-    lays = lay[1:, :S]
     lane = np.arange(2 * SPAN)
     turned = np.where(lane >= SPAN, lane - 2 * SPAN, lane)
-    urow = mm(table, bucket_rows(-turned, table.shape[0]).astype(BF), ((0,), (1,))).reshape(H // 2, 2, 2 * SPAN)
+    basis = jnp.asarray(bucket_rows(-turned, table.shape[0]).T, BF)
     gains = jnp.pad(jnp.stack([gain_one, gain_two], axis=1), ((0, 0), (0, 126)))
     o, pa, pb, cs, grow, q, kf, vf, ks, vs, nkt, nst, *wholes = forward_call(
-        flag, tokens, layt, lays, urow, [gains, wq, wk, wv, wo, wi, wt], S
+        lengths, tokens, layout, table, basis, [gains, wq, wk, wv, wo, wi, wt], S
     )
     flat = lambda a: a.reshape(-1, a.shape[-1])
     wq_all, wk_all, wv_all, wo_all, wi_all, wt_all = [flat(a) for a in wholes]
     rows = lambda a: a.reshape(n * R, D)
     mixed, dresid, datt, dwo, *handed = feed_forward_call(
-        flag, rows(o), rows(tokens), rows(grad_out), wo_all, grow, wi_all, wt_all
+        lengths, rows(o), rows(tokens), rows(grad_out), wo_all, grow, wi_all, wt_all
     )
     count = 2 * (4 - FF_SUMS)
     dg2, done = handed[count], handed[count + 1 :]
     planes = sum([(None, j) for j in range(FF_SUMS, 4)], ()) + (None,)
     gtok, small, *sums = backward_call(
-        flag, q, kf, vf, ks, vs, o, datt.reshape(n, R, D), pa, pb, cs, layt, lays,
+        lengths, q, kf, vf, ks, vs, o, datt.reshape(n, R, D), pa, pb, cs, layout,
         handed[:count] + [dwo.reshape(4, 2, 2, 2, -1, D)], planes,
         nkt, nst, wq_all, wk_all, wv_all, tokens, dresid, grow, dg2,
     )

time: 294 us -> 283 us (0.963)
  local copies, waits for them, and re-layouts: 15 us -> 9.88 us
  Pallas kernels: 270 us -> 265 us
    unnamed x30 -> x29, local copies, waits for them, and re-layouts: 5.7 us -> 7.06 us
where the time goes in v3:
time: 283 us; the launch traced here: 280 us
  Pallas kernels  265 us (94%)
  local copies, waits for them, and re-layouts  9.88 us (3%)
  other arithmetic  3.06 us (1%)
    pallas_call x1, Pallas kernels, forward_call(): pl.pallas_call(functools.partial(forward_kernel, R, L, S, E, pairs), grid...  108 us
    pallas_call x1, Pallas kernels, backward_call(): pl.pallas_call(functools.partial(backward_kernel, R, L, S, E, pairs, plan...  97.5 us
    pallas_call x1, Pallas kernels, feed_forward_call(): pl.pallas_call(functools.partial(feed_forward, R, blocks), grid=(blocks,)...  59.9 us
    unnamed x29, local copies, waits for them, and re-layouts  7.06 us

profile of v3, /device:TPU:0, one launch (start us, length us, event | category | flops | bytes accessed | tf_op | source)
XLA Modules:
  0.0 280.0 jit_solution(6757504013869631104)
XLA Ops:
  0.6 0.7 pad_maximum_fusion.1
  1.3 0.1 copy.29
  1.4 0.6 pad.4.refs_5_
  2.0 1.4 copy.30.refs_3_
  3.4 107.9 %forward.1 = (bf16[2,512,768]{2,1,0:T(8,128)(2,1)}, bf16[6,2,512,512]{3,2,1,0:T(8,128)(2,1)}, bf16[6,2,640,512]{3,2,1,0:T(8,128)(2,1)}, f32[3,6,2,512]{3,2,1,0:T...) custom-call(s32[2]{0:T(128)} %refs_0_.5, ...), custom_call_target="tpu_custom_call" | custom-call | tf_op jit(solution)/shard_map/forward/pallas_call | solution.py:863
  111.3 59.9 %feed_forward.1 = (bf16[1024,768]{1,0:T(8,128)(2,1)}, f32[1024,768]{1,0:T(8,128)}, bf16[1024,768]{1,0:T(8,128)(2,1)}, bf16[768,768]{1,0:T(8,128)(2,1)}, bf16[4,2...) custom-call(s32[2]{0:T(128)} %refs_0_.5, ...), custom_call_target="tpu_custom_call" | custom-call | tf_op jit(solution)/shard_map/feed_forward/pallas_call | solution.py:583
  171.2 0.0 copy-start.2
  171.2 0.0 copy-start.4
  171.2 0.0 copy-start.5
  171.2 0.0 copy-start.6
  171.2 0.0 copy-start.3
  171.2 97.5 %backward.1 = (bf16[2,512,768]{2,1,0:T(8,128)(2,1)}, f32[64,128]{1,0:T(8,128)}, f32[24,768]{1,0:T(8,128)}, f32[96,768]{1,0:T(8,128)}, f32[24,768]{1,0:T(8,128)},...) custom-call(s32[2]{0:T(128)} %refs_0_.5, bf16[2,512,768]{2,1,0:T(8,128)(2,1)} %get-tuple-element.54.refs_1_, ...), custom_call_target="tpu_custom_call" | custom-call | tf_op jit(solution)/shard_map/backward/pallas_call | solution.py:1234
  268.7 0.0 copy-start
  268.8 0.0 copy-done.2
  268.8 0.8 broadcast_select_fusion
  269.5 0.0 copy-done.4
  269.5 0.0 copy-done.5
  269.5 0.0 copy-done.6
  269.5 1.6 pad_maximum_fusion
  271.2 0.8 slice.4
  271.9 0.0 copy-done.3
  271.9 0.9 fusion.1
  272.8 1.4 fusion
  274.2 0.0 copy-done
  274.2 0.0 copy-start.1
  274.2 1.1 copy.37
  275.3 0.8 copy-done.1
  276.1 0.0 copy-start.10
  276.1 0.0 copy-start.9
  276.1 0.0 copy-start.8
  276.1 0.0 copy-start.7
  276.1 1.1 copy.38
  277.3 0.0 copy-done.10
  277.3 0.6 copy.39
  277.9 0.0 copy-done.9
  277.9 0.6 copy.40
  278.6 0.0 copy-done.8
  278.6 0.6 copy.41
  279.2 0.0 copy-done.7
  279.2 0.6 copy.42
  (1 shorter events, 0.0 us)
Async XLA Ops:
  171.2 97.6 %copy-start.2 = (f32[96,768]{1,0:T(8,128)S(1)}, f32[96,768]{1,0:T(8,128)}, u32[]{:S(2)}) copy-start(f32[96,768]{1,0:T(8,128)} %get-tuple-element.84) | copy-start | bytes 884740
  171.2 98.4 %copy-start.4 = (f32[24,768]{1,0:T(8,128)S(1)}, f32[24,768]{1,0:T(8,128)}, u32[]{:S(2)}) copy-start(f32[24,768]{1,0:T(8,128)} %get-tuple-element.79) | copy-start | bytes 221188
  171.2 98.4 %copy-start.5 = (f32[24,768]{1,0:T(8,128)S(1)}, f32[24,768]{1,0:T(8,128)}, u32[]{:S(2)}) copy-start(f32[24,768]{1,0:T(8,128)} %get-tuple-element.80) | copy-start | bytes 221188
  171.2 98.4 %copy-start.6 = (f32[24,768]{1,0:T(8,128)S(1)}, f32[24,768]{1,0:T(8,128)}, u32[]{:S(2)}) copy-start(f32[24,768]{1,0:T(8,128)} %get-tuple-element.81) | copy-start | bytes 221188
  171.2 100.7 %copy-start.3 = (f32[512,32]{1,0:T(8,128)S(1)}, f32[512,32]{1,0:T(8,128)}, u32[]{:S(2)}) copy-start(f32[512,32]{1,0:T(8,128)} %constant.42.clone) | copy-start | bytes 196612
  268.7 5.4 %copy-start = (bf16[1024,768]{1,0:T(8,128)(2,1)S(1)}, bf16[1024,768]{1,0:T(8,128)(2,1)}, u32[]{:S(2)}) copy-start(bf16[1024,768]{1,0:T(8,128)(2,1)} %get-tuple-element.53) | copy-start | bytes 4718596
  274.2 2.0 copy-start.1
  276.1 1.2 copy-start.10
  276.1 1.8 copy-start.9
  276.1 2.4 copy-start.8
  276.1 3.1 %copy-start.7 = (f32[24,768]{1,0:T(8,128)S(1)}, f32[24,768]{1,0:T(8,128)}, u32[]{:S(2)}) copy-start(f32[24,768]{1,0:T(8,128)} %get-tuple-element.104) | copy-start | bytes 221188

commit v4 on v3

--- a/solution.py
+++ b/solution.py
@@ -169,8 +169,9 @@
 
 
 EPSILON = 1e-06
+FORWARD_TOKENS = (-8.5, -8, -7, -6, -5, -4, -3, -2)
 FORWARD_PIECES = 3
-FORWARD_WAYS = (0,) * 11
+FORWARD_WAYS = (0,) * 5 + (1,) * 4 + (0,) * 2
 FORWARD_AT = (
     (-9, -8, -7, -6, -5),
     (-8, -7, -6, -5, -4),
@@ -671,15 +672,18 @@
     chains = [together(chains[0], chains[1])] + chains[2:]
     plan = turn_plan(chains, FORWARD_AT)
     spare = GATHER_COPIES * count
-    long = remote(tok.at[0], xfar, sems, spare, at.along_x())
-    short = remote(tok.at[1, pl.ds(0, S)], xshort, sems, spare + 1, at.along_x())
+    short = remote(tok.at[1, pl.ds(0, S)], xshort, sems, spare, at.along_x())
+    long = []
+    for i in range(len(FORWARD_TOKENS)):
+        some = pl.ds(i * R // len(FORWARD_TOKENS), R // len(FORWARD_TOKENS))
+        long.append(remote(tok.at[0, some], xfar.at[some], sems, spare + 1 + i, at.along_x()))
     out = lambda i, a, b: pltpu.make_async_copy(a, b, local.at[count + i])
     weights_out = [out(i, slabs[1 + i], wholes[i]) for i in range(3)]
     kept_out = [out(3 + i, a, b) for i, (a, b) in enumerate(zip(inner, kept))]
 
-    def send_tokens():
-        long.start()
-        pl.when(at.x == 0)(short.start)
+    for place, copy in zip(FORWARD_TOKENS, long):
+        plan.setdefault(place, []).append(copy.start)
+    plan[FORWARD_TOKENS[-1]].append(lambda: pl.when(at.x == 0)(short.start))
 
     def turn(t):
         for stage in plan.get(t, []):
@@ -693,12 +697,12 @@
         at.greet()
         turn(-9)
         tok[0], tok[1] = swapped(flag, tokens[0], tokens[1])
-        send_tokens()
+        turn(-8.5)
         long_keys, short_keys, *queries = coordinates(at, flag, layout, R, S)
         for i, (base, row) in enumerate([(0, long_keys), (L, short_keys)]):
             kcat[base : base + row.shape[1], W:] = jnp.transpose(eye_of(row, SPAN, False).astype(F32)).astype(BF)
             ohq[i] = eye_of(queries[i], SPAN, False)
-        rows = lax.dot_general(table[...], basis[...], (((0,), (0,)), ((), ())), preferred_element_type=F32)
+        rows = lax.dot_general(table[...].astype(BF), basis[...], (((0,), (0,)), ((), ())), preferred_element_type=F32)
         for h in range(2 * pairs):
             u[h] = rows[h : h + 1]
         vt[:, E:] = jnp.ones((2, vt.shape[1] - E, vt.shape[2]), BF)
@@ -730,7 +734,8 @@
     def _():
         nkt[:, :R] = flipped(normed[0])
         nst[...] = flipped(normed[1])
-        long.wait()
+        for copy in long:
+            copy.wait()
 
         @pl.when(at.x == 0)
         def _():
@@ -850,7 +855,7 @@
     late = lambda j: jnp.maximum(j - pairs, 0)
     kept = [(n, R, D), (L, D), (L, D), (S, D), (S, D), (D, KT), (D, R)]
     chains = 5 + 2 * FORWARD_PIECES
-    copies = GATHER_COPIES * chains + 2
+    copies = GATHER_COPIES * chains + 1 + len(FORWARD_TOKENS)
     gathered = [(4, 2, 2, 2) + s.shape for s in shards]
     filled = gathered[1:]
     blocked = [
@@ -1412,9 +1417,10 @@
     lane = np.arange(2 * SPAN)
     turned = np.where(lane >= SPAN, lane - 2 * SPAN, lane)
     basis = jnp.asarray(bucket_rows(-turned, table.shape[0]).T, BF)
-    gains = jnp.pad(jnp.stack([gain_one, gain_two], axis=1), ((0, 0), (0, 126)))
+    column = jnp.arange(128)[None, :]
+    gains = jnp.where(column == 0, gain_one[:, None], jnp.where(column == 1, gain_two[:, None], 0)).astype(BF)
     o, pa, pb, cs, grow, q, kf, vf, ks, vs, nkt, nst, *wholes = forward_call(
-        lengths, tokens, layout, table, basis, [gains, wq, wk, wv, wo, wi, wt], S
+        lengths, tokens, layout, table.astype(F32), basis, [gains, wq, wk, wv, wo, wi, wt], S
     )
     flat = lambda a: a.reshape(-1, a.shape[-1])
     wq_all, wk_all, wv_all, wo_all, wi_all, wt_all = [flat(a) for a in wholes]

time: 283 us -> 279 us (0.986)
  Pallas kernels: 265 us -> 261 us
    pallas_call x1, Pallas kernels: 108 us -> 103 us  [forward_call(): pl.pallas_call(functools.partial(forward_kernel, R, L, S, E, pairs), grid...]
    unnamed x29 -> x28, local copies, waits for them, and re-layouts: 7.06 us -> 5.69 us
where the time goes in v4:
time: 279 us; the launch traced here: 276 us
  Pallas kernels  261 us (94%)
  local copies, waits for them, and re-layouts  9.19 us (3%)
  other arithmetic  3.72 us (1%)
    pallas_call x1, Pallas kernels, forward_call(): pl.pallas_call(functools.partial(forward_kernel, R, L, S, E, pairs), grid...  103 us
    pallas_call x1, Pallas kernels, backward_call(): pl.pallas_call(functools.partial(backward_kernel, R, L, S, E, pairs, plan...  97.5 us
    pallas_call x1, Pallas kernels, feed_forward_call(): pl.pallas_call(functools.partial(feed_forward, R, blocks), grid=(blocks,)...  60.2 us
    unnamed x28, local copies, waits for them, and re-layouts  5.69 us

profile of v4, /device:TPU:0, one launch (start us, length us, event | category | flops | bytes accessed | tf_op | source)
XLA Modules:
  0.0 275.9 jit_solution(6993463780628581754)
XLA Ops:
  0.7 1.3 select_select_fusion.refs_5_
  2.0 1.4 copy.27.refs_3_
  3.4 103.4 %forward.1 = (bf16[2,512,768]{2,1,0:T(8,128)(2,1)}, bf16[6,2,512,512]{3,2,1,0:T(8,128)(2,1)}, bf16[6,2,640,512]{3,2,1,0:T(8,128)(2,1)}, f32[3,6,2,512]{3,2,1,0:T...) custom-call(s32[2]{0:T(128)} %refs_0_.5, ...), custom_call_target="tpu_custom_call" | custom-call | tf_op jit(solution)/shard_map/forward/pallas_call | solution.py:868
  106.8 60.2 %feed_forward.1 = (bf16[1024,768]{1,0:T(8,128)(2,1)}, f32[1024,768]{1,0:T(8,128)}, bf16[1024,768]{1,0:T(8,128)(2,1)}, bf16[768,768]{1,0:T(8,128)(2,1)}, bf16[4,2...) custom-call(s32[2]{0:T(128)} %refs_0_.5, ...), custom_call_target="tpu_custom_call" | custom-call | tf_op jit(solution)/shard_map/feed_forward/pallas_call | solution.py:584
  167.0 0.0 copy-start.2
  167.0 0.0 copy-start.4
  167.0 0.0 copy-start.5
  167.0 0.0 copy-start.6
  167.0 0.0 copy-start.3
  167.0 97.5 %backward.1 = (bf16[2,512,768]{2,1,0:T(8,128)(2,1)}, f32[64,128]{1,0:T(8,128)}, f32[24,768]{1,0:T(8,128)}, f32[96,768]{1,0:T(8,128)}, f32[24,768]{1,0:T(8,128)},...) custom-call(s32[2]{0:T(128)} %refs_0_.5, bf16[2,512,768]{2,1,0:T(8,128)(2,1)} %get-tuple-element.54.refs_1_, ...), custom_call_target="tpu_custom_call" | custom-call | tf_op jit(solution)/shard_map/backward/pallas_call | solution.py:1239
  264.6 0.0 copy-start
  264.6 0.0 copy-done.2
  264.6 0.8 broadcast_select_fusion
  265.4 0.0 copy-done.4
  265.4 0.0 copy-done.5
  265.4 0.0 copy-done.6
  265.4 1.6 pad_maximum_fusion
  267.0 0.8 slice.4
  267.8 0.0 copy-done.3
  267.8 0.9 fusion.1
  268.6 1.4 fusion
  270.0 0.0 copy-done
  270.0 0.0 copy-start.1
  270.0 1.1 copy.34
  271.2 0.8 copy-done.1
  272.0 0.0 copy-start.10
  272.0 0.0 copy-start.9
  272.0 0.0 copy-start.8
  272.0 0.0 copy-start.7
  272.0 1.1 copy.35
  273.1 0.0 copy-done.10
  273.1 0.6 copy.36
  273.8 0.0 copy-done.9
  273.8 0.6 copy.37
  274.4 0.0 copy-done.8
  274.4 0.6 copy.38
  275.1 0.0 copy-done.7
  275.1 0.6 copy.39
  (2 shorter events, 0.0 us)
Async XLA Ops:
  167.0 97.6 %copy-start.2 = (f32[96,768]{1,0:T(8,128)S(1)}, f32[96,768]{1,0:T(8,128)}, u32[]{:S(2)}) copy-start(f32[96,768]{1,0:T(8,128)} %get-tuple-element.84) | copy-start | bytes 884740
  167.0 98.4 %copy-start.4 = (f32[24,768]{1,0:T(8,128)S(1)}, f32[24,768]{1,0:T(8,128)}, u32[]{:S(2)}) copy-start(f32[24,768]{1,0:T(8,128)} %get-tuple-element.79) | copy-start | bytes 221188
  167.0 98.4 %copy-start.5 = (f32[24,768]{1,0:T(8,128)S(1)}, f32[24,768]{1,0:T(8,128)}, u32[]{:S(2)}) copy-start(f32[24,768]{1,0:T(8,128)} %get-tuple-element.80) | copy-start | bytes 221188
  167.0 98.4 %copy-start.6 = (f32[24,768]{1,0:T(8,128)S(1)}, f32[24,768]{1,0:T(8,128)}, u32[]{:S(2)}) copy-start(f32[24,768]{1,0:T(8,128)} %get-tuple-element.81) | copy-start | bytes 221188
  167.0 100.8 %copy-start.3 = (f32[512,32]{1,0:T(8,128)S(1)}, f32[512,32]{1,0:T(8,128)}, u32[]{:S(2)}) copy-start(f32[512,32]{1,0:T(8,128)} %constant.44.clone) | copy-start | bytes 196612
  264.6 5.4 %copy-start = (bf16[1024,768]{1,0:T(8,128)(2,1)S(1)}, bf16[1024,768]{1,0:T(8,128)(2,1)}, u32[]{:S(2)}) copy-start(bf16[1024,768]{1,0:T(8,128)(2,1)} %get-tuple-element.53) | copy-start | bytes 4718596
  270.0 2.0 copy-start.1
  272.0 1.2 copy-start.10
  272.0 1.8 copy-start.9
  272.0 2.4 copy-start.8
  272.0 3.1 %copy-start.7 = (f32[24,768]{1,0:T(8,128)S(1)}, f32[24,768]{1,0:T(8,128)}, u32[]{:S(2)}) copy-start(f32[24,768]{1,0:T(8,128)} %get-tuple-element.106) | copy-start | bytes 221188

commit v5 on v4

--- a/solution.py
+++ b/solution.py
@@ -171,7 +171,7 @@
 EPSILON = 1e-06
 FORWARD_TOKENS = (-8.5, -8, -7, -6, -5, -4, -3, -2)
 FORWARD_PIECES = 3
-FORWARD_WAYS = (0,) * 5 + (1,) * 4 + (0,) * 2
+FORWARD_WAYS = (0,) * 5 + (1,) * 5 + (0,) * 1
 FORWARD_AT = (
     (-9, -8, -7, -6, -5),
     (-8, -7, -6, -5, -4),

time: 279 us -> 280 us (level)
  no operation moved by 1% of the time
where the time goes in v5:
time: 280 us; the launch traced here: 277 us
  Pallas kernels  262 us (94%)
  local copies, waits for them, and re-layouts  9.19 us (3%)
  other arithmetic  3.72 us (1%)
    pallas_call x1, Pallas kernels, forward_call(): pl.pallas_call(functools.partial(forward_kernel, R, L, S, E, pairs), grid...  105 us
    pallas_call x1, Pallas kernels, backward_call(): pl.pallas_call(functools.partial(backward_kernel, R, L, S, E, pairs, plan...  97.3 us
    pallas_call x1, Pallas kernels, feed_forward_call(): pl.pallas_call(functools.partial(feed_forward, R, blocks), grid=(blocks,)...  60.3 us
    unnamed x28, local copies, waits for them, and re-layouts  5.69 us

profile of v5, /device:TPU:0, one launch (start us, length us, event | category | flops | bytes accessed | tf_op | source)
XLA Modules:
  0.0 277.2 jit_solution(7766033161335203364)
XLA Ops:
  0.7 1.3 select_select_fusion.refs_5_
  2.0 1.4 copy.27.refs_3_
  3.4 104.8 %forward.1 = (bf16[2,512,768]{2,1,0:T(8,128)(2,1)}, bf16[6,2,512,512]{3,2,1,0:T(8,128)(2,1)}, bf16[6,2,640,512]{3,2,1,0:T(8,128)(2,1)}, f32[3,6,2,512]{3,2,1,0:T...) custom-call(s32[2]{0:T(128)} %refs_0_.5, ...), custom_call_target="tpu_custom_call" | custom-call | tf_op jit(solution)/shard_map/forward/pallas_call | solution.py:868
  108.2 60.3 %feed_forward.1 = (bf16[1024,768]{1,0:T(8,128)(2,1)}, f32[1024,768]{1,0:T(8,128)}, bf16[1024,768]{1,0:T(8,128)(2,1)}, bf16[768,768]{1,0:T(8,128)(2,1)}, bf16[4,2...) custom-call(s32[2]{0:T(128)} %refs_0_.5, ...), custom_call_target="tpu_custom_call" | custom-call | tf_op jit(solution)/shard_map/feed_forward/pallas_call | solution.py:584
  168.5 0.0 copy-start.2
  168.5 0.0 copy-start.4
  168.6 0.0 copy-start.5
  168.6 0.0 copy-start.6
  168.6 0.0 copy-start.3
  168.6 97.3 %backward.1 = (bf16[2,512,768]{2,1,0:T(8,128)(2,1)}, f32[64,128]{1,0:T(8,128)}, f32[24,768]{1,0:T(8,128)}, f32[96,768]{1,0:T(8,128)}, f32[24,768]{1,0:T(8,128)},...) custom-call(s32[2]{0:T(128)} %refs_0_.5, bf16[2,512,768]{2,1,0:T(8,128)(2,1)} %get-tuple-element.54.refs_1_, ...), custom_call_target="tpu_custom_call" | custom-call | tf_op jit(solution)/shard_map/backward/pallas_call | solution.py:1239
  265.9 0.0 copy-start
  266.0 0.0 copy-done.2
  266.0 0.8 broadcast_select_fusion
  266.7 0.0 copy-done.4
  266.7 0.0 copy-done.5
  266.7 0.0 copy-done.6
  266.8 1.6 pad_maximum_fusion
  268.4 0.8 slice.4
  269.1 0.0 copy-done.3
  269.1 0.9 fusion.1
  270.0 1.4 fusion
  271.4 0.0 copy-done
  271.4 0.0 copy-start.1
  271.4 1.1 copy.34
  272.5 0.8 copy-done.1
  273.3 0.0 copy-start.10
  273.3 0.0 copy-start.9
  273.3 0.0 copy-start.8
  273.4 0.0 copy-start.7
  273.4 1.1 copy.35
  274.5 0.0 copy-done.10
  274.5 0.6 copy.36
  275.1 0.0 copy-done.9
  275.1 0.6 copy.37
  275.8 0.0 copy-done.8
  275.8 0.6 copy.38
  276.4 0.0 copy-done.7
  276.4 0.6 copy.39
  (2 shorter events, 0.0 us)
Async XLA Ops:
  168.5 97.4 %copy-start.2 = (f32[96,768]{1,0:T(8,128)S(1)}, f32[96,768]{1,0:T(8,128)}, u32[]{:S(2)}) copy-start(f32[96,768]{1,0:T(8,128)} %get-tuple-element.84) | copy-start | bytes 884740
  168.5 98.2 %copy-start.4 = (f32[24,768]{1,0:T(8,128)S(1)}, f32[24,768]{1,0:T(8,128)}, u32[]{:S(2)}) copy-start(f32[24,768]{1,0:T(8,128)} %get-tuple-element.79) | copy-start | bytes 221188
  168.6 98.2 %copy-start.5 = (f32[24,768]{1,0:T(8,128)S(1)}, f32[24,768]{1,0:T(8,128)}, u32[]{:S(2)}) copy-start(f32[24,768]{1,0:T(8,128)} %get-tuple-element.80) | copy-start | bytes 221188
  168.6 98.2 %copy-start.6 = (f32[24,768]{1,0:T(8,128)S(1)}, f32[24,768]{1,0:T(8,128)}, u32[]{:S(2)}) copy-start(f32[24,768]{1,0:T(8,128)} %get-tuple-element.81) | copy-start | bytes 221188
  168.6 100.6 %copy-start.3 = (f32[512,32]{1,0:T(8,128)S(1)}, f32[512,32]{1,0:T(8,128)}, u32[]{:S(2)}) copy-start(f32[512,32]{1,0:T(8,128)} %constant.44.clone) | copy-start | bytes 196612
  265.9 5.4 %copy-start = (bf16[1024,768]{1,0:T(8,128)(2,1)S(1)}, bf16[1024,768]{1,0:T(8,128)(2,1)}, u32[]{:S(2)}) copy-start(bf16[1024,768]{1,0:T(8,128)(2,1)} %get-tuple-element.53) | copy-start | bytes 4718596
  271.4 2.0 copy-start.1
  273.3 1.2 copy-start.10
  273.3 1.8 copy-start.9
  273.3 2.4 copy-start.8
  273.4 3.1 %copy-start.7 = (f32[24,768]{1,0:T(8,128)S(1)}, f32[24,768]{1,0:T(8,128)}, u32[]{:S(2)}) copy-start(f32[24,768]{1,0:T(8,128)} %get-tuple-element.106) | copy-start | bytes 221188
